TPU v7x, 32 devices: a whole 2x2x4 slice. The times are simulated.
32 devices in a mesh: dp: 2 (over x), ctx: 4 (over z), exp: 4 (over y, core).
Axes of the slice: x: 2, y: 2, z: 4, core: 2. Of those that a mesh axis runs over, the one named last changes fastest.
Arguments:
- tokens: bfloat16 [8, 1024, 1536], P(('dp', 'exp'), 'ctx'), may hold values from -6 to 6
- gain_attn: float32 [1536], replicated, may hold values from 0.5 to 1.5
- w_query: bfloat16 [1536, 1536], P(('dp', 'ctx', 'exp')), may hold values from -1.25 to 1.25
- w_key: bfloat16 [1536, 512], P(('dp', 'ctx', 'exp')), may hold values from -0.15625 to 0.15625
- w_value: bfloat16 [1536, 512], P(('dp', 'ctx', 'exp')), may hold values from -0.15625 to 0.15625
- w_out: bfloat16 [1536, 1536], P(('dp', 'ctx', 'exp')), may hold values from -6 to 6
- gain_moe: float32 [1536], replicated, may hold values from 0.5 to 1.5
- w_in: bfloat16 [16, 1536, 1024], P('exp', ('dp', 'ctx')), may hold values from -0.15625 to 0.15625
- w_down: bfloat16 [16, 512, 1536], P('exp', ('dp', 'ctx')), may hold values from -1.5 to 1.5
- routes: int32 [8, 1024, 8], P(('dp', 'exp'), 'ctx'), may hold values from 0 to 15, all different within a row; in each aligned block of 256 rows (0 to 255, 256 to 511, ..., all dimensions but the last counted through in order) at most 192 rows name the same one
- gates: bfloat16 [8, 1024, 8], P(('dp', 'exp'), 'ctx'), may hold values from 0.19921875 to 0.59765625
- lengths: int32 [8, 3], P(('dp', 'exp')), may hold values from 1 to 896, 1024 in all within a row
- cotangent: float32 [8, 1024, 1536], P(('dp', 'exp'), 'ctx'), may hold values from -6 to 6
Outputs:
- mixed: bfloat16 [8, 1024, 1536], P(('dp', 'exp'), 'ctx')
- grad_tokens: float32 [8, 1024, 1536], P(('dp', 'exp'), 'ctx')
- grad_gain_attn: float32 [1536], P(('dp', 'ctx', 'exp'))
- grad_query: float32 [1536, 1536], P(('dp', 'ctx', 'exp'))
- grad_key: float32 [1536, 512], P(('dp', 'ctx', 'exp'))
- grad_value: float32 [1536, 512], P(('dp', 'ctx', 'exp'))
- grad_out: float32 [1536, 1536], P(('dp', 'ctx', 'exp'))
- grad_gain_moe: float32 [1536], P(('dp', 'ctx', 'exp'))
- grad_in: float32 [16, 1536, 1024], P('exp', ('dp', 'ctx'))
- grad_down: float32 [16, 512, 1536], P('exp', ('dp', 'ctx'))
Inputs may be any that keep to these rules, and one draw needn't show every extreme that they name: `routes`: each row names 8 different experts. In each aligned block of 256 rows (the rows of one device) no expert is named by more than 192 rows. Each group's 3 lengths sum to 1024, and its longest is exactly 896.
All inputs are finite; a program needn't handle non-finite values.
Results may differ from a plain program's by a relative error of at most 0.017.
Values may be sent and summed in bfloat16 or wider, within the bound.
No kernel may reach another device: no remote copies, remote signals or barrier semaphores. Data moves between devices by JAX's collectives and lax.ppermute only.
A program may use at most 256 MiB of HBM per device.

v0:
```python
import jax
import jax.numpy as jnp
from jax import lax
from jax.sharding import PartitionSpec as P

HEADS = 24
KV_HEADS = 8
HEAD_DIM = 64
FF = 512
TOP = 8
CAP = 192


eps_norm = 1e-06
score_scale = 0.015625
residual_scale = 0.22
rope_base = 10000.0


def rms_parts(vectors):
    inv_rms = lax.rsqrt(jnp.mean(vectors * vectors, axis=-1, keepdims=True) + eps_norm)
    return (vectors * inv_rms, inv_rms)


def rms_back(grad_out, normal, inv_rms, gain_vec):
    weighted = grad_out * gain_vec
    grad_in = inv_rms * (weighted - normal * jnp.mean(weighted * normal, axis=-1, keepdims=True))
    return (grad_in, jnp.sum(grad_out * normal, axis=0))


def rotate(vectors, position, direction):
    half_dim = vectors.shape[-1] // 2
    frequency = rope_base ** (-2.0 * jnp.arange(half_dim, dtype=jnp.float32) / vectors.shape[-1])
    angles = position.astype(jnp.float32)[:, None] * frequency[None, :]
    cosine = jnp.cos(angles)[:, None, :]
    sines = direction * jnp.sin(angles)[:, None, :]
    front_half = vectors[..., :half_dim]
    second = vectors[..., half_dim:]
    return jnp.concatenate(
        [front_half * cosine - second * sines, second * cosine + front_half * sines], axis=-1
    )


def documents(lengths, length_all):
    doc_ends = jnp.cumsum(lengths)
    doc_starts = doc_ends - lengths
    places = jnp.arange(length_all, dtype=jnp.int32)
    doc_ids = jnp.sum((places[:, None] >= doc_ends[None, :]).astype(jnp.int32), axis=1)
    chosen = doc_ids[:, None] == jnp.arange(lengths.shape[0], dtype=jnp.int32)[None, :]
    offsets = jnp.sum(jnp.where(chosen, doc_starts[None, :], 0), axis=1)
    return (doc_ids, places - offsets)


def per_device(
    tokens,
    gain_attn,
    w_query,
    w_key,
    w_value,
    w_out,
    gain_moe,
    w_in,
    w_down,
    routes,
    gates,
    lengths,
    cotangent,
):
    ctx_count = lax.axis_size("ctx")
    ctx_place = lax.axis_index("ctx")
    owners = lax.axis_size("exp")
    row_count = tokens.shape[1]
    model_width = tokens.shape[2]
    seq_span = row_count * ctx_count
    kv_width = w_key.shape[1]
    local_experts = w_in.shape[0]
    experts = local_experts * owners
    group_size = HEADS // KV_HEADS
    doc_all, pos_all = documents(lengths[0], seq_span)
    first_row = ctx_place * row_count
    doc_mine = lax.dynamic_slice_in_dim(doc_all, first_row, row_count)
    pos_mine = lax.dynamic_slice_in_dim(pos_all, first_row, row_count)
    key_index = jnp.arange(seq_span, dtype=jnp.int32)
    query_index = first_row + jnp.arange(row_count, dtype=jnp.int32)
    allowed = (doc_mine[:, None] == doc_all[None, :]) & (key_index[None, :] <= query_index[:, None])
    inputs = tokens[0].astype(jnp.float32)
    query_w, key_w, value_w, out_w = (
        lax.all_gather(w_query, ("dp", "ctx", "exp"), axis=0, tiled=True),
        lax.all_gather(w_key, ("dp", "ctx", "exp"), axis=0, tiled=True),
        lax.all_gather(w_value, ("dp", "ctx", "exp"), axis=0, tiled=True),
        lax.all_gather(w_out, ("dp", "ctx", "exp"), axis=0, tiled=True),
    )
    normal_a, inv_rms_a = rms_parts(inputs)
    normed_a = (normal_a * gain_attn).astype(jnp.bfloat16)
    query_f = jnp.dot(normed_a, query_w, preferred_element_type=jnp.float32)
    key_f = jnp.dot(normed_a, key_w, preferred_element_type=jnp.float32)
    value_f = jnp.dot(normed_a, value_w, preferred_element_type=jnp.float32)
    query_r = rotate(query_f.reshape(row_count, HEADS, HEAD_DIM), pos_mine, 1.0).astype(
        jnp.bfloat16
    )
    key_r = (
        rotate(key_f.reshape(row_count, KV_HEADS, HEAD_DIM), pos_mine, 1.0)
        .astype(jnp.bfloat16)
        .reshape(row_count, kv_width)
    )
    value_b = value_f.astype(jnp.bfloat16)
    keys_all, values_all = (
        lax.all_gather(key_r, "ctx", axis=0, tiled=True),
        lax.all_gather(value_b, "ctx", axis=0, tiled=True),
    )
    query_heads = jnp.transpose(
        query_r.reshape(row_count, KV_HEADS, group_size, HEAD_DIM), (1, 0, 2, 3)
    )
    key_heads = jnp.transpose(keys_all.reshape(seq_span, KV_HEADS, HEAD_DIM), (1, 0, 2))
    value_heads = jnp.transpose(values_all.reshape(seq_span, KV_HEADS, HEAD_DIM), (1, 0, 2))

    def head_forward(operands):
        query_head, key_head, value_head = operands
        scores = (
            jnp.einsum("sgd,td->gst", query_head, key_head, preferred_element_type=jnp.float32)
            * score_scale
        )
        scores = jnp.where(allowed[None], scores, -1e30)
        peak = jnp.max(scores, axis=-1, keepdims=True)
        exponent = jnp.exp(scores - peak)
        totals = jnp.sum(exponent, axis=-1, keepdims=True)
        chances = (exponent / totals).astype(jnp.bfloat16)
        mixture = jnp.einsum("gst,td->sgd", chances, value_head, preferred_element_type=jnp.float32)
        return (mixture, peak + jnp.log(totals))

    mixed_heads, log_totals = lax.map(head_forward, (query_heads, key_heads, value_heads))
    attn_mixed = (
        jnp.transpose(mixed_heads, (1, 0, 2, 3))
        .reshape(row_count, model_width)
        .astype(jnp.bfloat16)
    )
    branch = jnp.dot(attn_mixed, out_w, preferred_element_type=jnp.float32)
    middle = inputs + residual_scale * branch
    normal_m, inv_rms_m = rms_parts(middle)
    hidden = (normal_m * gain_moe).astype(jnp.bfloat16)
    expert_in, expert_down = (
        lax.all_gather(w_in, ("dp", "ctx"), axis=1, tiled=True),
        lax.all_gather(w_down, ("dp", "ctx"), axis=1, tiled=True),
    )
    route_rows = routes[0]
    gate_rows = gates[0].astype(jnp.float32)
    grad_final = cotangent[0]
    scaled = residual_scale * grad_final
    pair_expert = route_rows.reshape(-1)
    hit_marks = (pair_expert[:, None] == jnp.arange(experts, dtype=jnp.int32)[None, :]).astype(
        jnp.int32
    )
    ranking = jnp.sum((jnp.cumsum(hit_marks, axis=0) - 1) * hit_marks, axis=1)
    target = pair_expert * CAP + ranking
    pair_token = jnp.repeat(jnp.arange(row_count, dtype=jnp.int32), TOP)
    slot_token = jnp.zeros((experts * CAP,), jnp.int32).at[target].set(pair_token)
    slot_gate = jnp.zeros((experts * CAP,), jnp.float32).at[target].set(gate_rows.reshape(-1))
    slot_live = jnp.zeros((experts * CAP,), jnp.bool_).at[target].set(True)
    outgoing = jnp.where(
        slot_live[:, None], hidden[slot_token], jnp.zeros((), jnp.bfloat16)
    ).reshape(experts, CAP, model_width)
    received = lax.all_to_all(outgoing, "exp", split_axis=0, concat_axis=1, tiled=True)
    gate_up = jnp.einsum("erd,edf->erf", received, expert_in, preferred_element_type=jnp.float32)
    sigmoid_gate = jax.nn.sigmoid(gate_up[..., :FF])
    active = (gate_up[..., :FF] * sigmoid_gate * gate_up[..., FF:]).astype(jnp.bfloat16)
    result = jnp.einsum(
        "erf,efd->erd", active, expert_down, preferred_element_type=jnp.float32
    ).astype(jnp.bfloat16)
    gate_up, active, result = (gate_up, active, result)
    returned = lax.all_to_all(result, "exp", split_axis=1, concat_axis=0, tiled=True).reshape(
        experts * CAP, model_width
    )
    picked = returned[target].reshape(row_count, TOP, model_width).astype(jnp.float32)
    expert_sum = jnp.sum(gate_rows[:, :, None] * picked, axis=1)
    grad_outgoing = (
        (slot_gate[:, None] * scaled[slot_token])
        .astype(jnp.bfloat16)
        .reshape(experts, CAP, model_width)
    )
    grad_received = lax.all_to_all(grad_outgoing, "exp", split_axis=0, concat_axis=1, tiled=True)
    grad_active = jnp.einsum(
        "erd,efd->erf", grad_received, expert_down, preferred_element_type=jnp.float32
    )
    grad_active = grad_active.astype(jnp.bfloat16).astype(jnp.float32)
    gate_part = gate_up[..., :FF]
    up_part = gate_up[..., FF:]
    sigmoid_gate = jax.nn.sigmoid(gate_part)
    grad_gate = grad_active * up_part * sigmoid_gate * (1.0 + gate_part * (1.0 - sigmoid_gate))
    grad_up = grad_active * gate_part * sigmoid_gate
    grad_both = jnp.concatenate([grad_gate, grad_up], axis=-1).astype(jnp.bfloat16)
    grad_down_part = jnp.einsum(
        "erf,erd->efd", active, grad_received, preferred_element_type=jnp.float32
    )
    grad_in_part = jnp.einsum(
        "erd,erf->edf", received, grad_both, preferred_element_type=jnp.float32
    )
    grad_rows = jnp.einsum("erf,edf->erd", grad_both, expert_in, preferred_element_type=jnp.float32)
    grad_in_part, grad_down_part, grad_rows = (grad_in_part, grad_down_part, grad_rows)
    grad_returned = (
        lax.all_to_all(
            grad_rows.astype(jnp.bfloat16), "exp", split_axis=1, concat_axis=0, tiled=True
        )
        .astype(grad_rows.dtype)
        .reshape(experts * CAP, model_width)
    )
    grad_hidden = jnp.sum(grad_returned[target].reshape(row_count, TOP, model_width), axis=1)
    final_sum = middle + residual_scale * expert_sum
    mixed_out = final_sum.astype(jnp.bfloat16)[None]
    grad_in_w, grad_down_w = (
        lax.psum_scatter(
            grad_in_part.astype(jnp.bfloat16), ("dp", "ctx"), scatter_dimension=1, tiled=True
        ).astype(jnp.float32),
        lax.psum_scatter(
            grad_down_part.astype(jnp.bfloat16), ("dp", "ctx"), scatter_dimension=1, tiled=True
        ).astype(jnp.float32),
    )
    grad_norm_m, grad_gain_m = rms_back(grad_hidden, normal_m, inv_rms_m, gain_moe)
    grad_middle = grad_final + grad_norm_m
    grad_branch = (residual_scale * grad_middle).astype(jnp.bfloat16)
    grad_out_w = jnp.einsum(
        "sd,se->de", attn_mixed, grad_branch, preferred_element_type=jnp.float32
    )
    grad_mixed = jnp.einsum(
        "se,de->sd", grad_branch, out_w, preferred_element_type=jnp.float32
    ).astype(jnp.bfloat16)
    grad_heads = jnp.transpose(
        grad_mixed.reshape(row_count, KV_HEADS, group_size, HEAD_DIM), (1, 0, 2, 3)
    )

    def head_backward(operands):
        query_head, key_head, value_head, log_total, grad_head = operands
        scores = (
            jnp.einsum("sgd,td->gst", query_head, key_head, preferred_element_type=jnp.float32)
            * score_scale
        )
        scores = jnp.where(allowed[None], scores, -1e30)
        chances = jnp.exp(scores - log_total)
        grad_chances = jnp.einsum(
            "sgd,td->gst", grad_head, value_head, preferred_element_type=jnp.float32
        )
        row_dot = jnp.sum(chances * grad_chances, axis=-1, keepdims=True)
        grad_scores = (chances * (grad_chances - row_dot) * score_scale).astype(jnp.bfloat16)
        grad_query_head = jnp.einsum(
            "gst,td->sgd", grad_scores, key_head, preferred_element_type=jnp.float32
        )
        grad_key_head = jnp.einsum(
            "gst,sgd->td", grad_scores, query_head, preferred_element_type=jnp.float32
        )
        grad_value_head = jnp.einsum(
            "gst,sgd->td",
            chances.astype(jnp.bfloat16),
            grad_head,
            preferred_element_type=jnp.float32,
        )
        return (grad_query_head, grad_key_head, grad_value_head)

    grad_q_heads, grad_k_heads, grad_v_heads = lax.map(
        head_backward, (query_heads, key_heads, value_heads, log_totals, grad_heads)
    )
    grad_query_r = jnp.transpose(grad_q_heads, (1, 0, 2, 3)).reshape(row_count, HEADS, HEAD_DIM)
    grad_keys_all = jnp.transpose(grad_k_heads, (1, 0, 2)).reshape(seq_span, kv_width)
    grad_values_all = jnp.transpose(grad_v_heads, (1, 0, 2)).reshape(seq_span, kv_width)
    grad_keys_r, grad_values_f = (
        lax.psum_scatter(
            grad_keys_all.astype(jnp.bfloat16), "ctx", scatter_dimension=0, tiled=True
        ).astype(jnp.float32),
        lax.psum_scatter(
            grad_values_all.astype(jnp.bfloat16), "ctx", scatter_dimension=0, tiled=True
        ).astype(jnp.float32),
    )
    grad_queries = (
        rotate(grad_query_r, pos_mine, -1.0).reshape(row_count, model_width).astype(jnp.bfloat16)
    )
    grad_keys = (
        rotate(grad_keys_r.reshape(row_count, KV_HEADS, HEAD_DIM), pos_mine, -1.0)
        .reshape(row_count, kv_width)
        .astype(jnp.bfloat16)
    )
    grad_values = grad_values_f.astype(jnp.bfloat16)
    grad_query_w = jnp.einsum(
        "sd,se->de", normed_a, grad_queries, preferred_element_type=jnp.float32
    )
    grad_key_w = jnp.einsum("sd,se->de", normed_a, grad_keys, preferred_element_type=jnp.float32)
    grad_value_w = jnp.einsum(
        "sd,se->de", normed_a, grad_values, preferred_element_type=jnp.float32
    )
    grad_normed = jnp.einsum("se,de->sd", grad_queries, query_w, preferred_element_type=jnp.float32)
    grad_normed = grad_normed + jnp.einsum(
        "se,de->sd", grad_keys, key_w, preferred_element_type=jnp.float32
    )
    grad_normed = grad_normed + jnp.einsum(
        "se,de->sd", grad_values, value_w, preferred_element_type=jnp.float32
    )
    grad_norm_a, grad_gain_a = rms_back(grad_normed, normal_a, inv_rms_a, gain_attn)
    grad_inputs = grad_middle + grad_norm_a
    summed = (
        lax.psum_scatter(grad_query_w, ("dp", "ctx", "exp"), scatter_dimension=0, tiled=True),
        lax.psum_scatter(grad_key_w, ("dp", "ctx", "exp"), scatter_dimension=0, tiled=True),
        lax.psum_scatter(grad_value_w, ("dp", "ctx", "exp"), scatter_dimension=0, tiled=True),
        lax.psum_scatter(grad_out_w, ("dp", "ctx", "exp"), scatter_dimension=0, tiled=True),
        lax.psum_scatter(grad_gain_a, ("dp", "ctx", "exp"), scatter_dimension=0, tiled=True),
        lax.psum_scatter(grad_gain_m, ("dp", "ctx", "exp"), scatter_dimension=0, tiled=True),
    )
    return (
        mixed_out,
        grad_inputs[None],
        summed[4],
        summed[0],
        summed[1],
        summed[2],
        summed[3],
        summed[5],
        grad_in_w,
        grad_down_w,
    )


def solution(mesh):
    return jax.shard_map(
        per_device,
        mesh=mesh,
        in_specs=(
            P(("dp", "exp"), "ctx", None),
            P(),
            P(("dp", "ctx", "exp"), None),
            P(("dp", "ctx", "exp"), None),
            P(("dp", "ctx", "exp"), None),
            P(("dp", "ctx", "exp"), None),
            P(),
            P("exp", ("dp", "ctx"), None),
            P("exp", ("dp", "ctx"), None),
            P(("dp", "exp"), "ctx", None),
            P(("dp", "exp"), "ctx", None),
            P(("dp", "exp"), None),
            P(("dp", "exp"), "ctx", None),
        ),
        out_specs=(
            P(("dp", "exp"), "ctx", None),
            P(("dp", "exp"), "ctx", None),
            P(("dp", "ctx", "exp")),
            P(("dp", "ctx", "exp"), None),
            P(("dp", "ctx", "exp"), None),
            P(("dp", "ctx", "exp"), None),
            P(("dp", "ctx", "exp"), None),
            P(("dp", "ctx", "exp")),
            P("exp", ("dp", "ctx"), None),
            P("exp", ("dp", "ctx"), None),
        ),
        check_vma=False,
    )
```

profile of v0, /device:TPU:0, one launch (start us, length us, event | category | flops | bytes accessed | tf_op | source)
XLA Modules:
  0.0 1936.4 jit_solution(14530424150204763785)
XLA Ops:
  10.1 58.5 %all-gather.9.cloned.1.call-done = bf16[1536,512]{1,0:T(8,128)(2,1)} async-done(((bf16[48,512]{1,0:T(8,128)(2,1)}), bf16[1536,512]{1,0:T(8,128)(2,1)}) %all-gather.9.cloned.1.call-update) | async-done | bytes 1572880 | tf_op jit(solution)/shard_map/all_gather | solution.py:90
  73.6 51.9 %all-gather.13.cloned.1.call-done = bf16[1536,512]{1,0:T(8,128)(2,1)} async-done(((bf16[48,512]{1,0:T(8,128)(2,1)}), bf16[1536,512]{1,0:T(8,128)(2,1)}) %all-gather.13.cloned.1.call-update) | async-done | bytes 1572880 | tf_op jit(solution)/shard_map/all_gather | solution.py:89
  199.0 30.0 %all-gather.17.cloned.1.call-done = bf16[1536,1536]{1,0:T(8,128)(2,1)} async-done(((bf16[48,1536]{1,0:T(8,128)(2,1)}), bf16[1536,1536]{1,0:T(8,128)(2,1)}) %all-gather.17.cloned.1.call-update) | async-done | bytes 4718608 | tf_op jit(solution)/shard_map/all_gather | solution.py:88
  240.9 19.2 all-gather.15.cloned.1.call-done
  260.1 34.6 %while.30 = (s32[]{:T(128)}, bf16[8,256,3,64]{1,3,2,0:T(8,128)(2,1)S(1)}, f32[8,3,256,1]{2,1,3,0:T(4,128)}, bf16[8,1024,64]{1,2,0:T(8,128)(2,1)S(1)}, bf16[8,102...) while((s32[]{:T(128)}, ...), condition=%wide.region_7.8_spmd.clone.clone, body=%wide.region_4.7_spmd.clone.sunk.clone | while | flops 211549440 | bytes 11079261 | solution.py:131
  294.7 30.7 %all-gather.19.cloned.1.call-done = bf16[1536,1536]{1,0:T(8,128)(2,1)} async-done(((bf16[48,1536]{1,0:T(8,128)(2,1)}), bf16[1536,1536]{1,0:T(8,128)(2,1)}) %all-gather.19.cloned.1.call-update) | async-done | bytes 4718608 | tf_op jit(solution)/shard_map/all_gather | solution.py:91
  367.8 96.3 %all-to-all-done = bf16[16,192,1536]{2,1,0:T(8,128)(2,1)} async-done(((bf16[16,192,1536]{2,1,0:T(8,128)(2,1)}), bf16[16,192,1536]{2,1,0:T(8,128)(2,1)}, u32[]{:S(2)}, u32[]{:S(2)}) %all-to-all-start) | async-done | bytes 9437216 | tf_op jit(solution)/shard_map/all_to_all | solution.py:162
  472.6 30.2 %all-gather.21.cloned.1.call-done = bf16[4,1536,1024]{2,1,0:T(8,128)(2,1)} async-done(((bf16[4,192,1024]{2,1,0:T(8,128)(2,1)}), bf16[4,1536,1024]{2,1,0:T(8,128)(2,1)}) %all-gather.21.cloned.1.call-update) | async-done | bytes 12582928 | tf_op jit(solution)/shard_map/all_gather | solution.py:142
  521.0 81.2 %all-gather.23.cloned.1.call-done = bf16[4,512,1536]{2,1,0:T(8,128)(2,1)} async-done(((bf16[4,64,1536]{2,1,0:T(8,128)(2,1)}), bf16[4,512,1536]{2,1,0:T(8,128)(2,1)}) %all-gather.23.cloned.1.call-update) | async-done | bytes 6291472 | tf_op jit(solution)/shard_map/all_gather | solution.py:143
  617.8 18.5 convolution_convert_fusion.1
  663.9 32.8 %copy.91 = bf16[4,768,1536]{2,0,1:T(4,128)(2,1)} copy(bf16[4,768,1536]{2,1,0:T(8,128)(2,1)S(1)} %convolution_convert_fusion.2) | data formatting | bytes 18874368 | tf_op jit(solution)/shard_map/convert_element_type | solution.py:168
  696.8 63.5 %all-to-all-done.3 = bf16[4,768,1536]{2,0,1:T(4,128)(2,1)} async-done(((bf16[4,768,1536]{2,0,1:T(4,128)(2,1)}), bf16[4,768,1536]{2,0,1:T(4,128)(2,1)}, u32[]{:S(2)}, u32[]{:S(2)}) %all-to-all-start.3) | async-done | bytes 9437216 | tf_op jit(solution)/shard_map/all_to_all | solution.py:200
  779.4 20.7 %gather_fusion.3 = f32[2048,1536]{1,0:T(8,128)} fusion(f32[3072,1536]{1,0:T(8,128)} %bitcast.349, s32[2048]{0:T(1024)S(1)} %broadcast_clamp_fusion), kind=kCustom, calls=%fused_computation.3 | custom fusion | bytes 25174016 | tf_op jit(solution)/shard_map/gather | solution.py:206
  808.2 62.2 %all-to-all-done.1 = bf16[4,768,1536]{2,0,1:T(4,128)(2,1)} async-done(((bf16[4,768,1536]{2,0,1:T(4,128)(2,1)}), bf16[4,768,1536]{2,0,1:T(4,128)(2,1)}, u32[]{:S(2)}, u32[]{:S(2)}) %all-to-all-start.1) | async-done | bytes 9437216 | tf_op jit(solution)/shard_map/all_to_all | solution.py:170
  879.9 18.5 gather_fusion.1
  912.8 136.7 %while.31 = (s32[]{:T(128)}, f32[8,256,3,64]{1,3,2,0:T(8,128)}, bf16[8,1024,64]{1,2,0:T(8,128)(2,1)}, bf16[8,1024,64]{1,2,0:T(8,128)(2,1)}, bf16[8,1024,64]{1,2,...) while((s32[]{:T(128)}, f32[8,256,3,64]{1,3,2,0:T(8,128)}, ...), condition=%wide.region_20.21_spmd.clone.clone, body=%wide.region_18.20_spmd.clone.sunk.clone | while | flops 515116544 | bytes 36655224 | solution.py:257
  1083.6 18.5 reduce-scatter.11.cloned.1.call-done
  1125.5 41.4 %all-reduce.2 = (f32[1536]{0:T(1024)S(1)}, f32[1536]{0:T(1024)S(1)}) all-reduce(f32[1536]{0:T(1024)S(1)} %get-tuple-element.161, f32[1536]{0:T(1024)S(1)} %get-tuple-element.159), channel_id=4, replica_groups=mesh['dp'=2,'ctx'=4,'exp'=4] {'dp','ctx','exp'}, use_global_device_ids=true, to_apply=%region_25.26.clone | all-reduce | flops 3072 | bytes 24576
  1171.1 52.6 %reduce-scatter.23.cloned.1.call-done = bf16[4,64,1536]{2,1,0:T(8,128)(2,1)} async-done(((bf16[4,512,1536]{2,1,0:T(8,128)(2,1)}), bf16[4,64,1536]{2,1,0:T(8,128)(2,1)}) %reduce-scatter.23.cloned.1.call-update) | async-done | bytes 786448 | tf_op jit(solution)/shard_map/reduce_scatter | solution.py:213
  1226.1 207.5 %reduce-scatter.21.cloned.1.call-done = bf16[4,192,1024]{2,1,0:T(8,128)(2,1)} async-done(((bf16[4,1536,1024]{2,1,0:T(8,128)(2,1)}), bf16[4,192,1024]{2,1,0:T(8,128)(2,1)}) %reduce-scatter.21.cloned.1.call-update) | async-done | bytes 1572880 | tf_op jit(solution)/shard_map/reduce_scatter | solution.py:210
  1437.2 103.2 %reduce-scatter.15.cloned.1.call-done = f32[48,512]{1,0:T(8,128)} async-done(((f32[1536,512]{1,0:T(8,128)}), f32[48,512]{1,0:T(8,128)}) %reduce-scatter.15.cloned.1.call-update) | async-done | bytes 98320 | tf_op jit(solution)/shard_map/reduce_scatter | solution.py:298
  1540.3 106.4 %reduce-scatter.17.cloned.1.call-done = f32[48,512]{1,0:T(8,128)} async-done(((f32[1536,512]{1,0:T(8,128)}), f32[48,512]{1,0:T(8,128)}) %reduce-scatter.17.cloned.1.call-update) | async-done | bytes 98320 | tf_op jit(solution)/shard_map/reduce_scatter | solution.py:299
  1646.7 141.0 %reduce-scatter.19.cloned.1.call-done = f32[48,1536]{1,0:T(8,128)} async-done(((f32[1536,1536]{1,0:T(8,128)}), f32[48,1536]{1,0:T(8,128)}) %reduce-scatter.19.cloned.1.call-update) | async-done | bytes 294928 | tf_op jit(solution)/shard_map/reduce_scatter | solution.py:300
  1787.8 141.9 %reduce-scatter.13.cloned.1.call-done = f32[48,1536]{1,0:T(8,128)} async-done(((f32[1536,1536]{1,0:T(8,128)}), f32[48,1536]{1,0:T(8,128)}) %reduce-scatter.13.cloned.1.call-update) | async-done | bytes 294928 | tf_op jit(solution)/shard_map/reduce_scatter | solution.py:297
  (313 shorter events, 494.3 us)
Async XLA Ops:
  7.2 61.5 %all-gather.9.cloned.1.call-start = ((), (), s32[]{:S(2)}) async-start(), calls=%async_computation.12 | async-start | bytes 1622016 | tf_op jit(solution)/shard_map/all_gather | solution.py:90
  7.9 117.6 %all-gather.13.cloned.1.call-start = ((), (), s32[]{:S(2)}) async-start(), calls=%async_computation.14 | async-start | bytes 1622016 | tf_op jit(solution)/shard_map/all_gather | solution.py:89
  8.7 188.9 %all-gather.11.cloned.1.call-start = ((), (), s32[]{:S(2)}) async-start(), calls=%async_computation.13 | async-start | bytes 1310720 | tf_op jit(solution)/shard_map/all_gather | solution.py:109
  10.1 225.6 %copy-start.26 = (f32[256]{0:T(256)}, f32[256]{0:T(256)S(1)}, u32[]{:S(2)}) copy-start(f32[256]{0:T(256)S(1)} %add_rsqrt_fusion.1) | copy-start | bytes 3076
  10.1 117.1 %copy-start = (bf16[1,256,1536]{2,1,0:T(8,128)(2,1)S(1)}, bf16[1,256,1536]{2,1,0:T(8,128)(2,1)}, u32[]{:S(2)}) copy-start(bf16[1,256,1536]{2,1,0:T(8,128)(2,1)} %param.17) | copy-start | bytes 2359300
  10.1 117.1 %copy-start.18 = (f32[1536]{0:T(1024)S(1)}, f32[1536]{0:T(1024)}, u32[]{:S(2)}) copy-start(f32[1536]{0:T(1024)} %param.18) | copy-start | bytes 18436
  71.7 157.3 %all-gather.17.cloned.1.call-start = ((), (), s32[]{:S(2)}) async-start(), calls=%async_computation.16 | async-start | bytes 4866048 | tf_op jit(solution)/shard_map/all_gather | solution.py:88
  72.3 187.8 %all-gather.15.cloned.1.call-start = ((), (), s32[]{:S(2)}) async-start(), calls=%async_computation.15 | async-start | bytes 1310720 | tf_op jit(solution)/shard_map/all_gather | solution.py:108
  73.6 166.1 %copy-start.13 = (f32[256,32]{0,1:T(8,128)}, f32[256,32]{0,1:T(8,128)S(1)}, u32[]{:S(2)}) copy-start(f32[256,32]{0,1:T(8,128)S(1)} %get-tuple-element.224) | copy-start | bytes 98308
  128.8 196.6 %all-gather.19.cloned.1.call-start = ((), (), s32[]{:S(2)}) async-start(), calls=%async_computation.17 | async-start | bytes 4866048 | tf_op jit(solution)/shard_map/all_gather | solution.py:91
  129.3 373.5 %all-gather.21.cloned.1.call-start = ((), (), s32[]{:S(2)}) async-start(), calls=%async_computation.18 | async-start | bytes 14155776 | tf_op jit(solution)/shard_map/all_gather | solution.py:142
  181.4 172.1 %all-to-all-start.2 = ((bf16[16,192,1536]{2,1,0:T(8,128)(2,1)}), bf16[16,192,1536]{2,1,0:T(8,128)(2,1)}, u32[]{:S(2)}, u32[]{:S(2)}) async-start(bf16[16,192,1536]{2,1,0:T(8,128)(2,1)} %multiply_convert_fusion), calls=%async_computation.2 | async-start | bytes 18874368 | tf_op jit(solution)/shard_map/all_to_all | solution.py:180
  187.2 415.0 %all-gather.23.cloned.1.call-start = ((), (), s32[]{:S(2)}) async-start(), calls=%async_computation.19 | async-start | bytes 7077888 | tf_op jit(solution)/shard_map/all_gather | solution.py:143
  353.5 110.6 %all-to-all-start = ((bf16[16,192,1536]{2,1,0:T(8,128)(2,1)}), bf16[16,192,1536]{2,1,0:T(8,128)(2,1)}, u32[]{:S(2)}, u32[]{:S(2)}) async-start(bf16[16,192,1536]{2,1,0:T(8,128)(2,1)} %broadcast_select_fusion), calls=%async_computation | async-start | bytes 18874368 | tf_op jit(solution)/shard_map/all_to_all | solution.py:162
  649.9 110.4 %all-to-all-start.3 = ((bf16[4,768,1536]{2,0,1:T(4,128)(2,1)}), bf16[4,768,1536]{2,0,1:T(4,128)(2,1)}, u32[]{:S(2)}, u32[]{:S(2)}) async-start(bf16[4,768,1536]{2,0,1:T(4,128)(2,1)} %copy.96), calls=%async_computation.3 | async-start | bytes 18874368 | tf_op jit(solution)/shard_map/all_to_all | solution.py:200
  760.3 110.2 %all-to-all-start.1 = ((bf16[4,768,1536]{2,0,1:T(4,128)(2,1)}), bf16[4,768,1536]{2,0,1:T(4,128)(2,1)}, u32[]{:S(2)}, u32[]{:S(2)}) async-start(bf16[4,768,1536]{2,0,1:T(4,128)(2,1)} %copy.91), calls=%async_computation.1 | async-start | bytes 18874368 | tf_op jit(solution)/shard_map/all_to_all | solution.py:170
  766.0 313.8 %reduce-scatter.9.cloned.1.call-start = ((), (), s32[]{:S(2)}) async-start(), calls=%async_computation.20 | async-start | bytes 1310720 | tf_op jit(solution)/shard_map/reduce_scatter | solution.py:264
  1049.5 52.7 %reduce-scatter.11.cloned.1.call-start = ((), (), s32[]{:S(2)}) async-start(), calls=%async_computation.21 | async-start | bytes 1310720 | tf_op jit(solution)/shard_map/reduce_scatter | solution.py:267
  1050.1 173.6 %reduce-scatter.23.cloned.1.call-start = ((), (), s32[]{:S(2)}) async-start(), calls=%async_computation.27 | async-start | bytes 7077888 | tf_op jit(solution)/shard_map/reduce_scatter | solution.py:213
  1061.7 372.0 %reduce-scatter.21.cloned.1.call-start = ((), (), s32[]{:S(2)}) async-start(), calls=%async_computation.26 | async-start | bytes 14155776 | tf_op jit(solution)/shard_map/reduce_scatter | solution.py:210
  1079.8 460.5 %reduce-scatter.15.cloned.1.call-start = ((), (), s32[]{:S(2)}) async-start(), calls=%async_computation.23 | async-start | bytes 3244032 | tf_op jit(solution)/shard_map/reduce_scatter | solution.py:298
  1083.6 563.2 %reduce-scatter.17.cloned.1.call-start = ((), (), s32[]{:S(2)}) async-start(), calls=%async_computation.24 | async-start | bytes 3244032 | tf_op jit(solution)/shard_map/reduce_scatter | solution.py:299
  1105.5 682.3 %reduce-scatter.19.cloned.1.call-start = ((), (), s32[]{:S(2)}) async-start(), calls=%async_computation.25 | async-start | bytes 9732096 | tf_op jit(solution)/shard_map/reduce_scatter | solution.py:300
  1110.6 819.0 %reduce-scatter.13.cloned.1.call-start = ((), (), s32[]{:S(2)}) async-start(), calls=%async_computation.22 | async-start | bytes 9732096 | tf_op jit(solution)/shard_map/reduce_scatter | solution.py:297
  (36 other events, 614.6 us)
Sparse Core Ops, SparseCore 0:
  10.9 57.6 all-gather.8
  71.5 53.8 all-gather.12
  127.6 26.8 all-gather.10
  157.3 71.7 all-gather.16
  231.0 29.0 all-gather.14
  262.8 62.5 all-gather.18
  327.5 175.2 all-gather.20
  504.9 97.2 all-gather.22
  1049.6 24.4 reduce-scatter.8
  1076.3 25.7 reduce-scatter.10
  1105.7 117.9 reduce-scatter.22
  1227.1 206.5 reduce-scatter.20
  1439.7 100.6 reduce-scatter.14
  1546.2 100.4 reduce-scatter.16
  1653.1 134.6 reduce-scatter.18
  1795.1 134.4 reduce-scatter.12
where the time goes:
time: 1950 us; the launch traced here: 1940 us
  waiting for transfers between devices  1300 us (67%)
  matrix products  274 us (14%)
  local copies, waits for them, and re-layouts  205 us (11%)
  other arithmetic  76.1 us (4%)
  blocking collectives  41.4 us (2%)
  starting transfers between devices  24.6 us (1%)
    reduce_scatter x1, waiting for transfers between devices, per_device(): lax.psum_scatter(grad_in_part.astype(jnp.bfloat16), ('dp', 'ctx'), scatte...  208 us
    reduce_scatter x1, waiting for transfers between devices, per_device(): lax.psum_scatter(grad_query_w, ('dp', 'ctx', 'exp'), scatter_dimension=0,...  142 us
    reduce_scatter x1, waiting for transfers between devices, per_device(): lax.psum_scatter(grad_out_w, ('dp', 'ctx', 'exp'), scatter_dimension=0, t...  141 us
    reduce_scatter x1, waiting for transfers between devices, per_device(): lax.psum_scatter(grad_value_w, ('dp', 'ctx', 'exp'), scatter_dimension=0,...  106 us
    reduce_scatter x1, waiting for transfers between devices, per_device(): lax.psum_scatter(grad_key_w, ('dp', 'ctx', 'exp'), scatter_dimension=0, t...  103 us
    all_to_all x1, waiting for transfers between devices, per_device(): lax.all_to_all(outgoing, 'exp', split_axis=0, concat_axis=1, tiled=True)  96.3 us
    all_gather x1, waiting for transfers between devices, per_device(): lax.all_gather(w_down, ('dp', 'ctx'), axis=1, tiled=True)  81.2 us
    all_to_all x1, waiting for transfers between devices, per_device(): lax.all_to_all(grad_rows.astype(jnp.bfloat16), 'exp', split_axis=1, conca...  63.5 us
  transfers between devices with their start and end apart: 20, of which 17 were waited for; matrix products, arithmetic and copies ran while one was open for 17% of the time, Pallas kernels for 0%

commit v1 on v0

v1 whole, which is shorter than its diff:
```python
import functools

import jax
import jax.numpy as jnp
from jax import lax
from jax.experimental import pallas as pl
from jax.experimental.pallas import tpu as pltpu
from jax.sharding import PartitionSpec as P

HEADS = 24
KV_HEADS = 8
HEAD_DIM = 64
FF = 512
TOP = 8

eps_norm = 1e-06
score_scale = 0.015625
residual_scale = 0.22
rope_base = 10000.0

BF = jnp.bfloat16
F32 = jnp.float32
SCALE = 3
VMEM_LIMIT = 60 * 1024 * 1024
ANY = pl.BlockSpec(memory_space=pl.ANY)
VM = pl.BlockSpec(memory_space=pltpu.VMEM)
SM = pl.BlockSpec(memory_space=pltpu.SMEM)
NN = (((1,), (0,)), ((), ()))
NT = (((1,), (1,)), ((), ()))
TN = (((0,), (0,)), ((), ()))


def mm(a, b, dims=NN):
    return lax.dot_general(a, b, dims, preferred_element_type=F32)


def params(**kw):
    return pltpu.CompilerParams(vmem_limit_bytes=VMEM_LIMIT, **kw)


def cost(flops, nbytes, trans=0):
    return pl.CostEstimate(
        flops=int(flops / SCALE), bytes_accessed=int(nbytes / SCALE), transcendentals=0
    )


def shift(x, axis, by):
    n = lax.axis_size(axis)
    return lax.ppermute(x, axis, [(i, (i + by) % n) for i in range(n)])


def flip(x, axis, mask):
    n = lax.axis_size(axis)
    return lax.ppermute(x, axis, [(i, i ^ mask) for i in range(n)])


class Stages:
    def __init__(self, token):
        self.token = token

    def hold(self, x):
        leaves, tree = jax.tree.flatten(x)
        leaves = [lax.optimization_barrier((leaf, self.token))[0] for leaf in leaves]
        return jax.tree.unflatten(tree, leaves)

    def end(self, *outs):
        self.token = lax.optimization_barrier((self.token, *jax.tree.leaves(outs)))[0]


def ring(x, axis):
    out = [x]
    for _ in range(lax.axis_size(axis) - 1):
        out.append(shift(out[-1], axis, 1))
    return out


def hop(x, pairs):
    return lax.ppermute(x, "ctx", pairs)


UP, DOWN = [(0, 1), (1, 2), (2, 3)], [(1, 0), (2, 1), (3, 2)]
ACROSS = [(0, 2), (1, 3), (2, 0), (3, 1)]
INNER, OUTER = [(0, 1), (3, 2)], [(1, 0), (2, 3)]


def line_places(z):
    return [z, jnp.bitwise_xor(z, 2), jnp.where(z == 0, 3, z - 1), jnp.where(z == 3, 0, z + 1)]


def line_gather(across, below, above, end, x):
    z = lax.axis_index("ctx")
    return [x, across, jnp.where(z == 0, end, below), jnp.where(z == 3, end, above)]


def pick(x, index, dim=0):
    return lax.dynamic_index_in_dim(x, index, dim, False)


def dp_reduce(parts):
    n = lax.axis_size("dp")
    total = parts[n - 1]
    for k in range(1, n):
        total = (shift(total, "dp", 1).astype(F32) + parts[n - 1 - k].astype(F32)).astype(BF)
    return total


def assemble(found, places):
    found = [t.reshape(-1, *t.shape[-2:]) for t in found]
    each, rows, width = found[0].shape
    count = each * len(found)
    total = count * rows
    if rows % 16:
        blocks = jnp.concatenate(found)
        return jnp.zeros_like(blocks).at[places].set(blocks).reshape(total, width)

    def body(places_ref, *refs):
        refs, out_ref, sems = refs[:-2], refs[-2], refs[-1]
        copies = []
        for i in range(count):
            at = pl.multiple_of(places_ref[i] * rows, rows)
            copies.append(
                pltpu.make_async_copy(refs[i // each].at[i % each], out_ref.at[pl.ds(at, rows), :], sems.at[i])
            )
        for copy in copies:
            copy.start()
        for copy in copies:
            copy.wait()

    return pl.pallas_call(
        body,
        out_shape=jax.ShapeDtypeStruct((total, width), found[0].dtype),
        in_specs=[SM] + [ANY] * len(found),
        out_specs=VM,
        scratch_shapes=[pltpu.SemaphoreType.DMA((count,))],
        compiler_params=params(),
        cost_estimate=cost(0, 4 * total * width),
        name="assemble",
    )(places, *found)


def rms(v):
    return lax.rsqrt(jnp.mean(v * v, axis=-1, keepdims=True) + eps_norm)


def turn(block, cos, sin):
    lane = lax.broadcasted_iota(jnp.int32, block.shape, 1)
    partner = jnp.where(
        (lane & 63) < 32, pltpu.roll(block, 96, 1), pltpu.roll(block, 32, 1)
    )
    return block * cos + partner * sin


def project(tok, gain, w, cos, sin, block_at):
    rows, d = tok.shape
    n = w.shape[1]
    blocks = (n - 128) // 128

    def body(at_ref, tok_ref, gain_ref, w_ref, cos_ref, sin_ref, out_ref):
        t = tok_ref[...].astype(F32)
        normed = (t * rms(t) * gain_ref[...]).astype(BF)
        u = mm(normed, w_ref[...])
        for b in range(blocks):
            out_ref[:, b * 128 : (b + 1) * 128] = turn(
                u[:, b * 128 : (b + 1) * 128], cos_ref[...], sin_ref[...]
            ).astype(BF)
        out_ref[:, blocks * 128 :] = u[:, blocks * 128 :].astype(BF)

    return pl.pallas_call(
        body,
        grid_spec=pltpu.PrefetchScalarGridSpec(
            num_scalar_prefetch=1,
            grid=(1,),
            in_specs=[
                pl.BlockSpec((rows, d), lambda i, at: (0, 0)),
                pl.BlockSpec((1, d), lambda i, at: (0, 0)),
                pl.BlockSpec((d, n), lambda i, at: (0, 0)),
                pl.BlockSpec((rows, 128), lambda i, at: (at[0], 0)),
                pl.BlockSpec((rows, 128), lambda i, at: (at[0], 0)),
            ],
            out_specs=pl.BlockSpec((rows, n), lambda i, at: (0, 0)),
        ),
        out_shape=jax.ShapeDtypeStruct((rows, n), BF),
        compiler_params=params(),
        cost_estimate=cost(2 * rows * d * n, 2 * d * n + 4 * rows * d),
        name="project",
    )(block_at, tok, gain, w, cos, sin)


def swapped(e):
    return (e & 1) * 2 + (e >> 1)


def lower_half(shape):
    return lax.broadcasted_iota(jnp.int32, shape, 1) < 64


def stage_heads(block, dst, rows_at, heads, factor):
    rows = block.shape[0]
    low = lower_half((rows, 128))
    for h in range(heads):
        part = block[:, (h // 2) * 128 : (h // 2 + 1) * 128].astype(F32) * factor
        keep = low if h % 2 == 0 else jnp.logical_not(low)
        dst[h, rows_at, :] = jnp.where(keep, part, 0.0).astype(BF)


def doubled(block):
    block = block.astype(F32)
    low = lower_half(block.shape)
    other = pltpu.roll(block, 64, 1)
    return jnp.where(low, block, other), jnp.where(low, other, block)


def allowed_mask(s_ref, keys, rows, first):
    q = lax.broadcasted_iota(jnp.int32, (1, rows), 1) + first
    begin = jnp.zeros_like(q)
    for i in range(5, s_ref.shape[0] - 1):
        begin = jnp.where(q >= s_ref[i], jnp.maximum(begin, s_ref[i]), begin)
    k = lax.broadcasted_iota(jnp.int32, (keys, rows), 0)
    return (k >= begin) & (k <= q)


def attend(scalars, pieces, heads, kvs):
    blocks = len(pieces)
    rows, width = pieces[0].shape
    span = blocks * rows
    qw = heads * HEAD_DIM
    share = heads // kvs

    def body(s_ref, *refs):
        ins, (out_ref, lse_ref, qs, kd, vd, vt, ob) = refs[:blocks], refs[blocks:]
        me = s_ref[4]
        for k in range(blocks):
            at = pl.ds(pl.multiple_of(s_ref[k] * rows, rows), rows)
            block = ins[k][...]
            stage_heads(block, qs, at, heads, score_scale)
            for i, x in enumerate(doubled(block[:, qw : qw + 128])):
                kd[i, at, :] = x.astype(BF)
            for i, x in enumerate(doubled(block[:, qw + 128 : qw + 256])):
                vd[i, at, :] = x
        for i in range(kvs):
            vt[i] = vd[i].T.astype(BF)

        def one(h, _):
            kv = h // share
            for p in range(blocks):
                keys = (p + 1) * rows
                q = qs[h, p * rows : (p + 1) * rows, :]
                s = mm(kd[kv, :keys, :], q, NT)
                s = jnp.where(allowed_mask(s_ref, keys, rows, p * rows), s, -1e30)
                peak = jnp.max(s, axis=0, keepdims=True)
                e = jnp.exp(s - peak)
                total = jnp.sum(e, axis=0, keepdims=True)
                o = mm(vt[kv, :, :keys], e.astype(BF)) / total
                ob[h, p * rows : (p + 1) * rows, :] = o.T
                lse_ref[pl.ds(h, 1), p * rows : (p + 1) * rows] = peak + jnp.log(total)
            return 0

        lax.fori_loop(0, heads, one, 0)
        low = lower_half((rows, 128))
        for p in range(blocks):
            to = lax.rem(p - me + blocks, blocks)
            for b in range(heads // 2):
                at = slice(p * rows, (p + 1) * rows)
                out_ref[to, :, b * 128 : (b + 1) * 128] = jnp.where(
                    low, ob[2 * b, at, :], ob[2 * b + 1, at, :]
                ).astype(BF)

    pairs = heads * rows * rows * blocks * (blocks + 1) // 2
    return pl.pallas_call(
        body,
        out_shape=(
            jax.ShapeDtypeStruct((blocks, rows, qw), BF),
            jax.ShapeDtypeStruct((8, span), F32),
        ),
        in_specs=[SM] + [VM] * blocks,
        out_specs=(VM, VM),
        scratch_shapes=[
            pltpu.VMEM((heads, span, 128), BF),
            pltpu.VMEM((kvs, span, 128), BF),
            pltpu.VMEM((kvs, span, 128), F32),
            pltpu.VMEM((kvs, 128, span), BF),
            pltpu.VMEM((heads, span, 128), F32),
        ],
        compiler_params=params(),
        cost_estimate=cost(pairs * 1024, 4 * span * width, pairs),
        name="attend",
    )(scalars, *pieces)


def attend_back(scalars, pieces, grads, lse, cos, sin, heads, kvs):
    blocks = len(pieces)
    rows, width = pieces[0].shape
    span = blocks * rows
    qw = heads * HEAD_DIM
    share = heads // kvs

    def body(s_ref, *refs):
        ins, gins = refs[:blocks], refs[blocks : 2 * blocks]
        lse_ref, cos_ref, sin_ref, out_ref, qs, gs, kd, kf, kt, vd, dk, dv, dq = refs[2 * blocks :]
        me = s_ref[4]
        for k in range(blocks):
            at = pl.ds(pl.multiple_of(s_ref[k] * rows, rows), rows)
            block = ins[k][...]
            stage_heads(block, qs, at, heads, score_scale)
            for i, x in enumerate(doubled(block[:, qw : qw + 128])):
                kd[i, at, :] = x.astype(BF)
                kf[i, at, :] = x
            for i, x in enumerate(doubled(block[:, qw + 128 : qw + 256])):
                vd[i, at, :] = x.astype(BF)
            at = pl.ds(pl.multiple_of(lax.rem(me + k, blocks) * rows, rows), rows)
            stage_heads(gins[k][...], gs, at, heads, 1.0)
        for i in range(kvs):
            kt[i] = kf[i].T.astype(BF)
        dk[...] = jnp.zeros_like(dk)
        dv[...] = jnp.zeros_like(dv)

        def one(h, _):
            kv = h // share
            for p in range(blocks):
                keys = (p + 1) * rows
                at = slice(p * rows, (p + 1) * rows)
                q = qs[h, at, :]
                g = gs[h, at, :]
                s = mm(kd[kv, :keys, :], q, NT)
                log_total = lse_ref[pl.ds(h, 1), at]
                chances = jnp.where(
                    allowed_mask(s_ref, keys, rows, p * rows), jnp.exp(s - log_total), 0.0
                )
                gp = mm(vd[kv, :keys, :], g, NT)
                row_dot = jnp.sum(chances * gp, axis=0, keepdims=True)
                ds = (chances * (gp - row_dot)).astype(BF)
                dq[h, at, :] = mm(kt[kv, :, :keys], ds).T
                dk[kv, :keys, :] += mm(ds, q)
                dv[kv, :keys, :] += mm(chances.astype(BF), g)
            return 0

        lax.fori_loop(0, heads, one, 0)
        low = lower_half((rows, 128))
        for p in range(blocks):
            at = slice(p * rows, (p + 1) * rows)
            cosine, sine = cos_ref[at, :], -sin_ref[at, :]
            for b in range(heads // 2):
                x = jnp.where(low, dq[2 * b, at, :], dq[2 * b + 1, at, :]) * score_scale
                out_ref[at, b * 128 : (b + 1) * 128] = turn(x, cosine, sine).astype(BF)
            k0, k1, v0, v1 = dk[0, at, :], dk[1, at, :], dv[0, at, :], dv[1, at, :]
            k0, k1 = k0 + pltpu.roll(k0, 64, 1), k1 + pltpu.roll(k1, 64, 1)
            v0, v1 = v0 + pltpu.roll(v0, 64, 1), v1 + pltpu.roll(v1, 64, 1)
            out_ref[at, qw : qw + 128] = turn(jnp.where(low, k0, k1), cosine, sine).astype(BF)
            out_ref[at, qw + 128 : qw + 256] = jnp.where(low, v0, v1).astype(BF)

    pairs = heads * rows * rows * blocks * (blocks + 1) // 2
    return pl.pallas_call(
        body,
        out_shape=jax.ShapeDtypeStruct((span, width), BF),
        in_specs=[SM] + [VM] * (2 * blocks + 3),
        out_specs=VM,
        scratch_shapes=[
            pltpu.VMEM((heads, span, 128), BF),
            pltpu.VMEM((heads, span, 128), BF),
            pltpu.VMEM((kvs, span, 128), BF),
            pltpu.VMEM((kvs, span, 128), F32),
            pltpu.VMEM((kvs, 128, span), BF),
            pltpu.VMEM((kvs, span, 128), BF),
            pltpu.VMEM((kvs, span, 128), F32),
            pltpu.VMEM((kvs, span, 128), F32),
            pltpu.VMEM((heads, span, 128), F32),
        ],
        compiler_params=params(),
        cost_estimate=cost(pairs * 2560, 8 * span * width, pairs),
        name="attend_back",
    )(scalars, *pieces, *grads, lse, cos, sin)


def join(scalars, mixes, w_out, tok, gain):
    blocks = len(mixes)
    rows, part = mixes[0].shape
    d = tok.shape[1]

    def body(s_ref, *refs):
        ins, (w_ref, tok_ref, gain_ref, mid_ref, hid_ref) = refs[:blocks], refs[blocks:]
        me = s_ref[4]
        branch = jnp.zeros((rows, d), F32)
        for k in range(blocks):
            at = pl.ds(pl.multiple_of(lax.rem(me - k + blocks, blocks) * part, part), part)
            branch = branch + mm(ins[k][...], w_ref[at, :])
        middle = tok_ref[...].astype(F32) + residual_scale * branch
        mid_ref[...] = middle
        hid_ref[...] = (middle * rms(middle) * gain_ref[...]).astype(BF)

    return pl.pallas_call(
        body,
        out_shape=(jax.ShapeDtypeStruct((rows, d), F32), jax.ShapeDtypeStruct((rows, d), BF)),
        in_specs=[SM] + [VM] * (blocks + 3),
        out_specs=(VM, VM),
        compiler_params=params(),
        cost_estimate=cost(2 * rows * d * d, 2 * d * d + 10 * rows * d),
        name="join",
    )(scalars, *mixes, w_out, tok, gain)


def join_back(scalars, addends, middle, cot, gain, w_out, mixes, here, nd, ne):
    blocks = len(mixes)
    rows, part = mixes[0].shape
    d = middle.shape[1]

    w_rows = d // (nd * blocks * ne)

    def body(s_ref, here_ref, a_ref, b_ref, c_ref, mid_ref, cot_ref, gain_ref, w_ref, *refs):
        ins, (gmid_ref, gmix_ref, gw_ref, gg_ref) = refs[:blocks], refs[blocks:]
        me = s_ref[4]
        grad_hidden = a_ref[...].astype(F32) + b_ref[...].astype(F32) + c_ref[...].astype(F32)
        middle = mid_ref[...]
        inv = rms(middle)
        normal = middle * inv
        gg_ref[...] = jnp.sum(grad_hidden * normal, axis=0, keepdims=True)
        u = grad_hidden * gain_ref[...]
        grad_middle = cot_ref[...] + inv * (u - normal * jnp.mean(u * normal, axis=-1, keepdims=True))
        gmid_ref[...] = grad_middle
        branch = (residual_scale * grad_middle).astype(BF)
        for k in range(blocks):
            at = pl.ds(pl.multiple_of(lax.rem(me - k + blocks, blocks) * part, part), part)
            gmix_ref[k] = mm(branch, w_ref[at, :], NT).astype(BF)
            gw = mm(ins[k][...], branch, TN)
            for i in range(part // w_rows):
                q = lax.rem(me - k + blocks, blocks) * (part // w_rows) + i
                e = swapped(jnp.bitwise_xor(lax.rem(q, ne), here_ref[3]))
                b = lax.div(q, ne)
                m = lax.rem(lax.div(b, blocks) - here_ref[0] + nd, nd)
                gw_ref[e, m, lax.rem(b, blocks)] = gw[i * w_rows : (i + 1) * w_rows, :].astype(BF)

    return pl.pallas_call(
        body,
        out_shape=(
            jax.ShapeDtypeStruct((rows, d), F32),
            jax.ShapeDtypeStruct((blocks, rows, part), BF),
            jax.ShapeDtypeStruct((ne, nd, blocks, w_rows, d), BF),
            jax.ShapeDtypeStruct((1, d), F32),
        ),
        in_specs=[SM, SM] + [VM] * (7 + blocks),
        out_specs=(VM, VM, VM, VM),
        compiler_params=params(),
        cost_estimate=cost(4 * rows * d * d, 4 * d * d + 18 * rows * d),
        name="join_back",
    )(scalars, here, *addends, middle, cot, gain, w_out, *mixes)


def halves(w, odd, devices):
    n, r, width = w.shape
    unit = FF // devices
    if 2 * unit != 128:
        parts = w.reshape(n, r, 2, devices // 4, 2, 2, unit)
        parts = jnp.transpose(parts, (5, 0, 1, 2, 3, 4, 6)).reshape(2, n, r, FF)
        return pick(parts, odd), pick(parts, 1 - odd)

    def body(odd_ref, w_ref, mine_ref, their_ref):
        low = lower_half((r, 128))
        even = odd_ref[0] == 0
        for m in range(width // 256):
            a = w_ref[0, :, 2 * m * 128 : (2 * m + 1) * 128].astype(F32)
            b = w_ref[0, :, (2 * m + 1) * 128 : (2 * m + 2) * 128].astype(F32)
            evens = jnp.where(low, a, pltpu.roll(b, 64, 1))
            odds = jnp.where(low, pltpu.roll(a, 64, 1), b)
            at = slice(m * 128, (m + 1) * 128)
            mine_ref[0, :, at] = jnp.where(even, evens, odds).astype(BF)
            their_ref[0, :, at] = jnp.where(even, odds, evens).astype(BF)

    spec = pl.BlockSpec((1, r, FF), lambda e: (e, 0, 0))
    return pl.pallas_call(
        body,
        grid=(n,),
        out_shape=(jax.ShapeDtypeStruct((n, r, FF), BF),) * 2,
        in_specs=[SM, pl.BlockSpec((1, r, width), lambda e: (e, 0, 0))],
        out_specs=(spec, spec),
        compiler_params=params(),
        cost_estimate=cost(0, 4 * n * r * width),
        name="halves",
    )(odd[None].astype(jnp.int32), w)


def whole(own, other, theirs, odd, devices):
    _, r, width = own.shape
    r3 = r // 3
    unit = FF // devices
    if 2 * unit != 128:
        total = own.astype(F32) + other.astype(F32)
        theirs = theirs.astype(F32)
        parts = jnp.stack([jnp.where(odd == 0, total[0], theirs), jnp.where(odd == 0, theirs, total[0])])
        parts = parts.reshape(2, r, 2, devices // 4, 2, unit)
        down = [total[2, b * r3 : (b + 1) * r3] for b in range(3)]
        return jnp.transpose(parts, (1, 2, 3, 4, 0, 5)).reshape(r, 2 * width), jnp.concatenate(down, axis=1)

    def body(odd_ref, own_ref, other_ref, their_ref, in_ref, down_ref):
        low = lower_half((r, 128))
        even = odd_ref[0] == 0
        for m in range(width // 128):
            at = slice(m * 128, (m + 1) * 128)
            mine = own_ref[0, :, at].astype(F32) + other_ref[0, :, at].astype(F32)
            their = their_ref[:, at].astype(F32)
            evens, odds = jnp.where(even, mine, their), jnp.where(even, their, mine)
            in_ref[:, 2 * m * 128 : (2 * m + 1) * 128] = jnp.where(low, evens, pltpu.roll(odds, 64, 1))
            in_ref[:, (2 * m + 1) * 128 : (2 * m + 2) * 128] = jnp.where(low, pltpu.roll(evens, 64, 1), odds)
        for b in range(3):
            at = slice(b * r3, (b + 1) * r3)
            down_ref[:, b * width : (b + 1) * width] = own_ref[2, at, :].astype(F32) + other_ref[2, at, :].astype(F32)

    return pl.pallas_call(
        body,
        out_shape=(
            jax.ShapeDtypeStruct((r, 2 * width), F32),
            jax.ShapeDtypeStruct((r3, 3 * width), F32),
        ),
        in_specs=[SM, VM, VM, VM],
        out_specs=(VM, VM),
        compiler_params=params(),
        cost_estimate=cost(0, 20 * r * width),
        name="whole",
    )(odd[None].astype(jnp.int32), own, other, theirs)


def experts_rows(places, which, rows_in, cots, shards, sums, last):
    piece, d = rows_in[0].shape
    group = 2
    rows = piece * group
    tiles = len(rows_in) // group
    total = rows * tiles
    count = len(shards)
    n, _, r, width = shards[0].shape
    half = width // 2
    r3 = r // 3
    first = sums is None

    def body(places_ref, *refs):
        n_in = tiles * group
        h_refs, c_refs, refs = refs[:n_in], refs[n_in : 2 * n_in], refs[2 * n_in :]
        w_refs, refs = refs[:count], refs[count:]
        if not first:
            in_h, in_o, refs = refs[0], refs[1], refs[2:]
        if last:
            out_h, rest_h, out_o, rest_o, gb_ref, gat_ref, *refs = refs
        else:
            out_h, out_o, gb_ref, gat_ref, *refs = refs
        if first:
            ht_ref, *refs = refs
        wiv, wdv, ga_ref, hv, cv, sems, row_sems = refs
        t = pl.program_id(0)
        moves = []
        for i in range(n_in):
            at = pl.ds(i % group * piece, piece)
            moves.append(
                (
                    pltpu.make_async_copy(h_refs[i], hv.at[i // group, at, :], row_sems.at[0, i]),
                    pltpu.make_async_copy(c_refs[i], cv.at[i // group, at, :], row_sems.at[1, i]),
                )
            )

        @pl.when(t == 0)
        def _():
            copies = []
            for i in range(count):
                for e in range(n):
                    parts = []
                    for b in range(2):
                        at = pl.multiple_of(places_ref[3 * i + b] * r, r)
                        parts.append((w_refs[i].at[e, b], wiv.at[pl.ds(at, r), e * width : (e + 1) * width]))
                    at = pl.multiple_of(places_ref[3 * i + 2] * r3 + e * half, r3)
                    for b in range(3):
                        parts.append(
                            (
                                w_refs[i].at[e, 2, b * r3 : (b + 1) * r3, :],
                                wdv.at[pl.ds(at, r3), b * width : (b + 1) * width],
                            )
                        )
                    for k, (a, b) in enumerate(parts):
                        copies.append(pltpu.make_async_copy(a, b, sems.at[i, e, k]))
            for copy in copies:
                copy.start()
            for a, b in moves:
                a.start()
                b.start()
            for copy in copies:
                copy.wait()

        for i in range(tiles):

            @pl.when(t == i)
            def _():
                for a, b in moves[i * group : (i + 1) * group]:
                    a.wait()
                    b.wait()

        h = hv[t]
        c = cv[t, :, :d]
        gates = cv[t, :, d:].astype(F32)
        lane = lax.broadcasted_iota(jnp.int32, gates.shape, 1) - places_ref[3 * count]
        for e in range(n):
            g = jnp.sum(jnp.where(lane == which + e, gates, 0.0), axis=1, keepdims=True)
            gu = mm(h, wiv[:, e * width : (e + 1) * width])
            gate, up = gu[:, :half], gu[:, half:]
            sg = jax.nn.sigmoid(gate)
            silu = gate * sg
            ga = mm(c, wdv[e * half : (e + 1) * half, :], NT) * g
            ga_ref[:, e * half : (e + 1) * half] = (silu * up * g).astype(BF)
            gb_ref[:, e * width : e * width + half] = (ga * up * (sg + silu * (1.0 - sg))).astype(BF)
            gb_ref[:, e * width + half : (e + 1) * width] = (ga * silu).astype(BF)
        o = mm(ga_ref[...], wdv[...])
        gh = mm(gb_ref[...], wiv[...], NT)
        gat_ref[...] = ga_ref[...].T
        if first:
            ht_ref[...] = h.T
        if not first:
            o = o + in_o[...]
            gh = gh + in_h[...]
        if last:

            @pl.when(t < tiles // 2)
            def _():
                out_o[...] = o.astype(BF)
                out_h[...] = gh.astype(BF)

            @pl.when(t >= tiles // 2)
            def _():
                rest_o[...] = o.astype(BF)
                rest_h[...] = gh.astype(BF)

        else:
            out_o[...] = o
            out_h[...] = gh

    tile = lambda c: pl.BlockSpec((rows, c), lambda t: (t, 0))
    flat = lambda c: pl.BlockSpec((c, rows), lambda t: (0, t))
    if last:
        sum_shapes = (jax.ShapeDtypeStruct((total // 2, d), BF),) * 4
        front = pl.BlockSpec((rows, d), lambda t: (jnp.minimum(t, tiles // 2 - 1), 0))
        back = pl.BlockSpec((rows, d), lambda t: (jnp.maximum(t - tiles // 2, 0), 0))
        sum_specs = (front, back, front, back)
    else:
        sum_shapes = (jax.ShapeDtypeStruct((total, d), F32),) * 2
        sum_specs = (tile(d), tile(d))
    return pl.pallas_call(
        body,
        grid=(tiles,),
        out_shape=sum_shapes
        + (
            jax.ShapeDtypeStruct((total, n * width), BF),
            jax.ShapeDtypeStruct((n * half, total), BF),
        )
        + ((jax.ShapeDtypeStruct((d, total), BF),) if first else ()),
        in_specs=[SM]
        + [ANY] * (2 * len(rows_in) + count)
        + ([] if first else [tile(d), tile(d)]),
        out_specs=sum_specs + (tile(n * width), flat(n * half)) + ((flat(d),) if first else ()),
        scratch_shapes=[
            pltpu.VMEM((d, n * width), BF),
            pltpu.VMEM((n * half, d), BF),
            pltpu.VMEM((rows, n * half), BF),
            pltpu.VMEM((tiles, rows, d), BF),
            pltpu.VMEM((tiles, rows, cots[0].shape[1]), BF),
            pltpu.SemaphoreType.DMA((count, n, 5)),
            pltpu.SemaphoreType.DMA((2, len(rows_in))),
        ],
        compiler_params=params(),
        cost_estimate=cost(6 * n * total * d * width, 50e6, n * total * half),
        name="experts_rows",
    )(places, *rows_in, *cots, *shards, *(() if first else sums))


def experts_weights(scalars, rows_t, cots, gb, ga_t, n, devices):
    d, total = rows_t.shape
    width, half = gb.shape[1] // n, ga_t.shape[0] // n
    r = d // devices
    r3 = r // 3
    nd = devices // 4
    tiles = len(cots)
    rows = total // tiles

    def body(s_ref, h_any, gb_any, ga_any, *refs):
        c_refs, refs = refs[:tiles], refs[tiles:]
        outs, (down, h_ref, gb_ref, ga_ref, c_ref, stage, sems, c_sems, out_sems) = refs[: n * nd], refs[n * nd :]
        ahead = [lax.rem(s_ref[0] + k, nd) for k in range(nd)]
        spans = [pl.ds(pl.multiple_of(x * 4 * r, 4 * r), 4 * r) for x in ahead]
        first = [pltpu.make_async_copy(gb_any, gb_ref, sems.at[0])]
        first += [
            pltpu.make_async_copy(h_any.at[spans[k], :], h_ref.at[k], sems.at[1 + k]) for k in range(nd)
        ]
        second = [pltpu.make_async_copy(ga_any, ga_ref, c_sems.at[tiles])]
        second += [
            pltpu.make_async_copy(c_refs[i].at[:, :d], c_ref.at[pl.ds(i * rows, rows), :], c_sems.at[i])
            for i in range(tiles)
        ]
        for copy in first + second:
            copy.start()
        first[0].wait()
        for k in range(nd):
            first[1 + k].wait()
            part = mm(h_ref[k], gb_ref[...]).astype(BF)
            for z in range(4):
                where = jnp.bitwise_xor(s_ref[2], z // 2)
                slot = jnp.bitwise_xor(s_ref[1], z % 2)
                for e in range(n):
                    stage[e * nd + k, where, slot] = part[z * r : (z + 1) * r, e * width : (e + 1) * width]
        for copy in second:
            copy.wait()
        leaving = []
        for e in range(n):
            down[...] = mm(ga_ref[e * half : (e + 1) * half, :], c_ref[...]).astype(BF)
            for k in range(nd):
                for z in range(2):
                    where = jnp.bitwise_xor(s_ref[2], z)
                    at = pl.ds(pl.multiple_of((2 * ahead[k] + z) * r3, r3), r3)
                    for b in range(3):
                        stage[e * nd + k, where, 2, b * r3 : (b + 1) * r3, :] = down[
                            at, b * width : (b + 1) * width
                        ]
                leaving.append(
                    pltpu.make_async_copy(stage.at[e * nd + k], outs[e * nd + k], out_sems.at[e * nd + k])
                )
                leaving[-1].start()
        for copy in leaving:
            copy.wait()

    outs = pl.pallas_call(
        body,
        out_shape=[jax.ShapeDtypeStruct((2, 3, r, width), BF)] * (n * nd),
        in_specs=[SM] + [ANY] * (3 + tiles),
        out_specs=[ANY] * (n * nd),
        scratch_shapes=[
            pltpu.VMEM((half, d), BF),
            pltpu.VMEM((nd, 4 * r, total), BF),
            pltpu.VMEM((total, n * width), BF),
            pltpu.VMEM((n * half, total), BF),
            pltpu.VMEM((total, d), BF),
            pltpu.VMEM((n * nd, 2, 3, r, width), BF),
            pltpu.SemaphoreType.DMA((1 + nd,)),
            pltpu.SemaphoreType.DMA((tiles + 1,)),
            pltpu.SemaphoreType.DMA((n * nd,)),
        ],
        compiler_params=params(),
        cost_estimate=cost(3 * n * total * d * width, 20e6),
        name="experts_weights",
    )(scalars, rows_t, gb, ga_t, *cots)
    return [outs[e * nd : (e + 1) * nd] for e in range(n)]


def finish(scalars, dqkv, w, toks, gain, gain_grad, here, nd, ne):
    blocks = len(toks)
    rows, d = toks[0].shape
    width = dqkv.shape[1]

    w_rows = d // (nd * blocks * ne)

    def body(s_ref, here_ref, dq_ref, w_ref, gain_ref, gg_ref, *refs):
        ins, (gn_ref, gw_ref, acc) = refs[:blocks], refs[blocks:]
        gg = jnp.zeros((1, d), F32)
        for k in range(blocks):
            to = s_ref[k]
            at = pl.ds(pl.multiple_of(to * rows, rows), rows)
            dqkv_block = dq_ref[at, :]
            t = ins[k][...].astype(F32)
            normal = t * rms(t)
            normed = (normal * gain_ref[...]).astype(BF)
            gn = mm(dqkv_block, w_ref[...], NT)
            gg = gg + jnp.sum(gn * normal, axis=0, keepdims=True)
            gn_ref[to] = gn.astype(BF)
            part = mm(normed, dqkv_block, TN)
            acc[...] = part if k == 0 else acc[...] + part
        row = lax.broadcasted_iota(jnp.int32, (128, d), 0)
        both = jnp.where(row == 0, gg, jnp.where(row == 1, gg_ref[...], 0.0)).T
        for q in range(d // w_rows):
            e = swapped(jnp.bitwise_xor(q % ne, here_ref[3]))
            m = lax.rem(q // ne // blocks - here_ref[0] + nd, nd)
            at = slice(q * w_rows, (q + 1) * w_rows)
            gw_ref[e, m, q // ne % blocks, :, :width] = acc[at, :].astype(BF)
            gw_ref[e, m, q // ne % blocks, :, width:] = both[at, :].astype(BF)

    return pl.pallas_call(
        body,
        out_shape=(
            jax.ShapeDtypeStruct((blocks, rows, d), BF),
            jax.ShapeDtypeStruct((ne, nd, blocks, w_rows, width + 128), BF),
        ),
        in_specs=[SM, SM] + [VM] * (4 + blocks),
        out_specs=(VM, VM),
        scratch_shapes=[pltpu.VMEM((d, width), F32)],
        compiler_params=params(),
        cost_estimate=cost(4 * blocks * rows * d * width, 8 * blocks * rows * d),
        name="finish",
    )(scalars, here, dqkv, w, gain, gain_grad, *toks)


def per_device(
    tokens,
    gain_attn,
    w_query,
    w_key,
    w_value,
    w_out,
    gain_moe,
    w_in,
    w_down,
    routes,
    gates,
    lengths,
    cotangent,
):
    nd, nz, ne = lax.axis_size("dp"), lax.axis_size("ctx"), lax.axis_size("exp")
    x, z, j = lax.axis_index("dp"), lax.axis_index("ctx"), lax.axis_index("exp")
    rows, d = tokens.shape[1:]
    span = rows * nz
    w_rows = w_query.shape[0]
    heads, kvs = HEADS // nz, KV_HEADS // nz
    qw, kw = heads * HEAD_DIM, kvs * HEAD_DIM
    local_experts = w_in.shape[0]
    experts = local_experts * ne
    i32 = jnp.int32
    mod = lambda v, n: lax.rem(v + 8 * n, n)

    ends = jnp.cumsum(lengths[0]).astype(i32)
    places = [mod(z - k, nz) for k in range(nz)]
    scalars = jnp.concatenate([jnp.stack(places + [z]).astype(i32), ends])
    place = jnp.arange(span, dtype=i32)
    place = place - jnp.max(jnp.where(place[:, None] >= ends[None, :-1], ends[None, :-1], 0), axis=1)
    lane = jnp.arange(128, dtype=i32)
    half = HEAD_DIM // 2
    frequency = rope_base ** (-2.0 * jnp.arange(half, dtype=F32) / HEAD_DIM)
    angles = place.astype(F32)[:, None] * frequency[None, :]
    cos = jnp.tile(jnp.cos(angles), (1, 128 // half))
    sin = jnp.tile(jnp.sin(angles), (1, 128 // half)) * jnp.where((lane & 63) < 32, -1.0, 1.0)[None, :]

    run = Stages(gain_attn)
    gain_a, gain_m = gain_attn[None, :], gain_moe[None, :]
    devices = nd * nz
    odd, zh = jnp.bitwise_and(z, 1), z // 2
    batch = local_experts // 2
    tok, cot = tokens[0], cotangent[0]
    cot_b = (residual_scale * cot).astype(BF)
    flip_e = lambda v, e: flip(v, "exp", e)

    def row_blocks(found, owners):
        at = [
            (mod(x - m, nd) * nz + p) * ne + jnp.bitwise_xor(j, e + 2 * b)
            for e in (0, 1) for m in range(nd) for b in (0, 1) for p in owners
        ]
        return assemble(found, jnp.stack(at).astype(i32))

    here = jnp.stack([x, odd, zh, j]).astype(i32)

    parts = [
        jnp.concatenate(
            [
                w_query[:, p * qw : (p + 1) * qw],
                w_key[:, p * kw : (p + 1) * kw],
                w_value[:, p * kw : (p + 1) * kw],
            ],
            axis=1,
        )
        for p in range(nz)
    ]
    w_parts = jnp.stack(parts)
    toks = [tok, shift(tok, "ctx", 1)]
    w_mine = [pick(w_parts, z)] + [shift(pick(w_parts, mod(z + k, nz)), "ctx", k) for k in range(1, nz)]
    hits = routes[0][:, :, None] == jnp.arange(128, dtype=i32)[None, None, :]
    dense = jnp.sum(jnp.where(hits, gates[0].astype(F32)[:, :, None], 0.0), axis=1).astype(BF)
    cot_b = jnp.concatenate([cot_b, dense], axis=1)
    mine_in, their_in = halves(w_in, odd, devices)
    down = jnp.concatenate([w_down[:, :, b * FF : (b + 1) * FF] for b in range(d // FF)], axis=1)
    run.end(toks, w_mine)

    cut = rows // 2
    half_2 = [shift(run.hold(toks[1][:cut]), "ctx", 1)]
    w_mine = jnp.stack(w_mine)
    w_mine = jnp.stack([w_mine, flip_e(run.hold(w_mine), 2)])
    line = [hop(run.hold(w_out), pairs) for pairs in (ACROSS, UP, DOWN)]
    run.end(half_2, w_mine, line, mine_in)

    half_2.append(shift(run.hold(toks[1][cut:]), "ctx", 1))
    w_found = ring(run.hold(w_mine), "dp")
    line_end = hop(run.hold(line[0]), OUTER)
    run.end(half_2, w_found, line_end)

    toks.append(jnp.concatenate(half_2))
    toks.append(shift(run.hold(toks[2]), "ctx", 1))
    got_1 = flip(run.hold(their_in[:batch]), "ctx", 1)
    w_found = w_found + [flip_e(t, 1) for t in run.hold(w_found)]
    w_line = ring(run.hold(jnp.stack(line_gather(*line, line_end, w_out))), "dp")
    cot_2 = flip_e(run.hold(cot_b), 2)
    w_qkv = row_blocks(w_found, places)
    at = [p[None].astype(i32) for p in places]
    pieces = [project(toks[k], gain_a, w_qkv, cos, sin, at[k]) for k in range(nz - 1)]
    run.end(toks, pieces, got_1, w_line, cot_2)

    near_1 = jnp.stack([mine_in[:batch], got_1, down[:batch]], axis=1)
    far = [flip(run.hold(near_1[:1]), "ctx", 2)]
    own_1 = ring(run.hold(near_1), "dp")
    w_line = jnp.stack(w_line)
    w_line = jnp.stack([w_line, flip_e(run.hold(w_line), 2)], axis=1)
    cot_n = flip(run.hold(cot_b), "ctx", 1)
    pieces.append(project(run.hold(toks[3]), gain_a, w_qkv, cos, sin, at[3]))
    mix_out, lse = attend(scalars, pieces, heads, kvs)
    run.end(far, own_1, w_line, cot_n, mix_out)

    mixes = run.hold([mix_out[k] for k in range(nz)])
    mixes = [mixes[0]] + [shift(mixes[k], "ctx", k) for k in range(1, nz)]
    w_line = [w_line, flip_e(run.hold(w_line), 1)]
    cot_n2 = flip_e(run.hold(cot_n), 2)
    w_out_all = row_blocks(w_line, line_places(z))
    run.end(mixes, w_out_all, cot_n2)

    cot_1, cot_3 = flip_e(run.hold(cot_b), 1), flip_e(run.hold(cot_2), 1)
    got_2 = flip(run.hold(their_in[batch:]), "ctx", 1)
    middle, hidden = join(scalars, run.hold(mixes), w_out_all, tok, gain_m)
    run.end(hidden, got_2, cot_1, cot_3)

    hidden_2, hidden_n = flip_e(run.hold(hidden), 2), flip(run.hold(hidden), "ctx", 1)
    near_2 = jnp.stack([mine_in[batch:], got_2, down[batch:]], axis=1)
    far.append(flip(run.hold(near_1[1:]), "ctx", 2))
    own_2 = ring(run.hold(near_2), "dp")
    hidden_1 = flip_e(run.hold(hidden), 1)
    run.end(hidden_1, hidden_2, hidden_n, far, own_2)

    hidden_n2 = flip_e(run.hold(hidden_n), 2)
    hidden_n1, hidden_3 = flip_e(run.hold(hidden_n), 1), flip_e(run.hold(hidden_2), 1)
    over_1 = ring(run.hold(jnp.concatenate(far)), "dp")
    far_2 = [flip(run.hold(near_2[:1]), "ctx", 2)]
    run.end(hidden_n2, hidden_n1, hidden_3, over_1, far_2)

    hidden_n3 = flip_e(run.hold(hidden_n2), 1)
    cot_n1, cot_n3 = flip_e(run.hold(cot_n), 1), flip_e(run.hold(cot_n2), 1)
    rows_in = [hidden, hidden_n, hidden_2, hidden_n2, hidden_1, hidden_n1, hidden_3, hidden_n3]
    cots = [cot_b, cot_n, cot_2, cot_n2, cot_1, cot_n1, cot_3, cot_n3]
    w_at = []
    for zc in (z, jnp.bitwise_xor(z, 2)):
        for m in range(nd):
            xc = mod(x - m, nd)
            w_at += [xc * nz + zc, xc * nz + jnp.bitwise_xor(zc, 1), xc * 2 + zc // 2]
    w_at = jnp.stack(w_at + [j * local_experts]).astype(i32)
    far_2.append(flip(run.hold(near_2[1:]), "ctx", 2))
    over_2 = [ring(run.hold(far_2[0]), "dp")]
    sum_h, sum_o, gb, ga_t, rows_t = experts_rows(
        w_at, 0, run.hold(rows_in), cots, own_1 + over_1, None, False
    )
    run.end(far_2, over_2, sum_h)

    over_2.append(ring(run.hold(far_2[1]), "dp"))
    gw_1 = experts_weights(here, rows_t, cots, run.hold(gb), ga_t, batch, devices)
    run.end(over_2, gw_1)

    x_0 = dp_reduce(run.hold(gw_1[0]))
    over_2 = [jnp.concatenate(t) for t in zip(*over_2)]
    sum_h, rest_h, sum_o, rest_o, gb, ga_t = experts_rows(
        w_at, batch, run.hold(rows_in), cots, own_2 + over_2, (sum_h, sum_o), True
    )
    run.end(x_0, sum_h)

    def swap(own, other):
        return flip((own[0, 1].astype(F32) + other[1].astype(F32)).astype(BF), "ctx", 1)

    rest_h = flip_e(run.hold(rest_h), 1)
    run.end(rest_h)

    part = rows // 2
    sum_h = [
        (sum_h[a * part : b * part].astype(F32) + rest_h[a * part : b * part].astype(F32)).astype(BF)
        for a, b in ((0, 2), (2, 3), (3, 4), (4, 5), (5, 6), (6, 7), (7, 8))
    ]
    by_y, by_z = flip_e(run.hold(sum_h[5]), 2), flip(run.hold(sum_h[6]), "ctx", 1)
    z_0 = flip(run.hold(x_0)[1], "ctx", 2)
    x_1 = dp_reduce(run.hold(gw_1[1]))
    gw_2 = experts_weights(here, rows_t, cots, run.hold(gb), ga_t, batch, devices)
    run.end(by_y, by_z, z_0, x_1, gw_2)

    add = lambda a, b: (a.astype(F32) + b.astype(F32)).astype(BF)
    near_h = flip_e(run.hold(jnp.concatenate([sum_h[3], add(sum_h[4], by_z)])), 2)
    other_h = flip(run.hold(jnp.concatenate([add(sum_h[1], by_y), sum_h[2]])), "ctx", 1)
    z_1 = flip(run.hold(x_1)[1], "ctx", 2)
    x_2 = dp_reduce(run.hold(gw_2[0]))
    rest_o = flip_e(run.hold(rest_o), 1)
    run.end(near_h, other_h, z_1, x_2, rest_o)

    def fold(g):
        return g[0].astype(F32), (g[1].astype(F32) + g[3].astype(F32)).astype(BF)

    swap_0 = swap(*run.hold([x_0, z_0]))
    grad_middle, grad_mix, grad_w_out, grad_gain_m = join_back(
        scalars, [sum_h[0], *run.hold([near_h, other_h])], middle, cot, gain_m, w_out_all, mixes, here, nd, ne
    )
    grad_mixes = [grad_mix[0]] + [shift(grad_mix[k], "ctx", -k) for k in range(1, nz)]
    wo_core = flip_e(grad_w_out[2:], 1)
    run.end(grad_mixes, wo_core, swap_0)

    x_3 = dp_reduce(run.hold(gw_2[1]))
    z_2 = flip(run.hold(x_2)[1], "ctx", 2)
    swap_1 = swap(*run.hold([x_1, z_1]))
    wo_core = run.hold(wo_core)
    wo = add(grad_w_out[0], wo_core[0])
    wo_far = flip_e(add(grad_w_out[1], wo_core[1]), 2)
    dqkv = attend_back(scalars, pieces, run.hold(grad_mixes), lse, cos, sin, heads, kvs)
    sum_o = add(sum_o, run.hold(rest_o))
    run.end(x_3, z_2, swap_1, wo_far, dqkv, sum_o)

    wo = dp_reduce(list(run.hold(add(wo, wo_far))))
    grad_normed, grad_w = finish(
        scalars, run.hold(dqkv), w_qkv, toks, gain_a, grad_gain_m, here, nd, ne
    )
    run.end(grad_normed, grad_w, wo)

    tail = run.hold(grad_normed)
    feed = hop(pick(tail, 3 - z), INNER)
    z_3 = flip(run.hold(x_3)[1], "ctx", 2)
    far_o = flip_e(run.hold(sum_o[2 * rows :]), 2)
    gw_core = flip_e(run.hold(grad_w[2:]), 1)
    run.end(feed, z_3, far_o, gw_core)

    across = hop(run.hold(add(pick(tail, jnp.bitwise_xor(z, 2)), feed)), ACROSS)
    below = hop(run.hold(pick(tail, jnp.minimum(z + 1, 3))), UP)
    above = hop(run.hold(pick(tail, jnp.maximum(z - 1, 0))), DOWN)
    mine = add(grad_w[0], gw_core[0])
    mine = add(mine, flip_e(run.hold(add(grad_w[1], gw_core[1])), 2))
    mine = dp_reduce(list(mine))
    other_o = flip(run.hold(add(sum_o[rows : 2 * rows], far_o[rows:])), "ctx", 1)
    run.end(across, below, above, mine, other_o)

    swap_2, swap_3 = swap(*run.hold([x_2, z_2])), swap(*run.hold([x_3, z_3]))
    mine, wo = run.hold(mine), run.hold(wo)
    parts = [pick(mine, z)] + [shift(pick(mine, mod(z + k, nz)), "ctx", k) for k in range(1, nz)]
    outs = [pick(wo, z)] + [shift(pick(wo, mod(z + k, nz)), "ctx", k) for k in range(1, nz)]
    grad_out = sum(t.astype(F32) for t in outs)

    gn = pick(tail, z).astype(F32) + below.astype(F32) + above.astype(F32) + across.astype(F32)
    expert_sum = sum_o[:rows].astype(F32) + far_o[:rows].astype(F32) + other_o.astype(F32)
    mixed_out = (middle + residual_scale * expert_sum).astype(BF)
    gains = sum(p[:, qw + 2 * kw : qw + 2 * kw + 2].astype(F32) for p in parts)
    order = jnp.stack(parts)
    order = [pick(order, mod(z - p, nz)).astype(F32) for p in range(nz)]
    grad_query = jnp.concatenate([g[:, :qw] for g in order], axis=1)
    grad_key = jnp.concatenate([g[:, qw : qw + kw] for g in order], axis=1)
    grad_value = jnp.concatenate([g[:, qw + kw : qw + 2 * kw] for g in order], axis=1)

    grads = [
        whole(own[0], other, theirs, odd, devices)
        for own, other, theirs in (
            (x_0, z_0, swap_0), (x_1, z_1, swap_1), (x_2, z_2, swap_2), (x_3, z_3, swap_3)
        )
    ]
    grads_in = jnp.stack([g[0] for g in grads])
    grads_down = jnp.stack([g[1] for g in grads])

    t = tok.astype(F32)
    inv = rms(t)
    normal = t * inv
    u = gn * gain_a
    grad_tokens = grad_middle + inv * (u - normal * jnp.mean(u * normal, axis=-1, keepdims=True))
    return (
        mixed_out[None],
        grad_tokens[None],
        gains[:, 0],
        grad_query,
        grad_key,
        grad_value,
        grad_out.astype(F32),
        gains[:, 1],
        grads_in,
        grads_down,
    )


def solution(mesh):
    every = ("dp", "ctx", "exp")
    return jax.shard_map(
        per_device,
        mesh=mesh,
        in_specs=(
            P(("dp", "exp"), "ctx", None),
            P(),
            P(every, None),
            P(every, None),
            P(every, None),
            P(every, None),
            P(),
            P("exp", ("dp", "ctx"), None),
            P("exp", ("dp", "ctx"), None),
            P(("dp", "exp"), "ctx", None),
            P(("dp", "exp"), "ctx", None),
            P(("dp", "exp"), None),
            P(("dp", "exp"), "ctx", None),
        ),
        out_specs=(
            P(("dp", "exp"), "ctx", None),
            P(("dp", "exp"), "ctx", None),
            P(every),
            P(every, None),
            P(every, None),
            P(every, None),
            P(every, None),
            P(every),
            P("exp", ("dp", "ctx"), None),
            P("exp", ("dp", "ctx"), None),
        ),
        check_vma=False,
    )
```

time: 1950 us -> 658 us (0.34)
  waiting for transfers between devices: 1300 us -> 231 us
  matrix products: 274 us -> 0 us
  Pallas kernels: 0 us -> 206 us
  local copies, waits for them, and re-layouts: 205 us -> 57.2 us
  starting transfers between devices: 24.6 us -> 92.5 us
  blocking collectives: 41.4 us -> 0 us
    reduce_scatter x8 -> x0, waiting for transfers between devices: 771 us -> none  [the longest x1 208 us: per_device(): lax.psum_scatter(grad_in_part.astype(jnp.bfloat16), ('dp', 'ctx'), scatte...]
    all_gather x8 -> x0, waiting for transfers between devices: 302 us -> none  [the longest x1 81.2 us: per_device(): lax.all_gather(w_down, ('dp', 'ctx'), axis=1, tiled=True)]
    dot_general x74 -> x0, matrix products: 274 us -> none  [the longest x8 35.5 us: head_backward(): jnp.einsum('gst,td->sgd', grad_scores, key_head, preferred_element_type=j...]
    ppermute x0 -> x85, waiting for transfers between devices: none -> 231 us  [the longest x45 109 us: flip(): return lax.ppermute(x, axis, [(i, i ^ mask) for i in range(n)])]
    all_to_all x4 -> x0, waiting for transfers between devices: 222 us -> none  [the longest x1 96.3 us: per_device(): lax.all_to_all(outgoing, 'exp', split_axis=0, concat_axis=1, tiled=True)]
    pallas_call x0 -> x20, Pallas kernels: none -> 206 us  [the longest x2 65.1 us: experts_rows(): pl.pallas_call(body, grid=(tiles,), out_shape=sum_shapes + (jax.ShapeDtyp...]
    ppermute x0 -> x85, starting transfers between devices: none -> 92.5 us  [the longest x32 43.6 us: shift(): return lax.ppermute(x, axis, [(i, (i + by) % n) for i in range(n)])]
    gather x4 -> x0, local copies, waits for them, and re-layouts: 69.7 us -> none  [the longest x1 20.7 us: per_device(): grad_returned[target].reshape(row_count, TOP, model_width)]
  transfers between devices with their start and end apart: 20 -> 85, of which waited for: 17 -> 32; matrix products, arithmetic and copies ran while one was open for 17% -> 15% of each run, Pallas kernels for 0% -> 29%
where the time goes in v1:
time: 658 us; the launch traced here: 653 us
  waiting for transfers between devices  231 us (35%)
  Pallas kernels  206 us (31%)
  starting transfers between devices  92.5 us (14%)
  other arithmetic  64.6 us (10%)
  local copies, waits for them, and re-layouts  57.2 us (9%)
    ppermute x45, waiting for transfers between devices, flip(): return lax.ppermute(x, axis, [(i, i ^ mask) for i in range(n)])  109 us
    pallas_call x2, Pallas kernels, experts_rows(): pl.pallas_call(body, grid=(tiles,), out_shape=sum_shapes + (jax.ShapeDtyp...  65.1 us
    ppermute x32, waiting for transfers between devices, shift(): return lax.ppermute(x, axis, [(i, (i + by) % n) for i in range(n)])  64.5 us
    ppermute x8, waiting for transfers between devices, hop(): return lax.ppermute(x, 'ctx', pairs)  57.7 us
    ppermute x32, starting transfers between devices, shift(): return lax.ppermute(x, axis, [(i, (i + by) % n) for i in range(n)])  43.6 us
    pallas_call x2, Pallas kernels, experts_weights(): pl.pallas_call(body, out_shape=[jax.ShapeDtypeStruct((2, 3, r, width), BF...  36.4 us
    ppermute x45, starting transfers between devices, flip(): return lax.ppermute(x, axis, [(i, i ^ mask) for i in range(n)])  27 us
    pallas_call x1, Pallas kernels, attend_back(): pl.pallas_call(body, out_shape=jax.ShapeDtypeStruct((span, width), BF), i...  22.7 us
  transfers between devices with their start and end apart: 85, of which 32 were waited for; matrix products, arithmetic and copies ran while one was open for 15% of the time, Pallas kernels for 29%

profile of v1, /device:TPU:0, one launch (start us, length us, event | category | flops | bytes accessed | tf_op | source)
XLA Modules:
  0.0 653.1 jit_solution(828706828222482937)
XLA Ops:
  19.6 11.7 %collective-permute-done.3.tok_ref.refs_1_ = bf16[256,1536]{1,0:T(8,128)(2,1)S(1)} collective-permute-done((bf16[256,1536]{1,0:T(8,128)(2,1)S(1)}, bf16[256,1536]{1,0:T(8,128)(2,1)S(1)}, u32[]{:S(2)}, u32[]{:S(2)}) %collective-permute-start.3) | collective-permute-done | bytes 786464 | tf_op jit(solution)/shard_map/ppermute | solution.py:49
  56.1 10.8 %collective-permute-done.11 = bf16[48,1536]{1,0:T(8,128)(2,1)S(1)} collective-permute-done((bf16[48,1536]{1,0:T(8,128)(2,1)S(1)}, bf16[48,1536]{1,0:T(8,128)(2,1)S(1)}, u32[]{:S(2)}, u32[]{:S(2)}) %collective-permute-start.11) | collective-permute-done | bytes 147488 | tf_op jit(solution)/shard_map/ppermute | solution.py:78
  110.5 14.6 %attend.1 = (bf16[4,256,384]{2,1,0:T(8,128)(2,1)}, f32[8,1024]{1,0:T(8,128)}) custom-call(s32[8]{0:T(128)} %concatenate.48.s_ref, bf16[256,640]{1,0:T(8,128)(2,1)} %project.4.refs_0_, bf16[256,640]{1,0:T(8,128)(2,1)} %project.5.refs_1_, bf16[256,640]{1,0:T(8,128)(2,1)} %project.6.refs_2_, bf16[256,640]{1,0:T(8,128)(2,1)} %project.7.refs_3_), custom_call_target="tpu_custom_call" | custom-call | flops 1342177280 | bytes 873813 | tf_op jit(solution)/shard_map/attend/pallas_call | solution.py:269
  149.9 5.7 assemble.3.refs_4_.w_ref
  160.6 6.2 join.1
  175.2 28.7 %collective-permute-done.33 = bf16[1,3,192,512]{3,2,0,1:T(8,128)(2,1)S(1)} collective-permute-done((bf16[1,3,192,512]{3,2,0,1:T(8,128)(2,1)S(1)}, bf16[1,3,192,512]{3,2,0,1:T(8,128)(2,1)S(1)}, u32[]{:S(2)}, u32[]{:S(2)}) %collective-permute-start.33) | collective-permute-done | bytes 589856 | tf_op jit(solution)/shard_map/ppermute | solution.py:54
  210.8 27.4 %collective-permute-done.39 = bf16[1,3,192,512]{3,2,1,0:T(8,128)(2,1)S(1)} collective-permute-done((bf16[1,3,192,512]{3,2,1,0:T(8,128)(2,1)S(1)}, bf16[1,3,192,512]{3,2,1,0:T(8,128)(2,1)S(1)}, u32[]{:S(2)}, u32[]{:S(2)}) %collective-permute-start.39) | collective-permute-done | bytes 589856 | tf_op jit(solution)/shard_map/ppermute | solution.py:54
  248.6 30.0 %experts_rows.2 = (f32[2048,1536]{1,0:T(8,128)}, f32[2048,1536]{1,0:T(8,128)}, bf16[2048,1024]{1,0:T(8,128)(2,1)}, bf16[512,2048]{1,0:T(8,128)(2,1)}, bf16[1536,2048]{1,0:T(8,128)(2,1)}) custom-call(s32[13]{0:T(128)} %stack.516.places_ref, bf16[256,1536]{1,0:T(8,128)(2,1)} %get-tuple-element.250.refs_0_, bf16[256,1536]{1,0:T(8,128)(2,1)} %copy-done.52, ...), custom_call_target="tpu_custom_call" | custom-call | flops 6442450944 | bytes 16666666 | tf_op jit(solution)/shard_map/experts_rows/pallas_call | solution.py:639
  279.9 18.1 %experts_weights.2 = (bf16[2,3,192,512]{3,2,1,0:T(8,128)(2,1)}, bf16[2,3,192,512]{3,2,1,0:T(8,128)(2,1)}, bf16[2,3,192,512]{3,2,1,0:T(8,128)(2,1)}, bf16[2,3,192,512]{3,2,1,0:T(8,128)(2,1)}) custom-call(s32[4]{0:T(128)} %pad_add_fusion.s_ref.here_ref, bf16[1536,2048]{1,0:T(8,128)(2,1)} %get-tuple-element.241.h_any, ...), custom_call_target="tpu_custom_call" | custom-call | flops 3221225472 | bytes 6666666 | tf_op jit(solution)/shard_map/experts_weights/pallas_call | solution.py:721
  301.9 35.2 %experts_rows.3 = (bf16[1024,1536]{1,0:T(8,128)(2,1)}, bf16[1024,1536]{1,0:T(8,128)(2,1)}, bf16[1024,1536]{1,0:T(8,128)(2,1)}, bf16[1024,1536]{1,0:T(8,128)(2,1)...) custom-call(s32[13]{0:T(128)} %stack.516.places_ref, bf16[256,1536]{1,0:T(8,128)(2,1)} %get-tuple-element.250.refs_0_, ...), custom_call_target="tpu_custom_call" | custom-call | flops 6442450944 | bytes 16666666 | tf_op jit(solution)/shard_map/experts_rows/pallas_call | solution.py:639
  339.3 5.7 collective-permute-done.47
  352.2 18.2 %experts_weights.3 = (bf16[2,3,192,512]{3,2,1,0:T(8,128)(2,1)}, bf16[2,3,192,512]{3,2,1,0:T(8,128)(2,1)}, bf16[2,3,192,512]{3,2,1,0:T(8,128)(2,1)}, bf16[2,3,192,512]{3,2,1,0:T(8,128)(2,1)}) custom-call(s32[4]{0:T(128)} %pad_add_fusion.s_ref.here_ref, bf16[1536,2048]{1,0:T(8,128)(2,1)} %get-tuple-element.241.h_any, ...), custom_call_target="tpu_custom_call" | custom-call | flops 3221225472 | bytes 6666666 | tf_op jit(solution)/shard_map/experts_weights/pallas_call | solution.py:721
  384.3 22.1 %collective-permute-done.56 = bf16[2,3,192,512]{3,2,1,0:T(8,128)(2,1)S(1)} collective-permute-done((bf16[2,3,192,512]{3,2,1,0:T(8,128)(2,1)S(1)}, bf16[2,3,192,512]{3,2,1,0:T(8,128)(2,1)S(1)}, u32[]{:S(2)}, u32[]{:S(2)}) %collective-permute-start.56) | collective-permute-done | bytes 1179680 | tf_op jit(solution)/shard_map/ppermute | solution.py:49
  407.1 4.8 collective-permute-done.54.c_ref
  412.8 11.6 %join_back.1 = (f32[256,1536]{1,0:T(8,128)}, bf16[4,256,384]{2,1,0:T(8,128)(2,1)}, bf16[4,2,4,48,1536]{4,3,2,1,0:T(8,128)(2,1)}, f32[1,1536]{1,0:T(1,128)}) custom-call(s32[8]{0:T(128)} %concatenate.48.s_ref, s32[4]{0:T(128)} %pad_add_fusion.s_ref.here_ref, bf16[256,1536]{1,0:T(8,128)(2,1)} %add_convert_fusion.9.a_ref, ...), custom_call_target="tpu_custom_call" | custom-call | flops 805306368 | bytes 5505024 | tf_op jit(solution)/shard_map/join_back/pallas_call | solution.py:431
  436.6 6.3 collective-permute-done.57.refs_5_
  442.9 7.9 %collective-permute-done.58.refs_6_ = bf16[256,384]{1,0:T(8,128)(2,1)S(1)} collective-permute-done((bf16[256,384]{1,0:T(8,128)(2,1)S(1)}, bf16[256,384]{1,0:T(8,128)(2,1)S(1)}, u32[]{:S(2)}, u32[]{:S(2)}) %collective-permute-start.58) | collective-permute-done | bytes 196640 | tf_op jit(solution)/shard_map/ppermute | solution.py:49
  463.3 22.7 %attend_back.1.dq_ref = bf16[1024,640]{1,0:T(8,128)(2,1)} custom-call(s32[8]{0:T(128)} %concatenate.48.s_ref, bf16[256,640]{1,0:T(8,128)(2,1)} %project.4.refs_0_, bf16[256,640]{1,0:T(8,128)(2,1)} %project.5.refs_1_, bf16[256,640]{1,0:T(8,128)(2,1)} %project.6.refs_2_, bf16[256,640]{1,0:T(8,128)(2,1)} %project.7.refs_3_, ...), custom_call_target="tpu_custom_call" | custom-call | flops 3355443200 | bytes 1747626 | tf_op jit(solution)/shard_map/attend_back/pallas_call | solution.py:352
  495.9 10.7 %finish.1 = (bf16[4,256,1536]{2,1,0:T(8,128)(2,1)}, bf16[4,2,4,48,768]{4,3,2,1,0:T(8,128)(2,1)}) custom-call(s32[8]{0:T(128)} %concatenate.48.s_ref, s32[4]{0:T(128)} %pad_add_fusion.s_ref.here_ref, bf16[1024,640]{1,0:T(8,128)(2,1)} %attend_back.1.dq_ref, bf16[1536,640]{1,0:T(8,128)(2,1)} %assemble.2.w_ref, f32[1,1536]{1,0:T(1,128)} %broadcast_in_dim.40.gain_ref, ...), custom_call_target="tpu_custom_call" | custom-call | flops 1342177280 | bytes 4194304 | tf_op jit(solution)/shard_map/finish/pallas_call | solution.py:775
  514.1 5.1 collective-permute-start.68
  529.5 18.7 %collective-permute-done.69.other_ref = bf16[3,192,512]{2,1,0:T(8,128)(2,1)} collective-permute-done((bf16[3,192,512]{2,1,0:T(8,128)(2,1)}, bf16[3,192,512]{2,1,0:T(8,128)(2,1)}, u32[]{:S(2)}, u32[]{:S(2)}) %collective-permute-start.69) | collective-permute-done | bytes 589856 | tf_op jit(solution)/shard_map/ppermute | solution.py:54
  565.4 6.9 %collective-permute-done.72 = bf16[256,1536]{1,0:T(8,128)(2,1)S(1)} collective-permute-done((bf16[256,1536]{1,0:T(8,128)(2,1)S(1)}, bf16[256,1536]{1,0:T(8,128)(2,1)S(1)}, u32[]{:S(2)}, u32[]{:S(2)}) %collective-permute-start.72) | collective-permute-done | bytes 786464 | tf_op jit(solution)/shard_map/ppermute | solution.py:78
  572.4 5.5 collective-permute-done.73
  577.9 31.9 %collective-permute-done.74 = bf16[256,1536]{1,0:T(8,128)(2,1)S(1)} collective-permute-done((bf16[256,1536]{1,0:T(8,128)(2,1)S(1)}, bf16[256,1536]{1,0:T(8,128)(2,1)S(1)}, u32[]{:S(2)}, u32[]{:S(2)}) %collective-permute-start.74) | collective-permute-done | bytes 786464 | tf_op jit(solution)/shard_map/ppermute | solution.py:78
  (452 shorter events, 284.6 us)
Async XLA Ops:
  103.8 33.6 %collective-permute-start.19 = (bf16[2,3,192,512]{3,2,0,1:T(8,128)(2,1)S(1)}, bf16[2,3,192,512]{3,2,0,1:T(8,128)(2,1)}, u32[]{:S(2)}, u32[]{:S(2)}) collective-permute-start(bf16[2,3,192,512]{3,2,0,1:T(8,128)(2,1)S(1)} %pad_maximum_fusion.3), channel_id=1, source_target_pairs={{0,16},{16,0},{1,17},{17,1},{2,18},{18,2},{3,19},{19,3},{4,20},{20... | collective-permute-start | bytes 3538952 | tf_op jit(solution)/shard_map/ppermute | solution.py:49
  104.4 32.9 %collective-permute-start.21 = (bf16[256,1664]{1,0:T(8,128)(2,1)S(1)}, bf16[256,1664]{1,0:T(8,128)(2,1)S(1)}, u32[]{:S(2)}, u32[]{:S(2)}) collective-permute-start(bf16[256,1664]{1,0:T(8,128)(2,1)S(1)} %pad_maximum_fusion.9.refs_8_.refs_0_), channel_id=1, source_target_pairs={{0,4},{4,0},{8,12},{12,8},{1,5},{5,1},{9,13},{13,9},{2,6},{6,2},{1... | collective-permute-start | bytes 2555912 | tf_op jit(solution)/shard_map/ppermute | solution.py:54
  171.4 34.4 %collective-permute-start.34 = (bf16[2,3,192,512]{3,2,1,0:T(8,128)(2,1)S(1)}, bf16[2,3,192,512]{3,2,1,0:T(8,128)(2,1)S(1)}, u32[]{:S(2)}, u32[]{:S(2)}) collective-permute-start(bf16[2,3,192,512]{3,2,1,0:T(8,128)(2,1)S(1)} %pad_maximum_fusion.5.refs_16_), channel_id=1, source_target_pairs={{0,16},{16,0},{1,17},{17,1},{2,18},{18,2},{3,19},{19,3},{4,20},{20... | collective-permute-start | bytes 3538952 | tf_op jit(solution)/shard_map/ppermute | solution.py:49
  173.0 31.1 %collective-permute-start.30 = (bf16[256,1536]{1,0:T(8,128)(2,1)S(1)}, bf16[256,1536]{1,0:T(8,128)(2,1)S(1)}, u32[]{:S(2)}, u32[]{:S(2)}) collective-permute-start(bf16[256,1536]{1,0:T(8,128)(2,1)S(1)} %copy-done.49), channel_id=1, source_target_pairs={{0,1},{1,0},{2,3},{3,2},{4,5},{5,4},{6,7},{7,6},{8,9},{9,8},{10,11... | collective-permute-start | bytes 2359304 | tf_op jit(solution)/shard_map/ppermute | solution.py:54
  173.0 31.1 %collective-permute-start.31 = (bf16[256,1536]{1,0:T(8,128)(2,1)S(1)}, bf16[256,1536]{1,0:T(8,128)(2,1)S(1)}, u32[]{:S(2)}, u32[]{:S(2)}) collective-permute-start(bf16[256,1536]{1,0:T(8,128)(2,1)S(1)} %copy-done.49), channel_id=1, source_target_pairs={{0,2},{1,3},{2,0},{3,1},{4,6},{5,7},{6,4},{7,5},{8,10},{9,11},{10,... | collective-permute-start | bytes 2359304 | tf_op jit(solution)/shard_map/ppermute | solution.py:54
  173.5 32.3 %collective-permute-start.32 = (bf16[256,1536]{1,0:T(8,128)(2,1)S(1)}, bf16[256,1536]{1,0:T(8,128)(2,1)S(1)}, u32[]{:S(2)}, u32[]{:S(2)}) collective-permute-start(bf16[256,1536]{1,0:T(8,128)(2,1)S(1)} %copy-done.49), channel_id=1, source_target_pairs={{0,4},{4,0},{8,12},{12,8},{1,5},{5,1},{9,13},{13,9},{2,6},{6,2},{1... | collective-permute-start | bytes 2359304 | tf_op jit(solution)/shard_map/ppermute | solution.py:54
  205.8 32.3 %collective-permute-start.38 = (bf16[2,3,192,512]{3,2,0,1:T(8,128)(2,1)S(1)}, bf16[2,3,192,512]{3,2,0,1:T(8,128)(2,1)S(1)}, u32[]{:S(2)}, u32[]{:S(2)}) collective-permute-start(bf16[2,3,192,512]{3,2,0,1:T(8,128)(2,1)S(1)} %pad_maximum_fusion.6), channel_id=1, source_target_pairs={{0,16},{16,0},{1,17},{17,1},{2,18},{18,2},{3,19},{19,3},{4,20},{20... | collective-permute-start | bytes 3538952 | tf_op jit(solution)/shard_map/ppermute | solution.py:49
  206.4 31.7 %collective-permute-start.35 = (bf16[256,1536]{1,0:T(8,128)(2,1)S(1)}, bf16[256,1536]{1,0:T(8,128)(2,1)}, u32[]{:S(2)}, u32[]{:S(2)}) collective-permute-start(bf16[256,1536]{1,0:T(8,128)(2,1)S(1)} %collective-permute-done.32.refs_1_), channel_id=1, source_target_pairs={{0,2},{1,3},{2,0},{3,1},{4,6},{5,7},{6,4},{7,5},{8,10},{9,11},{10,... | collective-permute-start | bytes 2359304 | tf_op jit(solution)/shard_map/ppermute | solution.py:54
  207.9 30.2 %collective-permute-start.36 = (bf16[256,1536]{1,0:T(8,128)(2,1)S(1)}, bf16[256,1536]{1,0:T(8,128)(2,1)S(1)}, u32[]{:S(2)}, u32[]{:S(2)}) collective-permute-start(bf16[256,1536]{1,0:T(8,128)(2,1)S(1)} %collective-permute-done.32.refs_1_), channel_id=1, source_target_pairs={{0,1},{1,0},{2,3},{3,2},{4,5},{5,4},{6,7},{7,6},{8,9},{9,8},{10,11... | collective-permute-start | bytes 2359304 | tf_op jit(solution)/shard_map/ppermute | solution.py:54
  245.1 33.6 %collective-permute-start.41 = (bf16[1,3,192,512]{3,2,1,0:T(8,128)(2,1)S(1)}, bf16[1,3,192,512]{3,2,1,0:T(8,128)(2,1)S(1)}, u32[]{:S(2)}, u32[]{:S(2)}) collective-permute-start(bf16[1,3,192,512]{3,2,1,0:T(8,128)(2,1)S(1)} %collective-permute-done.39), channel_id=1, source_target_pairs={{0,16},{16,0},{1,17},{17,1},{2,18},{18,2},{3,19},{19,3},{4,20},{20... | collective-permute-start | bytes 1769480 | tf_op jit(solution)/shard_map/ppermute | solution.py:49
  246.6 32.1 %collective-permute-start.40 = (bf16[1,3,192,512]{3,2,1,0:T(8,128)(2,1)}, bf16[1,3,192,512]{3,2,1,0:T(8,128)(2,1)S(1)}, u32[]{:S(2)}, u32[]{:S(2)}) collective-permute-start(bf16[1,3,192,512]{3,2,1,0:T(8,128)(2,1)} %get-tuple-element.226), channel_id=1, source_target_pairs={{0,8},{4,12},{8,0},{12,4},{1,9},{5,13},{9,1},{13,5},{2,10},{6,14},... | collective-permute-start | bytes 1769480 | tf_op jit(solution)/shard_map/ppermute | solution.py:54
  298.1 39.0 %collective-permute-start.46 = (bf16[2,3,192,512]{3,2,1,0:T(8,128)(2,1)}, bf16[2,3,192,512]{3,2,1,0:T(8,128)(2,1)S(1)}, u32[]{:S(2)}, u32[]{:S(2)}) collective-permute-start(bf16[2,3,192,512]{3,2,1,0:T(8,128)(2,1)} %get-tuple-element.261), channel_id=1, source_target_pairs={{0,16},{16,0},{1,17},{17,1},{2,18},{18,2},{3,19},{19,3},{4,20},{20... | collective-permute-start | bytes 3538952 | tf_op jit(solution)/shard_map/ppermute | solution.py:49
  375.8 36.1 %collective-permute-start.52 = (bf16[1024,1536]{1,0:T(8,128)(2,1)}, bf16[1024,1536]{1,0:T(8,128)(2,1)}, u32[]{:S(2)}, u32[]{:S(2)}) collective-permute-start(bf16[1024,1536]{1,0:T(8,128)(2,1)} %get-tuple-element.281), channel_id=1, source_target_pairs={{0,1},{1,0},{2,3},{3,2},{4,5},{5,4},{6,7},{7,6},{8,9},{9,8},{10,11... | collective-permute-start | bytes 9437192 | tf_op jit(solution)/shard_map/ppermute | solution.py:54
  380.0 31.9 %collective-permute-start.54 = (bf16[256,1536]{1,0:T(8,128)(2,1)S(1)}, bf16[256,1536]{1,0:T(8,128)(2,1)S(1)}, u32[]{:S(2)}, u32[]{:S(2)}) collective-permute-start(bf16[256,1536]{1,0:T(8,128)(2,1)S(1)} %pad_maximum_fusion.12), channel_id=1, source_target_pairs={{0,4},{4,0},{8,12},{12,8},{1,5},{5,1},{9,13},{13,9},{2,6},{6,2},{1... | collective-permute-start | bytes 2359304 | tf_op jit(solution)/shard_map/ppermute | solution.py:54
  381.2 30.8 %collective-permute-start.53 = (bf16[256,1536]{1,0:T(8,128)(2,1)S(1)}, bf16[256,1536]{1,0:T(8,128)(2,1)}, u32[]{:S(2)}, u32[]{:S(2)}) collective-permute-start(bf16[256,1536]{1,0:T(8,128)(2,1)S(1)} %pad_maximum_fusion.11), channel_id=1, source_target_pairs={{0,2},{1,3},{2,0},{3,1},{4,6},{5,7},{6,4},{7,5},{8,10},{9,11},{10,... | collective-permute-start | bytes 2359304 | tf_op jit(solution)/shard_map/ppermute | solution.py:54
  452.7 36.2 %collective-permute-start.64 = (bf16[192,512]{1,0:T(8,128)(2,1)}, bf16[192,512]{1,0:T(8,128)(2,1)S(1)}, u32[]{:S(2)}, u32[]{:S(2)}) collective-permute-start(bf16[192,512]{1,0:T(8,128)(2,1)} %fusion.23), channel_id=1, source_target_pairs={{0,4},{4,0},{8,12},{12,8},{1,5},{5,1},{9,13},{13,9},{2,6},{6,2},{1... | collective-permute-start | bytes 589832 | tf_op jit(solution)/shard_map/ppermute | solution.py:54
  453.9 32.0 %collective-permute-start.62 = (bf16[2,3,192,512]{3,2,1,0:T(8,128)(2,1)}, bf16[2,3,192,512]{3,2,1,0:T(8,128)(2,1)}, u32[]{:S(2)}, u32[]{:S(2)}) collective-permute-start(bf16[2,3,192,512]{3,2,1,0:T(8,128)(2,1)} %get-tuple-element.296), channel_id=1, source_target_pairs={{0,16},{16,0},{1,17},{17,1},{2,18},{18,2},{3,19},{19,3},{4,20},{20... | collective-permute-start | bytes 3538952 | tf_op jit(solution)/shard_map/ppermute | solution.py:49
  457.8 31.2 %collective-permute-start.65 = (bf16[2,4,48,1536]{3,2,1,0:T(8,128)(2,1)}, bf16[2,4,48,1536]{3,2,1,0:T(8,128)(2,1)}, u32[]{:S(2)}, u32[]{:S(2)}) collective-permute-start(bf16[2,4,48,1536]{3,2,1,0:T(8,128)(2,1)} %fusion.13), channel_id=1, source_target_pairs={{0,2},{1,3},{2,0},{3,1},{4,6},{5,7},{6,4},{7,5},{8,10},{9,11},{10,... | collective-permute-start | bytes 3538952 | tf_op jit(solution)/shard_map/ppermute | solution.py:54
  458.6 30.3 %collective-permute-start.63 = (bf16[3,192,512]{2,1,0:T(8,128)(2,1)}, bf16[3,192,512]{2,1,0:T(8,128)(2,1)S(1)}, u32[]{:S(2)}, u32[]{:S(2)}) collective-permute-start(bf16[3,192,512]{2,1,0:T(8,128)(2,1)} %slice_bitcast_fusion.6), channel_id=1, source_target_pairs={{0,8},{4,12},{8,0},{12,4},{1,9},{5,13},{9,1},{13,5},{2,10},{6,14},... | collective-permute-start | bytes 1769480 | tf_op jit(solution)/shard_map/ppermute | solution.py:54
  510.5 37.8 %collective-permute-start.67 = (bf16[512,1536]{1,0:T(8,128)(2,1)}, bf16[512,1536]{1,0:T(8,128)(2,1)}, u32[]{:S(2)}, u32[]{:S(2)}) collective-permute-start(bf16[512,1536]{1,0:T(8,128)(2,1)} %slice.414), channel_id=1, source_target_pairs={{0,2},{1,3},{2,0},{3,1},{4,6},{5,7},{6,4},{7,5},{8,10},{9,11},{10,... | collective-permute-start | bytes 4718600 | tf_op jit(solution)/shard_map/ppermute | solution.py:54
  514.1 34.1 %collective-permute-start.68 = (bf16[256,1536]{1,0:T(8,128)(2,1)}, bf16[256,1536]{1,0:T(8,128)(2,1)}, u32[]{:S(2)}, u32[]{:S(2)}) collective-permute-start(bf16[256,1536]{1,0:T(8,128)(2,1)} %get-tuple-element.350), channel_id=1, source_target_pairs={{0,4},{12,8},{1,5},{13,9},{2,6},{14,10},{3,7},{15,11},{16,20},{28,... | collective-permute-start | bytes 2359304 | tf_op jit(solution)/shard_map/ppermute | solution.py:78
  555.7 54.0 %collective-permute-start.74 = (bf16[256,1536]{1,0:T(8,128)(2,1)S(1)}, bf16[256,1536]{1,0:T(8,128)(2,1)S(1)}, u32[]{:S(2)}, u32[]{:S(2)}) collective-permute-start(bf16[256,1536]{1,0:T(8,128)(2,1)S(1)} %fusion.9), channel_id=1, source_target_pairs={{0,8},{4,12},{8,0},{12,4},{1,9},{5,13},{9,1},{13,5},{2,10},{6,14},... | collective-permute-start | bytes 2359304 | tf_op jit(solution)/shard_map/ppermute | solution.py:78
  561.5 51.0 %collective-permute-start.71 = (bf16[256,1536]{1,0:T(8,128)(2,1)S(1)}, bf16[256,1536]{1,0:T(8,128)(2,1)S(1)}, u32[]{:S(2)}, u32[]{:S(2)}) collective-permute-start(bf16[256,1536]{1,0:T(8,128)(2,1)S(1)} %add_convert_fusion.8), channel_id=1, source_target_pairs={{0,4},{4,0},{8,12},{12,8},{1,5},{5,1},{9,13},{13,9},{2,6},{6,2},{1... | collective-permute-start | bytes 2359304 | tf_op jit(solution)/shard_map/ppermute | solution.py:54
  564.4 50.6 %collective-permute-start.76 = (bf16[4,48,768]{2,1,0:T(8,128)(2,1)S(1)}, bf16[4,48,768]{2,1,0:T(8,128)(2,1)S(1)}, u32[]{:S(2)}, u32[]{:S(2)}) collective-permute-start(bf16[4,48,768]{2,1,0:T(8,128)(2,1)S(1)} %slice_bitcast_fusion.14), channel_id=1, source_target_pairs={{0,16},{16,0},{1,17},{17,1},{2,18},{18,2},{3,19},{19,3},{4,20},{20... | collective-permute-start | bytes 884744 | tf_op jit(solution)/shard_map/ppermute | solution.py:49
  (143 other events, 2321.2 us)

commit v2 on v1

--- a/solution.py
+++ b/solution.py
@@ -92,6 +92,10 @@
     return [x, across, jnp.where(z == 0, end, below), jnp.where(z == 3, end, above)]
 
 
+def add(a, b):
+    return (a.astype(F32) + b.astype(F32)).astype(BF)
+
+
 def pick(x, index, dim=0):
     return lax.dynamic_index_in_dim(x, index, dim, False)
 
@@ -100,8 +104,19 @@
     n = lax.axis_size("dp")
     total = parts[n - 1]
     for k in range(1, n):
-        total = (shift(total, "dp", 1).astype(F32) + parts[n - 1 - k].astype(F32)).astype(BF)
+        total = add(shift(total, "dp", 1), parts[n - 1 - k])
     return total
+
+
+def dp_reduce_pair(parts):
+    n = lax.axis_size("dp")
+    total = parts[n - 1]
+    for k in range(1, n - 1):
+        total = add(shift(total, "dp", 1), parts[n - 1 - k])
+    if n == 1:
+        return [total[0], total[1]]
+    total = shift(total, "dp", 1)
+    return [add(total[0], parts[0][0]), add(total[1], parts[0][1])]
 
 
 def assemble(found, places):
@@ -150,44 +165,47 @@
     return block * cos + partner * sin
 
 
-def project(tok, gain, w, cos, sin, block_at):
-    rows, d = tok.shape
+def project(toks, gain, w, cos, sin, places):
+    rows, d = toks[0].shape
     n = w.shape[1]
-    blocks = (n - 128) // 128
-
-    def body(at_ref, tok_ref, gain_ref, w_ref, cos_ref, sin_ref, out_ref):
-        t = tok_ref[...].astype(F32)
-        normed = (t * rms(t) * gain_ref[...]).astype(BF)
-        u = mm(normed, w_ref[...])
-        for b in range(blocks):
-            out_ref[:, b * 128 : (b + 1) * 128] = turn(
-                u[:, b * 128 : (b + 1) * 128], cos_ref[...], sin_ref[...]
-            ).astype(BF)
-        out_ref[:, blocks * 128 :] = u[:, blocks * 128 :].astype(BF)
+    turned = n - 128
+    count = len(toks)
+
+    def body(at_ref, gain_ref, w_ref, cos_ref, sin_ref, *refs):
+        for i in range(count):
+            tok_ref, out_ref = refs[i], refs[count + i]
+            at = pl.ds(pl.multiple_of(at_ref[i] * rows, rows), rows)
+            cosine, sine = cos_ref[at, :], sin_ref[at, :]
+            t = tok_ref[...].astype(F32)
+            normed = (t * rms(t) * gain_ref[...]).astype(BF)
+            u = mm(normed, w_ref[...])
+            for b in range(0, turned, 128):
+                out_ref[:, b : b + 128] = turn(u[:, b : b + 128], cosine, sine).astype(BF)
+            out_ref[:, turned:] = u[:, turned:].astype(BF)
 
     return pl.pallas_call(
         body,
-        grid_spec=pltpu.PrefetchScalarGridSpec(
-            num_scalar_prefetch=1,
-            grid=(1,),
-            in_specs=[
-                pl.BlockSpec((rows, d), lambda i, at: (0, 0)),
-                pl.BlockSpec((1, d), lambda i, at: (0, 0)),
-                pl.BlockSpec((d, n), lambda i, at: (0, 0)),
-                pl.BlockSpec((rows, 128), lambda i, at: (at[0], 0)),
-                pl.BlockSpec((rows, 128), lambda i, at: (at[0], 0)),
-            ],
-            out_specs=pl.BlockSpec((rows, n), lambda i, at: (0, 0)),
-        ),
-        out_shape=jax.ShapeDtypeStruct((rows, n), BF),
+        out_shape=[jax.ShapeDtypeStruct((rows, n), BF)] * count,
+        in_specs=[SM] + [VM] * (4 + count),
+        out_specs=[VM] * count,
         compiler_params=params(),
-        cost_estimate=cost(2 * rows * d * n, 2 * d * n + 4 * rows * d),
+        cost_estimate=cost(2 * count * rows * d * n, 2 * d * n + 4 * count * rows * d),
         name="project",
-    )(block_at, tok, gain, w, cos, sin)
+    )(places, gain, w, cos, sin, *toks)
 
 
 def swapped(e):
     return (e & 1) * 2 + (e >> 1)
+
+
+def split_store(a_ref, b_ref, e, at, value):
+    @pl.when(e < 2)
+    def _():
+        a_ref[(e, *at)] = value
+
+    @pl.when(e >= 2)
+    def _():
+        b_ref[(e - 2, *at)] = value
 
 
 def lower_half(shape):
@@ -398,15 +416,12 @@
     )(scalars, *mixes, w_out, tok, gain)
 
 
-def join_back(scalars, addends, middle, cot, gain, w_out, mixes, here, nd, ne):
-    blocks = len(mixes)
-    rows, part = mixes[0].shape
-    d = middle.shape[1]
-
-    w_rows = d // (nd * blocks * ne)
-
-    def body(s_ref, here_ref, a_ref, b_ref, c_ref, mid_ref, cot_ref, gain_ref, w_ref, *refs):
-        ins, (gmid_ref, gmix_ref, gw_ref, gg_ref) = refs[:blocks], refs[blocks:]
+def join_back(scalars, addends, middle, cot, gain, w_out):
+    blocks = 4
+    rows, d = middle.shape
+    part = d // blocks
+
+    def body(s_ref, a_ref, b_ref, c_ref, mid_ref, cot_ref, gain_ref, w_ref, gmid_ref, gmix_ref, br_ref, gg_ref):
         me = s_ref[4]
         grad_hidden = a_ref[...].astype(F32) + b_ref[...].astype(F32) + c_ref[...].astype(F32)
         middle = mid_ref[...]
@@ -416,32 +431,55 @@
         u = grad_hidden * gain_ref[...]
         grad_middle = cot_ref[...] + inv * (u - normal * jnp.mean(u * normal, axis=-1, keepdims=True))
         gmid_ref[...] = grad_middle
-        branch = (residual_scale * grad_middle).astype(BF)
+        br_ref[...] = (residual_scale * grad_middle).astype(BF)
         for k in range(blocks):
             at = pl.ds(pl.multiple_of(lax.rem(me - k + blocks, blocks) * part, part), part)
-            gmix_ref[k] = mm(branch, w_ref[at, :], NT).astype(BF)
-            gw = mm(ins[k][...], branch, TN)
+            gmix_ref[k] = mm(br_ref[...], w_ref[at, :], NT).astype(BF)
+
+    return pl.pallas_call(
+        body,
+        out_shape=(
+            jax.ShapeDtypeStruct((rows, d), F32),
+            jax.ShapeDtypeStruct((blocks, rows, part), BF),
+            jax.ShapeDtypeStruct((rows, d), BF),
+            jax.ShapeDtypeStruct((1, d), F32),
+        ),
+        in_specs=[SM] + [VM] * 7,
+        out_specs=(VM, VM, VM, VM),
+        compiler_params=params(),
+        cost_estimate=cost(2 * rows * d * d, 2 * d * d + 18 * rows * d),
+        name="join_back",
+    )(scalars, *addends, middle, cot, gain, w_out)
+
+
+def join_weights(scalars, here, branch, mixes, nd, ne):
+    blocks = len(mixes)
+    rows, part = mixes[0].shape
+    d = branch.shape[1]
+    w_rows = d // (nd * blocks * ne)
+
+    def body(s_ref, here_ref, br_ref, *refs):
+        ins, (gwa_ref, gwb_ref) = refs[:blocks], refs[blocks:]
+        me = s_ref[4]
+        for k in range(blocks):
+            gw = mm(ins[k][...], br_ref[...], TN)
             for i in range(part // w_rows):
                 q = lax.rem(me - k + blocks, blocks) * (part // w_rows) + i
                 e = swapped(jnp.bitwise_xor(lax.rem(q, ne), here_ref[3]))
                 b = lax.div(q, ne)
                 m = lax.rem(lax.div(b, blocks) - here_ref[0] + nd, nd)
-                gw_ref[e, m, lax.rem(b, blocks)] = gw[i * w_rows : (i + 1) * w_rows, :].astype(BF)
+                put = gw[i * w_rows : (i + 1) * w_rows, :].astype(BF)
+                split_store(gwa_ref, gwb_ref, e, (m, lax.rem(b, blocks)), put)
 
     return pl.pallas_call(
         body,
-        out_shape=(
-            jax.ShapeDtypeStruct((rows, d), F32),
-            jax.ShapeDtypeStruct((blocks, rows, part), BF),
-            jax.ShapeDtypeStruct((ne, nd, blocks, w_rows, d), BF),
-            jax.ShapeDtypeStruct((1, d), F32),
-        ),
-        in_specs=[SM, SM] + [VM] * (7 + blocks),
-        out_specs=(VM, VM, VM, VM),
+        out_shape=(jax.ShapeDtypeStruct((2, nd, blocks, w_rows, d), BF),) * 2,
+        in_specs=[SM, SM] + [VM] * (1 + blocks),
+        out_specs=(VM, VM),
         compiler_params=params(),
-        cost_estimate=cost(4 * rows * d * d, 4 * d * d + 18 * rows * d),
-        name="join_back",
-    )(scalars, here, *addends, middle, cot, gain, w_out, *mixes)
+        cost_estimate=cost(2 * rows * d * d, 2 * d * d + 4 * rows * d),
+        name="join_weights",
+    )(scalars, here, branch, *mixes)
 
 
 def halves(w, odd, devices):
@@ -477,19 +515,26 @@
     )(odd[None].astype(jnp.int32), w)
 
 
-def whole(own, other, theirs, odd, devices):
-    _, r, width = own.shape
+def whole(parts, odd, devices):
+    count = len(parts)
+    _, r, width = parts[0][0].shape
     r3 = r // 3
     unit = FF // devices
-    if 2 * unit != 128:
+
+    def plain(own, other, theirs):
         total = own.astype(F32) + other.astype(F32)
         theirs = theirs.astype(F32)
-        parts = jnp.stack([jnp.where(odd == 0, total[0], theirs), jnp.where(odd == 0, theirs, total[0])])
-        parts = parts.reshape(2, r, 2, devices // 4, 2, unit)
+        pair = jnp.stack([jnp.where(odd == 0, total[0], theirs), jnp.where(odd == 0, theirs, total[0])])
+        pair = pair.reshape(2, r, 2, devices // 4, 2, unit)
         down = [total[2, b * r3 : (b + 1) * r3] for b in range(3)]
-        return jnp.transpose(parts, (1, 2, 3, 4, 0, 5)).reshape(r, 2 * width), jnp.concatenate(down, axis=1)
-
-    def body(odd_ref, own_ref, other_ref, their_ref, in_ref, down_ref):
+        return jnp.transpose(pair, (1, 2, 3, 4, 0, 5)).reshape(r, 2 * width), jnp.concatenate(down, axis=1)
+
+    if 2 * unit != 128:
+        done = [plain(*p) for p in parts]
+        return jnp.stack([p[0] for p in done]), jnp.stack([p[1] for p in done])
+
+    def body(odd_ref, own_ref, other_ref, their_ref, *refs):
+        in_ref, down_ref = refs[-2], refs[-1]
         low = lower_half((r, 128))
         even = odd_ref[0] == 0
         for m in range(width // 128):
@@ -497,24 +542,37 @@
             mine = own_ref[0, :, at].astype(F32) + other_ref[0, :, at].astype(F32)
             their = their_ref[:, at].astype(F32)
             evens, odds = jnp.where(even, mine, their), jnp.where(even, their, mine)
-            in_ref[:, 2 * m * 128 : (2 * m + 1) * 128] = jnp.where(low, evens, pltpu.roll(odds, 64, 1))
-            in_ref[:, (2 * m + 1) * 128 : (2 * m + 2) * 128] = jnp.where(low, pltpu.roll(evens, 64, 1), odds)
+            in_ref[0, :, 2 * m * 128 : (2 * m + 1) * 128] = jnp.where(low, evens, pltpu.roll(odds, 64, 1))
+            in_ref[0, :, (2 * m + 1) * 128 : (2 * m + 2) * 128] = jnp.where(
+                low, pltpu.roll(evens, 64, 1), odds
+            )
         for b in range(3):
             at = slice(b * r3, (b + 1) * r3)
-            down_ref[:, b * width : (b + 1) * width] = own_ref[2, at, :].astype(F32) + other_ref[2, at, :].astype(F32)
-
-    return pl.pallas_call(
-        body,
-        out_shape=(
-            jax.ShapeDtypeStruct((r, 2 * width), F32),
-            jax.ShapeDtypeStruct((r3, 3 * width), F32),
-        ),
-        in_specs=[SM, VM, VM, VM],
-        out_specs=(VM, VM),
-        compiler_params=params(),
-        cost_estimate=cost(0, 20 * r * width),
-        name="whole",
-    )(odd[None].astype(jnp.int32), own, other, theirs)
+            down_ref[0, :, b * width : (b + 1) * width] = (
+                own_ref[2, at, :].astype(F32) + other_ref[2, at, :].astype(F32)
+            )
+
+    done = ()
+    for e, (own, other, theirs) in enumerate(parts):
+        fixed = lambda *shape: pl.BlockSpec(shape, lambda i: (0,) * len(shape))
+        done = pl.pallas_call(
+            body,
+            grid=(1,),
+            out_shape=(
+                jax.ShapeDtypeStruct((count, r, 2 * width), F32),
+                jax.ShapeDtypeStruct((count, r3, 3 * width), F32),
+            ),
+            in_specs=[SM, fixed(3, r, width), fixed(3, r, width), fixed(r, width)] + [ANY] * len(done),
+            out_specs=(
+                pl.BlockSpec((1, r, 2 * width), lambda i, e=e: (e, 0, 0)),
+                pl.BlockSpec((1, r3, 3 * width), lambda i, e=e: (e, 0, 0)),
+            ),
+            input_output_aliases={4: 0, 5: 1} if done else {},
+            compiler_params=params(),
+            cost_estimate=cost(0, 20 * r * width),
+            name="whole",
+        )(odd[None].astype(jnp.int32), own, other, theirs, *done)
+    return done
 
 
 def experts_rows(places, which, rows_in, cots, shards, sums, last):
@@ -523,8 +581,11 @@
     rows = piece * group
     tiles = len(rows_in) // group
     total = rows * tiles
-    count = len(shards)
-    n, _, r, width = shards[0].shape
+    count, n = len(shards), len(shards[0])
+    r, width = shards[0][0][0].shape[-2:]
+    arrays = {id(t): t for shard in shards for t, _ in shard}
+    slot = {key: k for k, key in enumerate(arrays)}
+    arrays = list(arrays.values())
     half = width // 2
     r3 = r // 3
     first = sums is None
@@ -532,7 +593,7 @@
     def body(places_ref, *refs):
         n_in = tiles * group
         h_refs, c_refs, refs = refs[:n_in], refs[n_in : 2 * n_in], refs[2 * n_in :]
-        w_refs, refs = refs[:count], refs[count:]
+        w_refs, refs = refs[: len(arrays)], refs[len(arrays) :]
         if not first:
             in_h, in_o, refs = refs[0], refs[1], refs[2:]
         if last:
@@ -558,15 +619,18 @@
             copies = []
             for i in range(count):
                 for e in range(n):
+                    array, which_of = shards[i][e]
+                    source = w_refs[slot[id(array)]]
+                    source = source if which_of is None else source.at[which_of]
                     parts = []
                     for b in range(2):
                         at = pl.multiple_of(places_ref[3 * i + b] * r, r)
-                        parts.append((w_refs[i].at[e, b], wiv.at[pl.ds(at, r), e * width : (e + 1) * width]))
+                        parts.append((source.at[b], wiv.at[pl.ds(at, r), e * width : (e + 1) * width]))
                     at = pl.multiple_of(places_ref[3 * i + 2] * r3 + e * half, r3)
                     for b in range(3):
                         parts.append(
                             (
-                                w_refs[i].at[e, 2, b * r3 : (b + 1) * r3, :],
+                                source.at[2, b * r3 : (b + 1) * r3, :],
                                 wdv.at[pl.ds(at, r3), b * width : (b + 1) * width],
                             )
                         )
@@ -574,11 +638,14 @@
                         copies.append(pltpu.make_async_copy(a, b, sems.at[i, e, k]))
             for copy in copies:
                 copy.start()
-            for a, b in moves:
+            for a, b in moves[:group]:
                 a.start()
                 b.start()
             for copy in copies:
                 copy.wait()
+            for a, b in moves[group:]:
+                a.start()
+                b.start()
 
         for i in range(tiles):
 
@@ -608,8 +675,8 @@
         if first:
             ht_ref[...] = h.T
         if not first:
-            o = o + in_o[...]
-            gh = gh + in_h[...]
+            o = o + in_o[...].astype(F32)
+            gh = gh + in_h[...].astype(F32)
         if last:
 
             @pl.when(t < tiles // 2)
@@ -623,8 +690,8 @@
                 rest_h[...] = gh.astype(BF)
 
         else:
-            out_o[...] = o
-            out_h[...] = gh
+            out_o[...] = o.astype(BF)
+            out_h[...] = gh.astype(BF)
 
     tile = lambda c: pl.BlockSpec((rows, c), lambda t: (t, 0))
     flat = lambda c: pl.BlockSpec((c, rows), lambda t: (0, t))
@@ -634,7 +701,7 @@
         back = pl.BlockSpec((rows, d), lambda t: (jnp.maximum(t - tiles // 2, 0), 0))
         sum_specs = (front, back, front, back)
     else:
-        sum_shapes = (jax.ShapeDtypeStruct((total, d), F32),) * 2
+        sum_shapes = (jax.ShapeDtypeStruct((total, d), BF),) * 2
         sum_specs = (tile(d), tile(d))
     return pl.pallas_call(
         body,
@@ -646,7 +713,7 @@
         )
         + ((jax.ShapeDtypeStruct((d, total), BF),) if first else ()),
         in_specs=[SM]
-        + [ANY] * (2 * len(rows_in) + count)
+        + [ANY] * (2 * len(rows_in) + len(arrays))
         + ([] if first else [tile(d), tile(d)]),
         out_specs=sum_specs + (tile(n * width), flat(n * half)) + ((flat(d),) if first else ()),
         scratch_shapes=[
@@ -661,7 +728,7 @@
         compiler_params=params(),
         cost_estimate=cost(6 * n * total * d * width, 50e6, n * total * half),
         name="experts_rows",
-    )(places, *rows_in, *cots, *shards, *(() if first else sums))
+    )(places, *rows_in, *cots, *arrays, *(() if first else sums))
 
 
 def experts_weights(scalars, rows_t, cots, gb, ga_t, n, devices):
@@ -687,11 +754,13 @@
             pltpu.make_async_copy(c_refs[i].at[:, :d], c_ref.at[pl.ds(i * rows, rows), :], c_sems.at[i])
             for i in range(tiles)
         ]
-        for copy in first + second:
+        for copy in first[:2]:
             copy.start()
         first[0].wait()
         for k in range(nd):
             first[1 + k].wait()
+            for copy in first[2:] + second if k == 0 else []:
+                copy.start()
             part = mm(h_ref[k], gb_ref[...]).astype(BF)
             for z in range(4):
                 where = jnp.bitwise_xor(s_ref[2], z // 2)
@@ -741,27 +810,43 @@
     return [outs[e * nd : (e + 1) * nd] for e in range(n)]
 
 
-def finish(scalars, dqkv, w, toks, gain, gain_grad, here, nd, ne):
+def finish(dqkv, w, blocks):
+    total, width = dqkv.shape
+    d = w.shape[0]
+    rows = total // blocks
+
+    def body(dq_ref, w_ref, gn_ref):
+        gn_ref[0] = mm(dq_ref[...], w_ref[...], NT).astype(BF)
+
+    return pl.pallas_call(
+        body,
+        grid=(blocks,),
+        out_shape=jax.ShapeDtypeStruct((blocks, rows, d), BF),
+        in_specs=[pl.BlockSpec((rows, width), lambda t: (t, 0)), pl.BlockSpec((d, width), lambda t: (0, 0))],
+        out_specs=pl.BlockSpec((1, rows, d), lambda t: (t, 0, 0)),
+        compiler_params=params(),
+        cost_estimate=cost(2 * total * d * width, 4 * total * d),
+        name="finish",
+    )(dqkv, w)
+
+
+def finish_weights(scalars, here, dqkv, gn, toks, gain, gain_grad, nd, ne):
     blocks = len(toks)
     rows, d = toks[0].shape
     width = dqkv.shape[1]
-
     w_rows = d // (nd * blocks * ne)
 
-    def body(s_ref, here_ref, dq_ref, w_ref, gain_ref, gg_ref, *refs):
-        ins, (gn_ref, gw_ref, acc) = refs[:blocks], refs[blocks:]
+    def body(s_ref, here_ref, dq_ref, gn_ref, gain_ref, gg_ref, *refs):
+        ins, (gwa_ref, gwb_ref, acc) = refs[:blocks], refs[blocks:]
         gg = jnp.zeros((1, d), F32)
         for k in range(blocks):
             to = s_ref[k]
             at = pl.ds(pl.multiple_of(to * rows, rows), rows)
-            dqkv_block = dq_ref[at, :]
             t = ins[k][...].astype(F32)
             normal = t * rms(t)
             normed = (normal * gain_ref[...]).astype(BF)
-            gn = mm(dqkv_block, w_ref[...], NT)
-            gg = gg + jnp.sum(gn * normal, axis=0, keepdims=True)
-            gn_ref[to] = gn.astype(BF)
-            part = mm(normed, dqkv_block, TN)
+            gg = gg + jnp.sum(gn_ref[to].astype(F32) * normal, axis=0, keepdims=True)
+            part = mm(normed, dq_ref[at, :], TN)
             acc[...] = part if k == 0 else acc[...] + part
         row = lax.broadcasted_iota(jnp.int32, (128, d), 0)
         both = jnp.where(row == 0, gg, jnp.where(row == 1, gg_ref[...], 0.0)).T
@@ -769,22 +854,19 @@
             e = swapped(jnp.bitwise_xor(q % ne, here_ref[3]))
             m = lax.rem(q // ne // blocks - here_ref[0] + nd, nd)
             at = slice(q * w_rows, (q + 1) * w_rows)
-            gw_ref[e, m, q // ne % blocks, :, :width] = acc[at, :].astype(BF)
-            gw_ref[e, m, q // ne % blocks, :, width:] = both[at, :].astype(BF)
+            put = jnp.concatenate([acc[at, :], both[at, :]], axis=1).astype(BF)
+            split_store(gwa_ref, gwb_ref, e, (m, q // ne % blocks), put)
 
     return pl.pallas_call(
         body,
-        out_shape=(
-            jax.ShapeDtypeStruct((blocks, rows, d), BF),
-            jax.ShapeDtypeStruct((ne, nd, blocks, w_rows, width + 128), BF),
-        ),
+        out_shape=(jax.ShapeDtypeStruct((2, nd, blocks, w_rows, width + 128), BF),) * 2,
         in_specs=[SM, SM] + [VM] * (4 + blocks),
         out_specs=(VM, VM),
         scratch_shapes=[pltpu.VMEM((d, width), F32)],
         compiler_params=params(),
-        cost_estimate=cost(4 * blocks * rows * d * width, 8 * blocks * rows * d),
-        name="finish",
-    )(scalars, here, dqkv, w, gain, gain_grad, *toks)
+        cost_estimate=cost(2 * blocks * rows * d * width, 6 * blocks * rows * d),
+        name="finish_weights",
+    )(scalars, here, dqkv, gn, gain, gain_grad, *toks)
 
 
 def per_device(
@@ -832,15 +914,17 @@
     odd, zh = jnp.bitwise_and(z, 1), z // 2
     batch = local_experts // 2
     tok, cot = tokens[0], cotangent[0]
-    cot_b = (residual_scale * cot).astype(BF)
     flip_e = lambda v, e: flip(v, "exp", e)
 
-    def row_blocks(found, owners):
+    def row_blocks(found, owners, order):
         at = [
             (mod(x - m, nd) * nz + p) * ne + jnp.bitwise_xor(j, e + 2 * b)
-            for e in (0, 1) for m in range(nd) for b in (0, 1) for p in owners
+            for e in (0, 1) for b, m in order for p in owners
         ]
         return assemble(found, jnp.stack(at).astype(i32))
+
+    by_m = [(b, m) for m in range(nd) for b in (0, 1)]
+    by_b = [(b, m) for b in (0, 1) for m in range(nd)]
 
     here = jnp.stack([x, odd, zh, j]).astype(i32)
 
@@ -855,27 +939,28 @@
         )
         for p in range(nz)
     ]
+    cut = rows // 2
+    toks = [tok, shift(tok, "ctx", 1)]
     w_parts = jnp.stack(parts)
-    toks = [tok, shift(tok, "ctx", 1)]
     w_mine = [pick(w_parts, z)] + [shift(pick(w_parts, mod(z + k, nz)), "ctx", k) for k in range(1, nz)]
-    hits = routes[0][:, :, None] == jnp.arange(128, dtype=i32)[None, None, :]
-    dense = jnp.sum(jnp.where(hits, gates[0].astype(F32)[:, :, None], 0.0), axis=1).astype(BF)
-    cot_b = jnp.concatenate([cot_b, dense], axis=1)
-    mine_in, their_in = halves(w_in, odd, devices)
-    down = jnp.concatenate([w_down[:, :, b * FF : (b + 1) * FF] for b in range(d // FF)], axis=1)
     run.end(toks, w_mine)
 
-    cut = rows // 2
-    half_2 = [shift(run.hold(toks[1][:cut]), "ctx", 1)]
+    half_2 = [shift(run.hold(toks[1])[:cut], "ctx", 1)]
+    mine_in, their_in = halves(run.hold(w_in), odd, devices)
+    down = run.hold(w_down)
+    down = jnp.concatenate([down[:, :, b * FF : (b + 1) * FF] for b in range(d // FF)], axis=1)
     w_mine = jnp.stack(w_mine)
     w_mine = jnp.stack([w_mine, flip_e(run.hold(w_mine), 2)])
     line = [hop(run.hold(w_out), pairs) for pairs in (ACROSS, UP, DOWN)]
     run.end(half_2, w_mine, line, mine_in)
 
-    half_2.append(shift(run.hold(toks[1][cut:]), "ctx", 1))
+    half_2.append(shift(run.hold(toks[1])[cut:], "ctx", 1))
+    hits = run.hold(routes)[0][:, :, None] == jnp.arange(128, dtype=i32)[None, None, :]
+    dense = jnp.sum(jnp.where(hits, gates[0].astype(F32)[:, :, None], 0.0), axis=1).astype(BF)
+    cot_b = jnp.concatenate([(residual_scale * run.hold(cot)).astype(BF), dense], axis=1)
     w_found = ring(run.hold(w_mine), "dp")
     line_end = hop(run.hold(line[0]), OUTER)
-    run.end(half_2, w_found, line_end)
+    run.end(half_2, w_found, line_end, cot_b)
 
     toks.append(jnp.concatenate(half_2))
     toks.append(shift(run.hold(toks[2]), "ctx", 1))
@@ -883,49 +968,49 @@
     w_found = w_found + [flip_e(t, 1) for t in run.hold(w_found)]
     w_line = ring(run.hold(jnp.stack(line_gather(*line, line_end, w_out))), "dp")
     cot_2 = flip_e(run.hold(cot_b), 2)
-    w_qkv = row_blocks(w_found, places)
-    at = [p[None].astype(i32) for p in places]
-    pieces = [project(toks[k], gain_a, w_qkv, cos, sin, at[k]) for k in range(nz - 1)]
+    w_qkv = row_blocks(w_found, places, by_m)
+    at = jnp.stack(places).astype(i32)
+    pieces = project(toks[: nz - 1], gain_a, w_qkv, cos, sin, at[: nz - 1])
     run.end(toks, pieces, got_1, w_line, cot_2)
 
-    near_1 = jnp.stack([mine_in[:batch], got_1, down[:batch]], axis=1)
-    far = [flip(run.hold(near_1[:1]), "ctx", 2)]
-    own_1 = ring(run.hold(near_1), "dp")
+    packet = lambda e, got: jnp.stack([mine_in[e], got[e % batch], down[e]])
+    near = [packet(e, got_1) for e in range(batch)]
+    far = [flip(run.hold(near[0]), "ctx", 2)]
+    own = [ring(run.hold(jnp.stack(near)), "dp")]
     w_line = jnp.stack(w_line)
-    w_line = jnp.stack([w_line, flip_e(run.hold(w_line), 2)], axis=1)
+    w_line = jnp.stack([w_line, flip_e(run.hold(w_line), 2)])
     cot_n = flip(run.hold(cot_b), "ctx", 1)
-    pieces.append(project(run.hold(toks[3]), gain_a, w_qkv, cos, sin, at[3]))
+    pieces = pieces + project([run.hold(toks[3])], gain_a, w_qkv, cos, sin, at[nz - 1 :])
     mix_out, lse = attend(scalars, pieces, heads, kvs)
-    run.end(far, own_1, w_line, cot_n, mix_out)
+    run.end(far, own, w_line, cot_n, mix_out)
 
     mixes = run.hold([mix_out[k] for k in range(nz)])
     mixes = [mixes[0]] + [shift(mixes[k], "ctx", k) for k in range(1, nz)]
     w_line = [w_line, flip_e(run.hold(w_line), 1)]
     cot_n2 = flip_e(run.hold(cot_n), 2)
-    w_out_all = row_blocks(w_line, line_places(z))
+    w_out_all = row_blocks(w_line, line_places(z), by_b)
     run.end(mixes, w_out_all, cot_n2)
 
     cot_1, cot_3 = flip_e(run.hold(cot_b), 1), flip_e(run.hold(cot_2), 1)
+    cot_n1, cot_n3 = flip_e(run.hold(cot_n), 1), flip_e(run.hold(cot_n2), 1)
     got_2 = flip(run.hold(their_in[batch:]), "ctx", 1)
     middle, hidden = join(scalars, run.hold(mixes), w_out_all, tok, gain_m)
-    run.end(hidden, got_2, cot_1, cot_3)
+    run.end(hidden, got_2, cot_1, cot_3, cot_n1, cot_n3)
 
     hidden_2, hidden_n = flip_e(run.hold(hidden), 2), flip(run.hold(hidden), "ctx", 1)
-    near_2 = jnp.stack([mine_in[batch:], got_2, down[batch:]], axis=1)
-    far.append(flip(run.hold(near_1[1:]), "ctx", 2))
-    own_2 = ring(run.hold(near_2), "dp")
+    far += [flip(run.hold(near[e]), "ctx", 2) for e in range(1, batch)]
+    near += [packet(e, got_2) for e in range(batch, local_experts)]
+    own.append(ring(run.hold(jnp.stack(near[batch:])), "dp"))
     hidden_1 = flip_e(run.hold(hidden), 1)
-    run.end(hidden_1, hidden_2, hidden_n, far, own_2)
+    run.end(hidden_1, hidden_2, hidden_n, far, own)
 
     hidden_n2 = flip_e(run.hold(hidden_n), 2)
     hidden_n1, hidden_3 = flip_e(run.hold(hidden_n), 1), flip_e(run.hold(hidden_2), 1)
-    over_1 = ring(run.hold(jnp.concatenate(far)), "dp")
-    far_2 = [flip(run.hold(near_2[:1]), "ctx", 2)]
-    run.end(hidden_n2, hidden_n1, hidden_3, over_1, far_2)
-
-    hidden_n3 = flip_e(run.hold(hidden_n2), 1)
-    cot_n1, cot_n3 = flip_e(run.hold(cot_n), 1), flip_e(run.hold(cot_n2), 1)
-    rows_in = [hidden, hidden_n, hidden_2, hidden_n2, hidden_1, hidden_n1, hidden_3, hidden_n3]
+    over = [ring(run.hold(jnp.stack(far)), "dp")]
+    far.append(flip(run.hold(near[batch]), "ctx", 2))
+    run.end(hidden_n1, hidden_3, hidden_n2, over, far)
+
+    rows_in = [hidden, hidden_n, hidden_2, hidden_n2, hidden_1, hidden_n1, hidden_3, None]
     cots = [cot_b, cot_n, cot_2, cot_n2, cot_1, cot_n1, cot_3, cot_n3]
     w_at = []
     for zc in (z, jnp.bitwise_xor(z, 2)):
@@ -933,116 +1018,110 @@
             xc = mod(x - m, nd)
             w_at += [xc * nz + zc, xc * nz + jnp.bitwise_xor(zc, 1), xc * 2 + zc // 2]
     w_at = jnp.stack(w_at + [j * local_experts]).astype(i32)
-    far_2.append(flip(run.hold(near_2[1:]), "ctx", 2))
-    over_2 = [ring(run.hold(far_2[0]), "dp")]
-    sum_h, sum_o, gb, ga_t, rows_t = experts_rows(
-        w_at, 0, run.hold(rows_in), cots, own_1 + over_1, None, False
-    )
-    run.end(far_2, over_2, sum_h)
-
-    over_2.append(ring(run.hold(far_2[1]), "dp"))
+    rows_in = run.hold(rows_in[:-1]) + [flip_e(run.hold(hidden_n2), 1)]
+    far += [flip(run.hold(near[e]), "ctx", 2) for e in range(batch + 1, local_experts)]
+    over.append(ring(run.hold(far[batch]), "dp"))
+    shards = [[(t, e) for e in range(batch)] for t in own[0] + over[0]]
+    sum_h, sum_o, gb, ga_t, rows_t = experts_rows(w_at, 0, rows_in, cots, shards, None, False)
+    run.end(far, over, sum_h)
+
+    over += [ring(run.hold(far[e]), "dp") for e in range(batch + 1, local_experts)]
     gw_1 = experts_weights(here, rows_t, cots, run.hold(gb), ga_t, batch, devices)
-    run.end(over_2, gw_1)
-
-    x_0 = dp_reduce(run.hold(gw_1[0]))
-    over_2 = [jnp.concatenate(t) for t in zip(*over_2)]
+    run.end(over, gw_1)
+
+    x_0 = dp_reduce_pair(run.hold(gw_1[0]))
+    shards = [[(t, e) for e in range(batch)] for t in own[1]]
+    shards += [[(t, None) for t in pair] for pair in zip(*over[1:])]
     sum_h, rest_h, sum_o, rest_o, gb, ga_t = experts_rows(
-        w_at, batch, run.hold(rows_in), cots, own_2 + over_2, (sum_h, sum_o), True
+        w_at, batch, run.hold(rows_in), cots, shards, (sum_h, sum_o), True
     )
     run.end(x_0, sum_h)
 
-    def swap(own, other):
-        return flip((own[0, 1].astype(F32) + other[1].astype(F32)).astype(BF), "ctx", 1)
-
     rest_h = flip_e(run.hold(rest_h), 1)
     run.end(rest_h)
 
     part = rows // 2
     sum_h = [
-        (sum_h[a * part : b * part].astype(F32) + rest_h[a * part : b * part].astype(F32)).astype(BF)
+        add(sum_h[a * part : b * part], rest_h[a * part : b * part])
         for a, b in ((0, 2), (2, 3), (3, 4), (4, 5), (5, 6), (6, 7), (7, 8))
     ]
     by_y, by_z = flip_e(run.hold(sum_h[5]), 2), flip(run.hold(sum_h[6]), "ctx", 1)
-    z_0 = flip(run.hold(x_0)[1], "ctx", 2)
-    x_1 = dp_reduce(run.hold(gw_1[1]))
+    z_0 = flip(run.hold(x_0[1]), "ctx", 2)
+    x_1 = dp_reduce_pair(run.hold(gw_1[1]))
+    rest_o = flip_e(run.hold(rest_o), 1)
     gw_2 = experts_weights(here, rows_t, cots, run.hold(gb), ga_t, batch, devices)
-    run.end(by_y, by_z, z_0, x_1, gw_2)
-
-    add = lambda a, b: (a.astype(F32) + b.astype(F32)).astype(BF)
-    near_h = flip_e(run.hold(jnp.concatenate([sum_h[3], add(sum_h[4], by_z)])), 2)
-    other_h = flip(run.hold(jnp.concatenate([add(sum_h[1], by_y), sum_h[2]])), "ctx", 1)
-    z_1 = flip(run.hold(x_1)[1], "ctx", 2)
-    x_2 = dp_reduce(run.hold(gw_2[0]))
-    rest_o = flip_e(run.hold(rest_o), 1)
-    run.end(near_h, other_h, z_1, x_2, rest_o)
-
-    def fold(g):
-        return g[0].astype(F32), (g[1].astype(F32) + g[3].astype(F32)).astype(BF)
-
-    swap_0 = swap(*run.hold([x_0, z_0]))
-    grad_middle, grad_mix, grad_w_out, grad_gain_m = join_back(
-        scalars, [sum_h[0], *run.hold([near_h, other_h])], middle, cot, gain_m, w_out_all, mixes, here, nd, ne
+    run.end(by_y, by_z, z_0, x_1, rest_o, gw_2)
+
+    near_h = flip_e(jnp.concatenate([sum_h[3], add(run.hold(sum_h[4]), by_z)]), 2)
+    other_h = flip(jnp.concatenate([add(run.hold(sum_h[1]), by_y), sum_h[2]]), "ctx", 1)
+    z_1 = flip(run.hold(x_1[1]), "ctx", 2)
+    x_2 = dp_reduce_pair(run.hold(gw_2[0]))
+    sum_o = [add(sum_o[a * rows : (a + 1) * rows], rest_o[a * rows : (a + 1) * rows]) for a in range(4)]
+    run.end(near_h, other_h, z_1, x_2, sum_o)
+
+    grad_middle, grad_mix, branch, grad_gain_m = join_back(
+        scalars, [sum_h[0], *run.hold([near_h, other_h])], middle, cot, gain_m, w_out_all
     )
     grad_mixes = [grad_mix[0]] + [shift(grad_mix[k], "ctx", -k) for k in range(1, nz)]
-    wo_core = flip_e(grad_w_out[2:], 1)
-    run.end(grad_mixes, wo_core, swap_0)
-
-    x_3 = dp_reduce(run.hold(gw_2[1]))
-    z_2 = flip(run.hold(x_2)[1], "ctx", 2)
-    swap_1 = swap(*run.hold([x_1, z_1]))
-    wo_core = run.hold(wo_core)
-    wo = add(grad_w_out[0], wo_core[0])
-    wo_far = flip_e(add(grad_w_out[1], wo_core[1]), 2)
+    x_3 = dp_reduce_pair(run.hold(gw_2[1]))
+    far_o1 = flip_e(run.hold(sum_o[3]), 2)
+    wo_a, wo_b = join_weights(scalars, here, branch, mixes, nd, ne)
+    run.end(grad_mixes, x_3, far_o1, wo_b)
+
+    z_2 = flip(run.hold(x_2[1]), "ctx", 2)
+    far_o = flip_e(run.hold(sum_o[2]), 2)
+    other_o = flip(add(sum_o[1], run.hold(far_o1)), "ctx", 1)
+    wo_b = flip_e(run.hold(wo_b), 1)
     dqkv = attend_back(scalars, pieces, run.hold(grad_mixes), lse, cos, sin, heads, kvs)
-    sum_o = add(sum_o, run.hold(rest_o))
-    run.end(x_3, z_2, swap_1, wo_far, dqkv, sum_o)
-
-    wo = dp_reduce(list(run.hold(add(wo, wo_far))))
-    grad_normed, grad_w = finish(
-        scalars, run.hold(dqkv), w_qkv, toks, gain_a, grad_gain_m, here, nd, ne
+    grad_normed = finish(dqkv, w_qkv, nz)
+    run.end(z_2, far_o, other_o, wo_b, grad_normed)
+
+    z_3 = flip(run.hold(x_3[1]), "ctx", 2)
+    gw_a, gw_b = finish_weights(scalars, here, dqkv, run.hold(grad_normed), toks, gain_a, grad_gain_m, nd, ne)
+    x_held = run.hold([x_0[0], x_1[0], x_2[0]])
+    swap = flip(jnp.stack([add(t[1], u[1]) for t, u in zip(x_held, (z_0, z_1, z_2))]), "ctx", 1)
+    wo = add(wo_a, lax.optimization_barrier((wo_b, gw_b))[0])
+    run.end(gw_b, swap, wo, z_3)
+
+    tail = run.hold(grad_normed)
+    total = shift(pick(tail, mod(z - 1, nz)), "ctx", 1)
+    gw_b = flip_e(run.hold(gw_b), 1)
+    wo_far = flip_e(run.hold(wo[1]), 2)
+    swap_3 = flip(add(run.hold(x_3[0])[1], z_3[1]), "ctx", 1)
+    gw = add(gw_a, gw_b)
+    run.end(total, gw, wo_far, swap_3)
+
+    total = shift(add(total, pick(run.hold(tail), mod(z - 2, nz))), "ctx", 1)
+    gw_far = flip_e(run.hold(gw[1]), 2)
+    wo = dp_reduce(list(run.hold(add(wo[0], wo_far))))
+    run.end(total, gw_far, wo)
+
+    total = shift(add(total, pick(run.hold(tail), mod(z - 3, nz))), "ctx", 1)
+    gw = dp_reduce(list(run.hold(add(gw[0], gw_far))))
+    run.end(total, gw)
+
+    mine = jnp.concatenate(run.hold([gw, wo]), axis=2)
+    parts = [pick(mine, z)] + [shift(pick(mine, mod(z + k, nz)), "ctx", k) for k in range(1, nz)]
+
+    gn = pick(tail, z).astype(F32) + total.astype(F32)
+    expert_sum = sum_o[0].astype(F32) + far_o.astype(F32) + other_o.astype(F32)
+    mixed_out = (middle + residual_scale * expert_sum).astype(BF)
+    q_end, k_end, v_end = qw, qw + kw, qw + 2 * kw
+    gains = sum(p[:, v_end : v_end + 2].astype(F32) for p in parts)
+    grad_out = sum(p[:, v_end + 128 :].astype(F32) for p in parts)
+    order = jnp.stack([p[:, :v_end] for p in parts])
+    order = [pick(order, mod(z - p, nz)).astype(F32) for p in range(nz)]
+    grad_query = jnp.concatenate([g[:, :q_end] for g in order], axis=1)
+    grad_key = jnp.concatenate([g[:, q_end:k_end] for g in order], axis=1)
+    grad_value = jnp.concatenate([g[:, k_end:] for g in order], axis=1)
+
+    grads_in, grads_down = whole(
+        [
+            (x_0[0], z_0, swap[0]), (x_1[0], z_1, swap[1]), (x_2[0], z_2, swap[2]), (x_3[0], z_3, swap_3)
+        ],
+        odd,
+        devices,
     )
-    run.end(grad_normed, grad_w, wo)
-
-    tail = run.hold(grad_normed)
-    feed = hop(pick(tail, 3 - z), INNER)
-    z_3 = flip(run.hold(x_3)[1], "ctx", 2)
-    far_o = flip_e(run.hold(sum_o[2 * rows :]), 2)
-    gw_core = flip_e(run.hold(grad_w[2:]), 1)
-    run.end(feed, z_3, far_o, gw_core)
-
-    across = hop(run.hold(add(pick(tail, jnp.bitwise_xor(z, 2)), feed)), ACROSS)
-    below = hop(run.hold(pick(tail, jnp.minimum(z + 1, 3))), UP)
-    above = hop(run.hold(pick(tail, jnp.maximum(z - 1, 0))), DOWN)
-    mine = add(grad_w[0], gw_core[0])
-    mine = add(mine, flip_e(run.hold(add(grad_w[1], gw_core[1])), 2))
-    mine = dp_reduce(list(mine))
-    other_o = flip(run.hold(add(sum_o[rows : 2 * rows], far_o[rows:])), "ctx", 1)
-    run.end(across, below, above, mine, other_o)
-
-    swap_2, swap_3 = swap(*run.hold([x_2, z_2])), swap(*run.hold([x_3, z_3]))
-    mine, wo = run.hold(mine), run.hold(wo)
-    parts = [pick(mine, z)] + [shift(pick(mine, mod(z + k, nz)), "ctx", k) for k in range(1, nz)]
-    outs = [pick(wo, z)] + [shift(pick(wo, mod(z + k, nz)), "ctx", k) for k in range(1, nz)]
-    grad_out = sum(t.astype(F32) for t in outs)
-
-    gn = pick(tail, z).astype(F32) + below.astype(F32) + above.astype(F32) + across.astype(F32)
-    expert_sum = sum_o[:rows].astype(F32) + far_o[:rows].astype(F32) + other_o.astype(F32)
-    mixed_out = (middle + residual_scale * expert_sum).astype(BF)
-    gains = sum(p[:, qw + 2 * kw : qw + 2 * kw + 2].astype(F32) for p in parts)
-    order = jnp.stack(parts)
-    order = [pick(order, mod(z - p, nz)).astype(F32) for p in range(nz)]
-    grad_query = jnp.concatenate([g[:, :qw] for g in order], axis=1)
-    grad_key = jnp.concatenate([g[:, qw : qw + kw] for g in order], axis=1)
-    grad_value = jnp.concatenate([g[:, qw + kw : qw + 2 * kw] for g in order], axis=1)
-
-    grads = [
-        whole(own[0], other, theirs, odd, devices)
-        for own, other, theirs in (
-            (x_0, z_0, swap_0), (x_1, z_1, swap_1), (x_2, z_2, swap_2), (x_3, z_3, swap_3)
-        )
-    ]
-    grads_in = jnp.stack([g[0] for g in grads])
-    grads_down = jnp.stack([g[1] for g in grads])
 
     t = tok.astype(F32)
     inv = rms(t)

time: 658 us -> 596 us (0.906)
  local copies, waits for them, and re-layouts: 57.2 us -> 30.2 us
  waiting for transfers between devices: 231 us -> 207 us
  starting transfers between devices: 92.5 us -> 84.3 us
  Pallas kernels: 206 us -> 198 us
    ppermute x8 -> x4, waiting for transfers between devices: 57.7 us -> 7.25 us  [hop(): return lax.ppermute(x, 'ctx', pairs)]
    ppermute x45 -> x44, waiting for transfers between devices: 109 us -> 127 us  [flip(): return lax.ppermute(x, axis, [(i, i ^ mask) for i in range(n)])]
    ppermute x8 -> x4, starting transfers between devices: 21.9 us -> 7.02 us  [hop(): return lax.ppermute(x, 'ctx', pairs)]
    ppermute x45 -> x44, starting transfers between devices: 27 us -> 37.1 us  [flip(): return lax.ppermute(x, axis, [(i, i ^ mask) for i in range(n)])]
    ppermute x32, waiting for transfers between devices: 64.5 us -> 72.7 us  [shift(): return lax.ppermute(x, axis, [(i, (i + by) % n) for i in range(n)])]
    slice x15, local copies, waits for them, and re-layouts: 10.9 us -> 3.62 us  [the longest x4 3.44 us: per_device(): packet = lambda e, got: jnp.stack([mine_in[e], got[e % batch], down[e]])]
    ppermute x3 -> x0, local copies, waits for them, and re-layouts: 6.92 us -> none  [the longest x2 3.63 us: shift(): return lax.ppermute(x, axis, [(i, (i + by) % n) for i in range(n)])]
    convert_element_type x21 -> x23, other arithmetic: 31.6 us -> 36.1 us  [the longest x22 36 us: add(): return (a.astype(F32) + b.astype(F32)).astype(BF)]
  transfers between devices with their start and end apart: 85 -> 80, of which waited for: 32 -> 35; matrix products, arithmetic and copies ran while one was open for 15% -> 14% of each run, Pallas kernels for 29% -> 34%
where the time goes in v2:
time: 596 us; the launch traced here: 589 us
  waiting for transfers between devices  207 us (35%)
  Pallas kernels  198 us (33%)
  starting transfers between devices  84.3 us (14%)
  other arithmetic  67.7 us (11%)
  local copies, waits for them, and re-layouts  30.2 us (5%)
    ppermute x44, waiting for transfers between devices, flip(): return lax.ppermute(x, axis, [(i, i ^ mask) for i in range(n)])  127 us
    ppermute x32, waiting for transfers between devices, shift(): return lax.ppermute(x, axis, [(i, (i + by) % n) for i in range(n)])  72.7 us
    pallas_call x2, Pallas kernels, experts_rows(): pl.pallas_call(body, grid=(tiles,), out_shape=sum_shapes + (jax.ShapeDtyp...  59.2 us
    ppermute x32, starting transfers between devices, shift(): return lax.ppermute(x, axis, [(i, (i + by) % n) for i in range(n)])  40.2 us
    ppermute x44, starting transfers between devices, flip(): return lax.ppermute(x, axis, [(i, i ^ mask) for i in range(n)])  37.1 us
    convert_element_type x22, other arithmetic, add(): return (a.astype(F32) + b.astype(F32)).astype(BF)  36 us
    pallas_call x2, Pallas kernels, experts_weights(): pl.pallas_call(body, out_shape=[jax.ShapeDtypeStruct((2, 3, r, width), BF...  31.8 us
    pallas_call x1, Pallas kernels, attend_back(): pl.pallas_call(body, out_shape=jax.ShapeDtypeStruct((span, width), BF), i...  22.6 us
  transfers between devices with their start and end apart: 80, of which 35 were waited for; matrix products, arithmetic and copies ran while one was open for 14% of the time, Pallas kernels for 34%

profile of v2, /device:TPU:0, one launch (start us, length us, event | category | flops | bytes accessed | tf_op | source)
XLA Modules:
  0.0 589.0 jit_solution(5914392555281166998)
XLA Ops:
  16.7 13.9 %collective-permute-done.3.refs_1_ = bf16[256,1536]{1,0:T(8,128)(2,1)S(1)} collective-permute-done((bf16[256,1536]{1,0:T(8,128)(2,1)S(1)}, bf16[256,1536]{1,0:T(8,128)(2,1)S(1)}, u32[]{:S(2)}, u32[]{:S(2)}) %collective-permute-start.3) | collective-permute-done | bytes 786464 | tf_op jit(solution)/shard_map/ppermute | solution.py:49
  60.0 7.2 %collective-permute-done.11 = bf16[48,1536]{1,0:T(8,128)(2,1)} collective-permute-done((bf16[48,1536]{1,0:T(8,128)(2,1)}, bf16[48,1536]{1,0:T(8,128)(2,1)}, u32[]{:S(2)}, u32[]{:S(2)}) %collective-permute-start.11) | collective-permute-done | bytes 147488 | tf_op jit(solution)/shard_map/ppermute | solution.py:78
  85.5 5.7 project.2
  108.0 14.6 %attend.1 = (bf16[4,256,384]{2,1,0:T(8,128)(2,1)}, f32[8,1024]{1,0:T(8,128)}) custom-call(s32[8]{0:T(128)} %concatenate.42.s_ref, bf16[256,640]{1,0:T(8,128)(2,1)} %get-tuple-element.197.refs_0_, bf16[256,640]{1,0:T(8,128)(2,1)} %get-tuple-element.198.refs_1_, bf16[256,640]{1,0:T(8,128)(2,1)} %get-tuple-element.199.refs_2_, bf16[256,640]{1,0:T(8,128)(2,1)} %project.3.refs_3_), custom_call_target="tpu_custom_call" | custom-call | flops 1342177280 | bytes 873813 | tf_op jit(solution)/shard_map/attend/pallas_call | solution.py:287
  137.6 5.7 assemble.3.refs_4_.w_ref
  143.3 9.9 %collective-permute-done.23.refs_2_ = bf16[256,384]{1,0:T(8,128)(2,1)} collective-permute-done((bf16[256,384]{1,0:T(8,128)(2,1)}, bf16[256,384]{1,0:T(8,128)(2,1)}, u32[]{:S(2)}, u32[]{:S(2)}) %collective-permute-start.23) | collective-permute-done | bytes 196640 | tf_op jit(solution)/shard_map/ppermute | solution.py:49
  155.5 6.2 %join.1 = (f32[256,1536]{1,0:T(8,128)}, bf16[256,1536]{1,0:T(8,128)(2,1)}) custom-call(s32[8]{0:T(128)} %concatenate.42.s_ref, bf16[256,384]{1,0:T(8,128)(2,1)} %get-tuple-element.221.refs_0_, bf16[256,384]{1,0:T(8,128)(2,1)} %collective-permute-done.22.refs_1_, bf16[256,384]{1,0:T(8,128)(2,1)} %collective-permute-done.23.refs_2_, ...), custom_call_target="tpu_custom_call" | custom-call | flops 402653184 | bytes 2883584 | tf_op jit(solution)/shard_map/join/pallas_call | solution.py:408
  173.5 27.6 %collective-permute-done.35 = bf16[3,192,512]{2,1,0:T(8,128)(2,1)S(1)} collective-permute-done((bf16[3,192,512]{2,1,0:T(8,128)(2,1)S(1)}, bf16[3,192,512]{2,1,0:T(8,128)(2,1)S(1)}, u32[]{:S(2)}, u32[]{:S(2)}) %collective-permute-start.35) | collective-permute-done | bytes 589856 | tf_op jit(solution)/shard_map/ppermute | solution.py:54
  209.4 25.9 %collective-permute-done.41.refs_18_ = bf16[3,192,512]{2,1,0:T(8,128)(2,1)S(1)} collective-permute-done((bf16[3,192,512]{2,1,0:T(8,128)(2,1)S(1)}, bf16[3,192,512]{2,1,0:T(8,128)(2,1)S(1)}, u32[]{:S(2)}, u32[]{:S(2)}) %collective-permute-start.41) | collective-permute-done | bytes 589856 | tf_op jit(solution)/shard_map/ppermute | solution.py:54
  240.4 27.8 %experts_rows.2 = (bf16[2048,1536]{1,0:T(8,128)(2,1)}, bf16[2048,1536]{1,0:T(8,128)(2,1)}, bf16[2048,1024]{1,0:T(8,128)(2,1)}, bf16[512,2048]{1,0:T(8,128)(2,1)}, bf16[1536,2048]{1,0:T(8,128)(2,1)}) custom-call(s32[13]{0:T(128)} %stack.518.places_ref, bf16[256,1536]{1,0:T(8,128)(2,1)} %get-tuple-element.263.refs_0_, bf16[256,1536]{1,0:T(8,128)(2,1)} %copy-done.57, ...), custom_call_target="tpu_custom_call" | custom-call | flops 6442450944 | bytes 16666666 | tf_op jit(solution)/shard_map/experts_rows/pallas_call | solution.py:706
  270.4 15.9 %experts_weights.2 = (bf16[2,3,192,512]{3,2,1,0:T(8,128)(2,1)}, bf16[2,3,192,512]{3,2,1,0:T(8,128)(2,1)}, bf16[2,3,192,512]{3,2,1,0:T(8,128)(2,1)}, bf16[2,3,192,512]{3,2,1,0:T(8,128)(2,1)}) custom-call(s32[4]{0:T(128)} %pad_add_fusion.1.s_ref.here_ref, bf16[1536,2048]{1,0:T(8,128)(2,1)} %get-tuple-element.254.h_any, ...), custom_call_target="tpu_custom_call" | custom-call | flops 3221225472 | bytes 6666666 | tf_op jit(solution)/shard_map/experts_weights/pallas_call | solution.py:790
  287.2 31.4 %experts_rows.3 = (bf16[1024,1536]{1,0:T(8,128)(2,1)}, bf16[1024,1536]{1,0:T(8,128)(2,1)}, bf16[1024,1536]{1,0:T(8,128)(2,1)}, bf16[1024,1536]{1,0:T(8,128)(2,1)...) custom-call(s32[13]{0:T(128)} %stack.518.places_ref, bf16[256,1536]{1,0:T(8,128)(2,1)} %get-tuple-element.263.refs_0_, ...), custom_call_target="tpu_custom_call" | custom-call | flops 6442450944 | bytes 16666666 | tf_op jit(solution)/shard_map/experts_rows/pallas_call | solution.py:706
  319.9 5.9 collective-permute-done.47
  333.2 15.9 %experts_weights.3 = (bf16[2,3,192,512]{3,2,1,0:T(8,128)(2,1)}, bf16[2,3,192,512]{3,2,1,0:T(8,128)(2,1)}, bf16[2,3,192,512]{3,2,1,0:T(8,128)(2,1)}, bf16[2,3,192,512]{3,2,1,0:T(8,128)(2,1)}) custom-call(s32[4]{0:T(128)} %pad_add_fusion.1.s_ref.here_ref, bf16[1536,2048]{1,0:T(8,128)(2,1)} %get-tuple-element.254.h_any, ...), custom_call_target="tpu_custom_call" | custom-call | flops 3221225472 | bytes 6666666 | tf_op jit(solution)/shard_map/experts_weights/pallas_call | solution.py:790
  368.2 15.4 %collective-permute-done.56 = bf16[2,3,192,512]{3,2,1,0:T(8,128)(2,1)S(1)} collective-permute-done((bf16[2,3,192,512]{3,2,1,0:T(8,128)(2,1)S(1)}, bf16[2,3,192,512]{3,2,1,0:T(8,128)(2,1)S(1)}, u32[]{:S(2)}, u32[]{:S(2)}) %collective-permute-start.56) | collective-permute-done | bytes 1179680 | tf_op jit(solution)/shard_map/ppermute | solution.py:49
  394.2 8.1 %join_back.1 = (f32[256,1536]{1,0:T(8,128)}, bf16[4,256,384]{2,1,0:T(8,128)(2,1)}, bf16[256,1536]{1,0:T(8,128)(2,1)}, f32[1,1536]{1,0:T(1,128)}) custom-call(s32[8]{0:T(128)} %concatenate.42.s_ref, bf16[256,1536]{1,0:T(8,128)(2,1)} %add_convert_fusion.4.a_ref, bf16[256,1536]{1,0:T(8,128)(2,1)} %copy-done.61, bf16[256,1536]{1,0:T(8,128)(2,1)} %copy-done.60, ...), custom_call_target="tpu_custom_call" | custom-call | flops 402653184 | bytes 3932160 | tf_op jit(solution)/shard_map/join_back/pallas_call | solution.py:439
  409.8 6.4 %join_weights.1 = (bf16[2,2,4,48,1536]{4,3,2,1,0:T(8,128)(2,1)}, bf16[2,2,4,48,1536]{4,3,2,1,0:T(8,128)(2,1)}) custom-call(s32[8]{0:T(128)} %concatenate.42.s_ref, s32[4]{0:T(128)} %pad_add_fusion.1.s_ref.here_ref, bf16[256,1536]{1,0:T(8,128)(2,1)} %get-tuple-element.307.br_ref, bf16[256,384]{1,0:T(8,128)(2,1)} %get-tuple-element.221.refs_0_, ...), custom_call_target="tpu_custom_call" | custom-call | flops 402653184 | bytes 2097152 | tf_op jit(solution)/shard_map/join_weights/pallas_call | solution.py:474
  429.5 22.6 %attend_back.1.dq_ref = bf16[1024,640]{1,0:T(8,128)(2,1)} custom-call(s32[8]{0:T(128)} %concatenate.42.s_ref, bf16[256,640]{1,0:T(8,128)(2,1)} %get-tuple-element.197.refs_0_, bf16[256,640]{1,0:T(8,128)(2,1)} %get-tuple-element.198.refs_1_, bf16[256,640]{1,0:T(8,128)(2,1)} %get-tuple-element.199.refs_2_, bf16[256,640]{1,0:T(8,128)(2,1)} %project.3.refs_3_, ...), custom_call_target="tpu_custom_call" | custom-call | flops 3355443200 | bytes 1747626 | tf_op jit(solution)/shard_map/attend_back/pallas_call | solution.py:370
  452.1 6.3 %finish.1.gn_ref = bf16[4,256,1536]{2,1,0:T(8,128)(2,1)} custom-call(bf16[1024,640]{1,0:T(8,128)(2,1)} %attend_back.1.dq_ref, bf16[1536,640]{1,0:T(8,128)(2,1)} %assemble.2.w_ref), custom_call_target="tpu_custom_call" | custom-call | flops 671088640 | bytes 2097152 | tf_op jit(solution)/shard_map/finish/pallas_call | solution.py:821
  465.5 9.2 %finish_weights.1 = (bf16[2,2,4,48,768]{4,3,2,1,0:T(8,128)(2,1)}, bf16[2,2,4,48,768]{4,3,2,1,0:T(8,128)(2,1)}) custom-call(s32[8]{0:T(128)} %concatenate.42.s_ref, s32[4]{0:T(128)} %pad_add_fusion.1.s_ref.here_ref, bf16[1024,640]{1,0:T(8,128)(2,1)} %attend_back.1.dq_ref, bf16[4,256,1536]{2,1,0:T(8,128)(2,1)} %finish.1.gn_ref, ...), custom_call_target="tpu_custom_call" | custom-call | flops 671088640 | bytes 3145728 | tf_op jit(solution)/shard_map/finish_weights/pallas_call | solution.py:860
  478.5 10.4 %collective-permute-done.66 = bf16[3,192,512]{2,1,0:T(8,128)(2,1)} collective-permute-done((bf16[3,192,512]{2,1,0:T(8,128)(2,1)}, bf16[3,192,512]{2,1,0:T(8,128)(2,1)}, u32[]{:S(2)}, u32[]{:S(2)}) %collective-permute-start.66) | collective-permute-done | bytes 589856 | tf_op jit(solution)/shard_map/ppermute | solution.py:54
  503.4 19.6 %collective-permute-done.71.their_ref = bf16[192,512]{1,0:T(8,128)(2,1)S(1)} collective-permute-done((bf16[192,512]{1,0:T(8,128)(2,1)S(1)}, bf16[192,512]{1,0:T(8,128)(2,1)S(1)}, u32[]{:S(2)}, u32[]{:S(2)}) %collective-permute-start.71) | collective-permute-done | bytes 196640 | tf_op jit(solution)/shard_map/ppermute | solution.py:54
  528.2 9.7 %collective-permute-done.73 = bf16[2,4,48,768]{3,2,1,0:T(8,128)(2,1)} collective-permute-done((bf16[2,4,48,768]{3,2,1,0:T(8,128)(2,1)}, bf16[2,4,48,768]{3,2,1,0:T(8,128)(2,1)}, u32[]{:S(2)}, u32[]{:S(2)}) %collective-permute-start.73) | collective-permute-done | bytes 589856 | tf_op jit(solution)/shard_map/ppermute | solution.py:54
  542.1 5.9 collective-permute-done.72
  (431 shorter events, 259.5 us)
Async XLA Ops:
  100.9 31.1 %collective-permute-start.19 = (bf16[2,3,192,512]{3,2,1,0:T(8,128)(2,1)}, bf16[2,3,192,512]{3,2,1,0:T(8,128)(2,1)}, u32[]{:S(2)}, u32[]{:S(2)}) collective-permute-start(bf16[2,3,192,512]{3,2,1,0:T(8,128)(2,1)} %pad_maximum_fusion.1.refs_16_), channel_id=1, source_target_pairs={{0,16},{16,0},{1,17},{17,1},{2,18},{18,2},{3,19},{19,3},{4,20},{20... | collective-permute-start | bytes 3538952 | tf_op jit(solution)/shard_map/ppermute | solution.py:49
  102.4 29.6 %collective-permute-start.21 = (bf16[256,1664]{1,0:T(8,128)(2,1)S(1)}, bf16[256,1664]{1,0:T(8,128)(2,1)}, u32[]{:S(2)}, u32[]{:S(2)}) collective-permute-start(bf16[256,1664]{1,0:T(8,128)(2,1)S(1)} %pad_maximum_fusion.5.refs_8_.refs_0_), channel_id=1, source_target_pairs={{0,4},{4,0},{8,12},{12,8},{1,5},{5,1},{9,13},{13,9},{2,6},{6,2},{1... | collective-permute-start | bytes 2555912 | tf_op jit(solution)/shard_map/ppermute | solution.py:54
  168.9 33.9 %collective-permute-start.36 = (bf16[2,3,192,512]{3,2,1,0:T(8,128)(2,1)S(1)}, bf16[2,3,192,512]{3,2,1,0:T(8,128)(2,1)S(1)}, u32[]{:S(2)}, u32[]{:S(2)}) collective-permute-start(bf16[2,3,192,512]{3,2,1,0:T(8,128)(2,1)S(1)} %pad_maximum_fusion.3.refs_16_), channel_id=1, source_target_pairs={{0,16},{16,0},{1,17},{17,1},{2,18},{18,2},{3,19},{19,3},{4,20},{20... | collective-permute-start | bytes 3538952 | tf_op jit(solution)/shard_map/ppermute | solution.py:49
  169.4 32.9 %collective-permute-start.32 = (bf16[256,1536]{1,0:T(8,128)(2,1)S(1)}, bf16[256,1536]{1,0:T(8,128)(2,1)S(1)}, u32[]{:S(2)}, u32[]{:S(2)}) collective-permute-start(bf16[256,1536]{1,0:T(8,128)(2,1)S(1)} %copy-done.54), channel_id=1, source_target_pairs={{0,1},{1,0},{2,3},{3,2},{4,5},{5,4},{6,7},{7,6},{8,9},{9,8},{10,11... | collective-permute-start | bytes 2359304 | tf_op jit(solution)/shard_map/ppermute | solution.py:54
  169.4 32.9 %collective-permute-start.33 = (bf16[256,1536]{1,0:T(8,128)(2,1)S(1)}, bf16[256,1536]{1,0:T(8,128)(2,1)S(1)}, u32[]{:S(2)}, u32[]{:S(2)}) collective-permute-start(bf16[256,1536]{1,0:T(8,128)(2,1)S(1)} %copy-done.54), channel_id=1, source_target_pairs={{0,2},{1,3},{2,0},{3,1},{4,6},{5,7},{6,4},{7,5},{8,10},{9,11},{10,... | collective-permute-start | bytes 2359304 | tf_op jit(solution)/shard_map/ppermute | solution.py:54
  170.5 32.3 %collective-permute-start.34 = (bf16[256,1536]{1,0:T(8,128)(2,1)S(1)}, bf16[256,1536]{1,0:T(8,128)(2,1)S(1)}, u32[]{:S(2)}, u32[]{:S(2)}) collective-permute-start(bf16[256,1536]{1,0:T(8,128)(2,1)S(1)} %copy-done.54), channel_id=1, source_target_pairs={{0,4},{4,0},{8,12},{12,8},{1,5},{5,1},{9,13},{13,9},{2,6},{6,2},{1... | collective-permute-start | bytes 2359304 | tf_op jit(solution)/shard_map/ppermute | solution.py:54
  171.3 29.8 %collective-permute-start.35 = (bf16[3,192,512]{2,1,0:T(8,128)(2,1)S(1)}, bf16[3,192,512]{2,1,0:T(8,128)(2,1)S(1)}, u32[]{:S(2)}, u32[]{:S(2)}) collective-permute-start(bf16[3,192,512]{2,1,0:T(8,128)(2,1)S(1)} %copy-done.62), channel_id=1, source_target_pairs={{0,8},{4,12},{8,0},{12,4},{1,9},{5,13},{9,1},{13,5},{2,10},{6,14},... | collective-permute-start | bytes 1769480 | tf_op jit(solution)/shard_map/ppermute | solution.py:54
  204.1 31.3 %collective-permute-start.40 = (bf16[2,3,192,512]{3,2,1,0:T(8,128)(2,1)S(1)}, bf16[2,3,192,512]{3,2,1,0:T(8,128)(2,1)S(1)}, u32[]{:S(2)}, u32[]{:S(2)}) collective-permute-start(bf16[2,3,192,512]{3,2,1,0:T(8,128)(2,1)S(1)} %pad_maximum_fusion.4.refs_18_), channel_id=1, source_target_pairs={{0,16},{16,0},{1,17},{17,1},{2,18},{18,2},{3,19},{19,3},{4,20},{20... | collective-permute-start | bytes 3538952 | tf_op jit(solution)/shard_map/ppermute | solution.py:49
  205.0 30.4 %collective-permute-start.38 = (bf16[256,1536]{1,0:T(8,128)(2,1)S(1)}, bf16[256,1536]{1,0:T(8,128)(2,1)S(1)}, u32[]{:S(2)}, u32[]{:S(2)}) collective-permute-start(bf16[256,1536]{1,0:T(8,128)(2,1)S(1)} %collective-permute-done.33.refs_2_), channel_id=1, source_target_pairs={{0,1},{1,0},{2,3},{3,2},{4,5},{5,4},{6,7},{7,6},{8,9},{9,8},{10,11... | collective-permute-start | bytes 2359304 | tf_op jit(solution)/shard_map/ppermute | solution.py:54
  205.0 30.4 %collective-permute-start.37 = (bf16[256,1536]{1,0:T(8,128)(2,1)S(1)}, bf16[256,1536]{1,0:T(8,128)(2,1)S(1)}, u32[]{:S(2)}, u32[]{:S(2)}) collective-permute-start(bf16[256,1536]{1,0:T(8,128)(2,1)S(1)} %collective-permute-done.34.refs_1_), channel_id=1, source_target_pairs={{0,1},{1,0},{2,3},{3,2},{4,5},{5,4},{6,7},{7,6},{8,9},{9,8},{10,11... | collective-permute-start | bytes 2359304 | tf_op jit(solution)/shard_map/ppermute | solution.py:54
  205.5 29.9 %collective-permute-start.39 = (bf16[256,1536]{1,0:T(8,128)(2,1)S(1)}, bf16[256,1536]{1,0:T(8,128)(2,1)}, u32[]{:S(2)}, u32[]{:S(2)}) collective-permute-start(bf16[256,1536]{1,0:T(8,128)(2,1)S(1)} %collective-permute-done.34.refs_1_), channel_id=1, source_target_pairs={{0,2},{1,3},{2,0},{3,1},{4,6},{5,7},{6,4},{7,5},{8,10},{9,11},{10,... | collective-permute-start | bytes 2359304 | tf_op jit(solution)/shard_map/ppermute | solution.py:54
  206.9 28.5 %collective-permute-start.41 = (bf16[3,192,512]{2,1,0:T(8,128)(2,1)S(1)}, bf16[3,192,512]{2,1,0:T(8,128)(2,1)S(1)}, u32[]{:S(2)}, u32[]{:S(2)}) collective-permute-start(bf16[3,192,512]{2,1,0:T(8,128)(2,1)S(1)} %get-tuple-element.240), channel_id=1, source_target_pairs={{0,8},{4,12},{8,0},{12,4},{1,9},{5,13},{9,1},{13,5},{2,10},{6,14},... | collective-permute-start | bytes 1769480 | tf_op jit(solution)/shard_map/ppermute | solution.py:54
  238.5 29.8 %collective-permute-start.43 = (bf16[3,192,512]{2,1,0:T(8,128)(2,1)}, bf16[3,192,512]{2,1,0:T(8,128)(2,1)}, u32[]{:S(2)}, u32[]{:S(2)}) collective-permute-start(bf16[3,192,512]{2,1,0:T(8,128)(2,1)} %copy-done.63), channel_id=1, source_target_pairs={{0,16},{16,0},{1,17},{17,1},{2,18},{18,2},{3,19},{19,3},{4,20},{20... | collective-permute-start | bytes 1769480 | tf_op jit(solution)/shard_map/ppermute | solution.py:49
  239.3 29.3 %collective-permute-start.42 = (bf16[3,192,512]{2,1,0:T(8,128)(2,1)}, bf16[3,192,512]{2,1,0:T(8,128)(2,1)}, u32[]{:S(2)}, u32[]{:S(2)}) collective-permute-start(bf16[3,192,512]{2,1,0:T(8,128)(2,1)} %get-tuple-element.243), channel_id=1, source_target_pairs={{0,8},{4,12},{8,0},{12,4},{1,9},{5,13},{9,1},{13,5},{2,10},{6,14},... | collective-permute-start | bytes 1769480 | tf_op jit(solution)/shard_map/ppermute | solution.py:54
  286.3 32.4 %collective-permute-start.46 = (bf16[2,3,192,512]{3,2,1,0:T(8,128)(2,1)}, bf16[2,3,192,512]{3,2,1,0:T(8,128)(2,1)S(1)}, u32[]{:S(2)}, u32[]{:S(2)}) collective-permute-start(bf16[2,3,192,512]{3,2,1,0:T(8,128)(2,1)} %get-tuple-element.274), channel_id=1, source_target_pairs={{0,16},{16,0},{1,17},{17,1},{2,18},{18,2},{3,19},{19,3},{4,20},{20... | collective-permute-start | bytes 3538952 | tf_op jit(solution)/shard_map/ppermute | solution.py:49
  325.8 30.5 %collective-permute-start.48 = (bf16[1024,1536]{1,0:T(8,128)(2,1)}, bf16[1024,1536]{1,0:T(8,128)(2,1)}, u32[]{:S(2)}, u32[]{:S(2)}) collective-permute-start(bf16[1024,1536]{1,0:T(8,128)(2,1)} %get-tuple-element.281), channel_id=1, source_target_pairs={{0,1},{1,0},{2,3},{3,2},{4,5},{5,4},{6,7},{7,6},{8,9},{9,8},{10,11... | collective-permute-start | bytes 9437192 | tf_op jit(solution)/shard_map/ppermute | solution.py:54
  325.9 28.6 %collective-permute-start.52 = (bf16[2,3,192,512]{3,2,1,0:T(8,128)(2,1)}, bf16[2,3,192,512]{3,2,1,0:T(8,128)(2,1)}, u32[]{:S(2)}, u32[]{:S(2)}) collective-permute-start(bf16[2,3,192,512]{3,2,1,0:T(8,128)(2,1)} %get-tuple-element.285), channel_id=1, source_target_pairs={{0,16},{16,0},{1,17},{17,1},{2,18},{18,2},{3,19},{19,3},{4,20},{20... | collective-permute-start | bytes 3538952 | tf_op jit(solution)/shard_map/ppermute | solution.py:49
  327.1 29.2 %collective-permute-start.51 = (bf16[3,192,512]{2,1,0:T(8,128)(2,1)}, bf16[3,192,512]{2,1,0:T(8,128)(2,1)}, u32[]{:S(2)}, u32[]{:S(2)}) collective-permute-start(bf16[3,192,512]{2,1,0:T(8,128)(2,1)} %get-tuple-element.284), channel_id=1, source_target_pairs={{0,8},{4,12},{8,0},{12,4},{1,9},{5,13},{9,1},{13,5},{2,10},{6,14},... | collective-permute-start | bytes 1769480 | tf_op jit(solution)/shard_map/ppermute | solution.py:54
  360.1 29.6 %collective-permute-start.54 = (bf16[256,1536]{1,0:T(8,128)(2,1)S(1)}, bf16[256,1536]{1,0:T(8,128)(2,1)S(1)}, u32[]{:S(2)}, u32[]{:S(2)}) collective-permute-start(bf16[256,1536]{1,0:T(8,128)(2,1)S(1)} %pad_maximum_fusion.8), channel_id=1, source_target_pairs={{0,4},{4,0},{8,12},{12,8},{1,5},{5,1},{9,13},{13,9},{2,6},{6,2},{1... | collective-permute-start | bytes 2359304 | tf_op jit(solution)/shard_map/ppermute | solution.py:54
  390.5 33.4 %collective-permute-start.61 = (bf16[256,1536]{1,0:T(8,128)(2,1)}, bf16[256,1536]{1,0:T(8,128)(2,1)}, u32[]{:S(2)}, u32[]{:S(2)}) collective-permute-start(bf16[256,1536]{1,0:T(8,128)(2,1)} %get-tuple-element.306), channel_id=1, source_target_pairs={{0,2},{1,3},{2,0},{3,1},{4,6},{5,7},{6,4},{7,5},{8,10},{9,11},{10,... | collective-permute-start | bytes 2359304 | tf_op jit(solution)/shard_map/ppermute | solution.py:54
  423.9 35.6 %collective-permute-start.65 = (bf16[2,2,4,48,1536]{4,3,2,1,0:T(8,128)(2,1)}, bf16[2,2,4,48,1536]{4,3,2,1,0:T(8,128)(2,1)}, u32[]{:S(2)}, u32[]{:S(2)}) collective-permute-start(bf16[2,2,4,48,1536]{4,3,2,1,0:T(8,128)(2,1)} %get-tuple-element.319), channel_id=1, source_target_pairs={{0,1},{1,0},{2,3},{3,2},{4,5},{5,4},{6,7},{7,6},{8,9},{9,8},{10,11... | collective-permute-start | bytes 7077896 | tf_op jit(solution)/shard_map/ppermute | solution.py:54
  423.9 34.5 %collective-permute-start.62 = (bf16[256,1536]{1,0:T(8,128)(2,1)}, bf16[256,1536]{1,0:T(8,128)(2,1)S(1)}, u32[]{:S(2)}, u32[]{:S(2)}) collective-permute-start(bf16[256,1536]{1,0:T(8,128)(2,1)} %get-tuple-element.310), channel_id=1, source_target_pairs={{0,2},{1,3},{2,0},{3,1},{4,6},{5,7},{6,4},{7,5},{8,10},{9,11},{10,... | collective-permute-start | bytes 2359304 | tf_op jit(solution)/shard_map/ppermute | solution.py:54
  427.0 32.5 %collective-permute-start.63 = (bf16[256,1536]{1,0:T(8,128)(2,1)}, bf16[256,1536]{1,0:T(8,128)(2,1)S(1)}, u32[]{:S(2)}, u32[]{:S(2)}) collective-permute-start(bf16[256,1536]{1,0:T(8,128)(2,1)} %add_convert_fusion.3), channel_id=1, source_target_pairs={{0,4},{4,0},{8,12},{12,8},{1,5},{5,1},{9,13},{13,9},{2,6},{6,2},{1... | collective-permute-start | bytes 2359304 | tf_op jit(solution)/shard_map/ppermute | solution.py:54
  427.5 31.0 %collective-permute-start.64 = (bf16[3,192,512]{2,1,0:T(8,128)(2,1)}, bf16[3,192,512]{2,1,0:T(8,128)(2,1)S(1)}, u32[]{:S(2)}, u32[]{:S(2)}) collective-permute-start(bf16[3,192,512]{2,1,0:T(8,128)(2,1)} %get-tuple-element.318), channel_id=1, source_target_pairs={{0,8},{4,12},{8,0},{12,4},{1,9},{5,13},{9,1},{13,5},{2,10},{6,14},... | collective-permute-start | bytes 1769480 | tf_op jit(solution)/shard_map/ppermute | solution.py:54
  (134 other events, 2207.0 us)

commit v3 on v2

--- a/solution.py
+++ b/solution.py
@@ -245,7 +245,7 @@
     share = heads // kvs
 
     def body(s_ref, *refs):
-        ins, (out_ref, lse_ref, qs, kd, vd, vt, ob) = refs[:blocks], refs[blocks:]
+        ins, outs, (lse_ref, qs, kd, vd, vt, ob) = refs[:blocks], refs[blocks : 2 * blocks], refs[2 * blocks :]
         me = s_ref[4]
         for k in range(blocks):
             at = pl.ds(pl.multiple_of(s_ref[k] * rows, rows), rows)
@@ -273,25 +273,26 @@
                 lse_ref[pl.ds(h, 1), p * rows : (p + 1) * rows] = peak + jnp.log(total)
             return 0
 
-        lax.fori_loop(0, heads, one, 0)
+        def some(i, _):
+            for u in range(share):
+                one(i * share + u, 0)
+            return 0
+
+        lax.fori_loop(0, kvs, some, 0)
         low = lower_half((rows, 128))
-        for p in range(blocks):
-            to = lax.rem(p - me + blocks, blocks)
+        for k in range(blocks):
+            at = pl.ds(pl.multiple_of(lax.rem(me + k, blocks) * rows, rows), rows)
             for b in range(heads // 2):
-                at = slice(p * rows, (p + 1) * rows)
-                out_ref[to, :, b * 128 : (b + 1) * 128] = jnp.where(
+                outs[k][:, b * 128 : (b + 1) * 128] = jnp.where(
                     low, ob[2 * b, at, :], ob[2 * b + 1, at, :]
                 ).astype(BF)
 
     pairs = heads * rows * rows * blocks * (blocks + 1) // 2
-    return pl.pallas_call(
+    *mixes, lse = pl.pallas_call(
         body,
-        out_shape=(
-            jax.ShapeDtypeStruct((blocks, rows, qw), BF),
-            jax.ShapeDtypeStruct((8, span), F32),
-        ),
+        out_shape=[jax.ShapeDtypeStruct((rows, qw), BF)] * blocks + [jax.ShapeDtypeStruct((8, span), F32)],
         in_specs=[SM] + [VM] * blocks,
-        out_specs=(VM, VM),
+        out_specs=[VM] * (blocks + 1),
         scratch_shapes=[
             pltpu.VMEM((heads, span, 128), BF),
             pltpu.VMEM((kvs, span, 128), BF),
@@ -303,6 +304,7 @@
         cost_estimate=cost(pairs * 1024, 4 * span * width, pairs),
         name="attend",
     )(scalars, *pieces)
+    return mixes, lse
 
 
 def attend_back(scalars, pieces, grads, lse, cos, sin, heads, kvs):
@@ -352,7 +354,8 @@
                 dv[kv, :keys, :] += mm(chances.astype(BF), g)
             return 0
 
-        lax.fori_loop(0, heads, one, 0)
+        for h in range(heads):
+            one(h, 0)
         low = lower_half((rows, 128))
         for p in range(blocks):
             at = slice(p * rows, (p + 1) * rows)
@@ -420,10 +423,12 @@
     blocks = 4
     rows, d = middle.shape
     part = d // blocks
-
-    def body(s_ref, a_ref, b_ref, c_ref, mid_ref, cot_ref, gain_ref, w_ref, gmid_ref, gmix_ref, br_ref, gg_ref):
+    count = len(addends)
+
+    def body(s_ref, *refs):
+        ins, (mid_ref, cot_ref, gain_ref, w_ref, gmid_ref, br_ref, gg_ref, *outs) = refs[:count], refs[count:]
         me = s_ref[4]
-        grad_hidden = a_ref[...].astype(F32) + b_ref[...].astype(F32) + c_ref[...].astype(F32)
+        grad_hidden = sum(t[...].astype(F32) for t in ins)
         middle = mid_ref[...]
         inv = rms(middle)
         normal = middle * inv
@@ -434,22 +439,28 @@
         br_ref[...] = (residual_scale * grad_middle).astype(BF)
         for k in range(blocks):
             at = pl.ds(pl.multiple_of(lax.rem(me - k + blocks, blocks) * part, part), part)
-            gmix_ref[k] = mm(br_ref[...], w_ref[at, :], NT).astype(BF)
-
-    return pl.pallas_call(
+            outs[k][...] = mm(br_ref[...], w_ref[at, :], NT).astype(BF)
+
+    front = lambda t: pl.BlockSpec((rows, d), lambda i: (0, 0))
+    fixed = lambda *shape: pl.BlockSpec(shape, lambda i: (0, 0))
+    grad_middle, branch, gain_grad, *mixes = pl.pallas_call(
         body,
-        out_shape=(
+        grid=(1,),
+        out_shape=[
             jax.ShapeDtypeStruct((rows, d), F32),
-            jax.ShapeDtypeStruct((blocks, rows, part), BF),
             jax.ShapeDtypeStruct((rows, d), BF),
             jax.ShapeDtypeStruct((1, d), F32),
-        ),
-        in_specs=[SM] + [VM] * 7,
-        out_specs=(VM, VM, VM, VM),
+        ]
+        + [jax.ShapeDtypeStruct((rows, part), BF)] * blocks,
+        in_specs=[SM]
+        + [front(t) for t in addends]
+        + [fixed(rows, d), fixed(rows, d), fixed(1, d), fixed(d, d)],
+        out_specs=[fixed(rows, d), fixed(rows, d), fixed(1, d)] + [fixed(rows, part)] * blocks,
         compiler_params=params(),
         cost_estimate=cost(2 * rows * d * d, 2 * d * d + 18 * rows * d),
         name="join_back",
     )(scalars, *addends, middle, cot, gain, w_out)
+    return grad_middle, mixes, branch, gain_grad
 
 
 def join_weights(scalars, here, branch, mixes, nd, ne):
@@ -577,7 +588,7 @@
 
 def experts_rows(places, which, rows_in, cots, shards, sums, last):
     piece, d = rows_in[0].shape
-    group = 2
+    group = 1
     rows = piece * group
     tiles = len(rows_in) // group
     total = rows * tiles
@@ -625,12 +636,12 @@
                     parts = []
                     for b in range(2):
                         at = pl.multiple_of(places_ref[3 * i + b] * r, r)
-                        parts.append((source.at[b], wiv.at[pl.ds(at, r), e * width : (e + 1) * width]))
+                        parts.append((source.at[2 * b], wiv.at[pl.ds(at, r), e * width : (e + 1) * width]))
                     at = pl.multiple_of(places_ref[3 * i + 2] * r3 + e * half, r3)
                     for b in range(3):
                         parts.append(
                             (
-                                source.at[2, b * r3 : (b + 1) * r3, :],
+                                source.at[1, b * r3 : (b + 1) * r3, :],
                                 wdv.at[pl.ds(at, r3), b * width : (b + 1) * width],
                             )
                         )
@@ -810,24 +821,26 @@
     return [outs[e * nd : (e + 1) * nd] for e in range(n)]
 
 
-def finish(dqkv, w, blocks):
+def finish(scalars, dqkv, w, blocks):
     total, width = dqkv.shape
     d = w.shape[0]
     rows = total // blocks
 
-    def body(dq_ref, w_ref, gn_ref):
-        gn_ref[0] = mm(dq_ref[...], w_ref[...], NT).astype(BF)
+    def body(s_ref, dq_ref, w_ref, *outs):
+        for k in range(blocks):
+            at = lax.rem(s_ref[4] - 1 - k + 2 * blocks, blocks)
+            at = pl.ds(pl.multiple_of(at * rows, rows), rows)
+            outs[k][...] = mm(dq_ref[at, :], w_ref[...], NT).astype(BF)
 
     return pl.pallas_call(
         body,
-        grid=(blocks,),
-        out_shape=jax.ShapeDtypeStruct((blocks, rows, d), BF),
-        in_specs=[pl.BlockSpec((rows, width), lambda t: (t, 0)), pl.BlockSpec((d, width), lambda t: (0, 0))],
-        out_specs=pl.BlockSpec((1, rows, d), lambda t: (t, 0, 0)),
+        out_shape=[jax.ShapeDtypeStruct((rows, d), BF)] * blocks,
+        in_specs=[SM, VM, VM],
+        out_specs=[VM] * blocks,
         compiler_params=params(),
         cost_estimate=cost(2 * total * d * width, 4 * total * d),
         name="finish",
-    )(dqkv, w)
+    )(scalars, dqkv, w)
 
 
 def finish_weights(scalars, here, dqkv, gn, toks, gain, gain_grad, nd, ne):
@@ -836,8 +849,8 @@
     width = dqkv.shape[1]
     w_rows = d // (nd * blocks * ne)
 
-    def body(s_ref, here_ref, dq_ref, gn_ref, gain_ref, gg_ref, *refs):
-        ins, (gwa_ref, gwb_ref, acc) = refs[:blocks], refs[blocks:]
+    def body(s_ref, here_ref, dq_ref, gain_ref, gg_ref, *refs):
+        ins, gns, (gwa_ref, gwb_ref, acc) = refs[:blocks], refs[blocks : 2 * blocks], refs[2 * blocks :]
         gg = jnp.zeros((1, d), F32)
         for k in range(blocks):
             to = s_ref[k]
@@ -845,7 +858,8 @@
             t = ins[k][...].astype(F32)
             normal = t * rms(t)
             normed = (normal * gain_ref[...]).astype(BF)
-            gg = gg + jnp.sum(gn_ref[to].astype(F32) * normal, axis=0, keepdims=True)
+            gn = gns[(k - 1) % blocks][...].astype(F32)
+            gg = gg + jnp.sum(gn * normal, axis=0, keepdims=True)
             part = mm(normed, dq_ref[at, :], TN)
             acc[...] = part if k == 0 else acc[...] + part
         row = lax.broadcasted_iota(jnp.int32, (128, d), 0)
@@ -860,13 +874,13 @@
     return pl.pallas_call(
         body,
         out_shape=(jax.ShapeDtypeStruct((2, nd, blocks, w_rows, width + 128), BF),) * 2,
-        in_specs=[SM, SM] + [VM] * (4 + blocks),
+        in_specs=[SM, SM] + [VM] * (3 + 2 * blocks),
         out_specs=(VM, VM),
         scratch_shapes=[pltpu.VMEM((d, width), F32)],
         compiler_params=params(),
         cost_estimate=cost(2 * blocks * rows * d * width, 6 * blocks * rows * d),
         name="finish_weights",
-    )(scalars, here, dqkv, gn, gain, gain_grad, *toks)
+    )(scalars, here, dqkv, gain, gain_grad, *toks, *gn)
 
 
 def per_device(
@@ -973,7 +987,7 @@
     pieces = project(toks[: nz - 1], gain_a, w_qkv, cos, sin, at[: nz - 1])
     run.end(toks, pieces, got_1, w_line, cot_2)
 
-    packet = lambda e, got: jnp.stack([mine_in[e], got[e % batch], down[e]])
+    packet = lambda e, got: jnp.stack([mine_in[e], down[e], got[e % batch]])
     near = [packet(e, got_1) for e in range(batch)]
     far = [flip(run.hold(near[0]), "ctx", 2)]
     own = [ring(run.hold(jnp.stack(near)), "dp")]
@@ -984,34 +998,36 @@
     mix_out, lse = attend(scalars, pieces, heads, kvs)
     run.end(far, own, w_line, cot_n, mix_out)
 
-    mixes = run.hold([mix_out[k] for k in range(nz)])
+    mixes = run.hold(mix_out)
     mixes = [mixes[0]] + [shift(mixes[k], "ctx", k) for k in range(1, nz)]
     w_line = [w_line, flip_e(run.hold(w_line), 1)]
     cot_n2 = flip_e(run.hold(cot_n), 2)
     w_out_all = row_blocks(w_line, line_places(z), by_b)
     run.end(mixes, w_out_all, cot_n2)
 
-    cot_1, cot_3 = flip_e(run.hold(cot_b), 1), flip_e(run.hold(cot_2), 1)
+    cot_1 = flip_e(run.hold(cot_b), 1)
     cot_n1, cot_n3 = flip_e(run.hold(cot_n), 1), flip_e(run.hold(cot_n2), 1)
     got_2 = flip(run.hold(their_in[batch:]), "ctx", 1)
+    over = [ring(run.hold(far[0]), "dp")]
     middle, hidden = join(scalars, run.hold(mixes), w_out_all, tok, gain_m)
-    run.end(hidden, got_2, cot_1, cot_3, cot_n1, cot_n3)
+    run.end(hidden, got_2, over, cot_1, cot_n1, cot_n3)
 
     hidden_2, hidden_n = flip_e(run.hold(hidden), 2), flip(run.hold(hidden), "ctx", 1)
     far += [flip(run.hold(near[e]), "ctx", 2) for e in range(1, batch)]
-    near += [packet(e, got_2) for e in range(batch, local_experts)]
-    own.append(ring(run.hold(jnp.stack(near[batch:])), "dp"))
+    near.append(packet(batch, got_2))
+    own.append(ring(run.hold(near[batch]), "dp"))
     hidden_1 = flip_e(run.hold(hidden), 1)
     run.end(hidden_1, hidden_2, hidden_n, far, own)
 
     hidden_n2 = flip_e(run.hold(hidden_n), 2)
     hidden_n1, hidden_3 = flip_e(run.hold(hidden_n), 1), flip_e(run.hold(hidden_2), 1)
-    over = [ring(run.hold(jnp.stack(far)), "dp")]
+    over += [ring(run.hold(far[e]), "dp") for e in range(1, batch)]
     far.append(flip(run.hold(near[batch]), "ctx", 2))
-    run.end(hidden_n1, hidden_3, hidden_n2, over, far)
+    near += [packet(e, run.hold(got_2)) for e in range(batch + 1, local_experts)]
+    run.end(hidden_n1, hidden_3, hidden_n2, over, far, near)
 
     rows_in = [hidden, hidden_n, hidden_2, hidden_n2, hidden_1, hidden_n1, hidden_3, None]
-    cots = [cot_b, cot_n, cot_2, cot_n2, cot_1, cot_n1, cot_3, cot_n3]
+    cots = [cot_b, cot_n, cot_2, cot_n2, cot_1, cot_n1, None, cot_n3]
     w_at = []
     for zc in (z, jnp.bitwise_xor(z, 2)):
         for m in range(nd):
@@ -1019,19 +1035,22 @@
             w_at += [xc * nz + zc, xc * nz + jnp.bitwise_xor(zc, 1), xc * 2 + zc // 2]
     w_at = jnp.stack(w_at + [j * local_experts]).astype(i32)
     rows_in = run.hold(rows_in[:-1]) + [flip_e(run.hold(hidden_n2), 1)]
+    cots[6] = flip_e(run.hold(cot_2), 1)
+    own += [ring(run.hold(near[e]), "dp") for e in range(batch + 1, local_experts)]
     far += [flip(run.hold(near[e]), "ctx", 2) for e in range(batch + 1, local_experts)]
     over.append(ring(run.hold(far[batch]), "dp"))
-    shards = [[(t, e) for e in range(batch)] for t in own[0] + over[0]]
+    shards = [[(t, e) for e in range(batch)] for t in own[0]]
+    shards += [[(t, None) for t in some] for some in zip(*over[:batch])]
     sum_h, sum_o, gb, ga_t, rows_t = experts_rows(w_at, 0, rows_in, cots, shards, None, False)
-    run.end(far, over, sum_h)
+    run.end(far, own, over, sum_h)
 
     over += [ring(run.hold(far[e]), "dp") for e in range(batch + 1, local_experts)]
     gw_1 = experts_weights(here, rows_t, cots, run.hold(gb), ga_t, batch, devices)
     run.end(over, gw_1)
 
     x_0 = dp_reduce_pair(run.hold(gw_1[0]))
-    shards = [[(t, e) for e in range(batch)] for t in own[1]]
-    shards += [[(t, None) for t in pair] for pair in zip(*over[1:])]
+    shards = [[(t, None) for t in some] for some in zip(*own[1:])]
+    shards += [[(t, None) for t in some] for some in zip(*over[batch:])]
     sum_h, rest_h, sum_o, rest_o, gb, ga_t = experts_rows(
         w_at, batch, run.hold(rows_in), cots, shards, (sum_h, sum_o), True
     )
@@ -1041,69 +1060,74 @@
     run.end(rest_h)
 
     part = rows // 2
+    all_h = sum_h
     sum_h = [
         add(sum_h[a * part : b * part], rest_h[a * part : b * part])
-        for a, b in ((0, 2), (2, 3), (3, 4), (4, 5), (5, 6), (6, 7), (7, 8))
+        for a, b in ((2, 3), (3, 4), (4, 5), (5, 6), (6, 7), (7, 8))
     ]
-    by_y, by_z = flip_e(run.hold(sum_h[5]), 2), flip(run.hold(sum_h[6]), "ctx", 1)
+    by_y, by_z = flip_e(run.hold(sum_h[4]), 2), flip(run.hold(sum_h[5]), "ctx", 1)
     z_0 = flip(run.hold(x_0[1]), "ctx", 2)
     x_1 = dp_reduce_pair(run.hold(gw_1[1]))
     rest_o = flip_e(run.hold(rest_o), 1)
     gw_2 = experts_weights(here, rows_t, cots, run.hold(gb), ga_t, batch, devices)
     run.end(by_y, by_z, z_0, x_1, rest_o, gw_2)
 
-    near_h = flip_e(jnp.concatenate([sum_h[3], add(run.hold(sum_h[4]), by_z)]), 2)
-    other_h = flip(jnp.concatenate([add(run.hold(sum_h[1]), by_y), sum_h[2]]), "ctx", 1)
+    near_h = flip_e(jnp.concatenate([sum_h[2], add(run.hold(sum_h[3]), by_z)]), 2)
+    other_h = flip(jnp.concatenate([add(run.hold(sum_h[0]), by_y), sum_h[1]]), "ctx", 1)
     z_1 = flip(run.hold(x_1[1]), "ctx", 2)
     x_2 = dp_reduce_pair(run.hold(gw_2[0]))
     sum_o = [add(sum_o[a * rows : (a + 1) * rows], rest_o[a * rows : (a + 1) * rows]) for a in range(4)]
     run.end(near_h, other_h, z_1, x_2, sum_o)
 
     grad_middle, grad_mix, branch, grad_gain_m = join_back(
-        scalars, [sum_h[0], *run.hold([near_h, other_h])], middle, cot, gain_m, w_out_all
+        scalars, [all_h, rest_h, *run.hold([near_h, other_h])], middle, cot, gain_m, w_out_all
     )
     grad_mixes = [grad_mix[0]] + [shift(grad_mix[k], "ctx", -k) for k in range(1, nz)]
     x_3 = dp_reduce_pair(run.hold(gw_2[1]))
     far_o1 = flip_e(run.hold(sum_o[3]), 2)
     wo_a, wo_b = join_weights(scalars, here, branch, mixes, nd, ne)
-    run.end(grad_mixes, x_3, far_o1, wo_b)
+    ready = lax.optimization_barrier((x_0[0], x_1[0], branch))
+    swap = jnp.stack([add(ready[0][1], z_0[1]), add(ready[1][1], z_1[1])])
+    run.end(grad_mixes, x_3, far_o1, wo_b, swap)
 
     z_2 = flip(run.hold(x_2[1]), "ctx", 2)
     far_o = flip_e(run.hold(sum_o[2]), 2)
     other_o = flip(add(sum_o[1], run.hold(far_o1)), "ctx", 1)
     wo_b = flip_e(run.hold(wo_b), 1)
     dqkv = attend_back(scalars, pieces, run.hold(grad_mixes), lse, cos, sin, heads, kvs)
-    grad_normed = finish(dqkv, w_qkv, nz)
+    grad_normed = finish(scalars, dqkv, w_qkv, nz)
     run.end(z_2, far_o, other_o, wo_b, grad_normed)
 
     z_3 = flip(run.hold(x_3[1]), "ctx", 2)
     gw_a, gw_b = finish_weights(scalars, here, dqkv, run.hold(grad_normed), toks, gain_a, grad_gain_m, nd, ne)
-    x_held = run.hold([x_0[0], x_1[0], x_2[0]])
-    swap = flip(jnp.stack([add(t[1], u[1]) for t, u in zip(x_held, (z_0, z_1, z_2))]), "ctx", 1)
-    wo = add(wo_a, lax.optimization_barrier((wo_b, gw_b))[0])
-    run.end(gw_b, swap, wo, z_3)
+    swap = flip(run.hold(swap), "ctx", 1)
+    swap_2 = flip(add(run.hold(x_2[0])[1], z_2[1]), "ctx", 1)
+    wo_b = run.hold(wo_b)
+    wo_far = flip_e(add(wo_a[1], wo_b[1]), 2)
+    run.end(gw_b, swap, swap_2, wo_far, z_3)
 
     tail = run.hold(grad_normed)
-    total = shift(pick(tail, mod(z - 1, nz)), "ctx", 1)
+    total = shift(tail[0], "ctx", 1)
     gw_b = flip_e(run.hold(gw_b), 1)
-    wo_far = flip_e(run.hold(wo[1]), 2)
     swap_3 = flip(add(run.hold(x_3[0])[1], z_3[1]), "ctx", 1)
     gw = add(gw_a, gw_b)
-    run.end(total, gw, wo_far, swap_3)
-
-    total = shift(add(total, pick(run.hold(tail), mod(z - 2, nz))), "ctx", 1)
+    run.end(total, gw, swap_3)
+
+    total = shift(add(run.hold(total), tail[1]), "ctx", 1)
     gw_far = flip_e(run.hold(gw[1]), 2)
-    wo = dp_reduce(list(run.hold(add(wo[0], wo_far))))
+    wo_b, wo_far = run.hold([wo_b, wo_far])
+    wo = (wo_a[0].astype(F32) + wo_b[0].astype(F32) + wo_far.astype(F32)).astype(BF)
+    wo = dp_reduce(list(wo))
     run.end(total, gw_far, wo)
 
-    total = shift(add(total, pick(run.hold(tail), mod(z - 3, nz))), "ctx", 1)
+    total = shift(add(run.hold(total), tail[2]), "ctx", 1)
     gw = dp_reduce(list(run.hold(add(gw[0], gw_far))))
     run.end(total, gw)
 
     mine = jnp.concatenate(run.hold([gw, wo]), axis=2)
     parts = [pick(mine, z)] + [shift(pick(mine, mod(z + k, nz)), "ctx", k) for k in range(1, nz)]
 
-    gn = pick(tail, z).astype(F32) + total.astype(F32)
+    gn = tail[3].astype(F32) + total.astype(F32)
     expert_sum = sum_o[0].astype(F32) + far_o.astype(F32) + other_o.astype(F32)
     mixed_out = (middle + residual_scale * expert_sum).astype(BF)
     q_end, k_end, v_end = qw, qw + kw, qw + 2 * kw
@@ -1117,7 +1141,7 @@
 
     grads_in, grads_down = whole(
         [
-            (x_0[0], z_0, swap[0]), (x_1[0], z_1, swap[1]), (x_2[0], z_2, swap[2]), (x_3[0], z_3, swap_3)
+            (x_0[0], z_0, swap[0]), (x_1[0], z_1, swap[1]), (x_2[0], z_2, swap_2), (x_3[0], z_3, swap_3)
         ],
         odd,
         devices,

time: 596 us -> 588 us (0.987)
  waiting for transfers between devices: 207 us -> 223 us
  other arithmetic: 67.7 us -> 56.1 us
  Pallas kernels: 198 us -> 191 us
    ppermute x32 -> x34, waiting for transfers between devices: 72.7 us -> 97.7 us  [shift(): return lax.ppermute(x, axis, [(i, (i + by) % n) for i in range(n)])]
    convert_element_type x22 -> x20, other arithmetic: 36 us -> 27.2 us  [add(): return (a.astype(F32) + b.astype(F32)).astype(BF)]
    ppermute x44 -> x45, waiting for transfers between devices: 127 us -> 118 us  [flip(): return lax.ppermute(x, axis, [(i, i ^ mask) for i in range(n)])]
    ppermute x44 -> x45, starting transfers between devices: 37.1 us -> 35 us  [flip(): return lax.ppermute(x, axis, [(i, i ^ mask) for i in range(n)])]
    ppermute x32 -> x34, starting transfers between devices: 40.2 us -> 41.2 us  [shift(): return lax.ppermute(x, axis, [(i, (i + by) % n) for i in range(n)])]
  transfers between devices with their start and end apart: 80 -> 83, of which waited for: 35 -> 36; matrix products, arithmetic and copies ran while one was open for 14% -> 11% of each run, Pallas kernels for 34% -> 33%
where the time goes in v3:
time: 588 us; the launch traced here: 582 us
  waiting for transfers between devices  223 us (38%)
  Pallas kernels  191 us (32%)
  starting transfers between devices  83.2 us (14%)
  other arithmetic  56.1 us (10%)
  local copies, waits for them, and re-layouts  25.5 us (4%)
    ppermute x45, waiting for transfers between devices, flip(): return lax.ppermute(x, axis, [(i, i ^ mask) for i in range(n)])  118 us
    ppermute x34, waiting for transfers between devices, shift(): return lax.ppermute(x, axis, [(i, (i + by) % n) for i in range(n)])  97.7 us
    pallas_call x2, Pallas kernels, experts_rows(): pl.pallas_call(body, grid=(tiles,), out_shape=sum_shapes + (jax.ShapeDtyp...  57.4 us
    ppermute x34, starting transfers between devices, shift(): return lax.ppermute(x, axis, [(i, (i + by) % n) for i in range(n)])  41.2 us
    ppermute x45, starting transfers between devices, flip(): return lax.ppermute(x, axis, [(i, i ^ mask) for i in range(n)])  35 us
    pallas_call x2, Pallas kernels, experts_weights(): pl.pallas_call(body, out_shape=[jax.ShapeDtypeStruct((2, 3, r, width), BF...  31.8 us
    convert_element_type x20, other arithmetic, add(): return (a.astype(F32) + b.astype(F32)).astype(BF)  27.2 us
    pallas_call x1, Pallas kernels, attend_back(): pl.pallas_call(body, out_shape=jax.ShapeDtypeStruct((span, width), BF), i...  20.3 us
  transfers between devices with their start and end apart: 83, of which 36 were waited for; matrix products, arithmetic and copies ran while one was open for 11% of the time, Pallas kernels for 33%

profile of v3, /device:TPU:0, one launch (start us, length us, event | category | flops | bytes accessed | tf_op | source)
XLA Modules:
  0.0 581.7 jit_solution(12875650818691048066)
XLA Ops:
  16.7 13.9 %collective-permute-done.3.refs_1_ = bf16[256,1536]{1,0:T(8,128)(2,1)S(1)} collective-permute-done((bf16[256,1536]{1,0:T(8,128)(2,1)S(1)}, bf16[256,1536]{1,0:T(8,128)(2,1)S(1)}, u32[]{:S(2)}, u32[]{:S(2)}) %collective-permute-start.3) | collective-permute-done | bytes 786464 | tf_op jit(solution)/shard_map/ppermute | solution.py:49
  60.0 7.2 %collective-permute-done.11 = bf16[48,1536]{1,0:T(8,128)(2,1)} collective-permute-done((bf16[48,1536]{1,0:T(8,128)(2,1)}, bf16[48,1536]{1,0:T(8,128)(2,1)}, u32[]{:S(2)}, u32[]{:S(2)}) %collective-permute-start.11) | collective-permute-done | bytes 147488 | tf_op jit(solution)/shard_map/ppermute | solution.py:78
  108.1 13.3 %attend.1 = (bf16[256,384]{1,0:T(8,128)(2,1)}, bf16[256,384]{1,0:T(8,128)(2,1)}, bf16[256,384]{1,0:T(8,128)(2,1)}, bf16[256,384]{1,0:T(8,128)(2,1)}, f32[8,1024]{1,0:T(8,128)}) custom-call(s32[8]{0:T(128)} %concatenate.42.s_ref, bf16[256,640]{1,0:T(8,128)(2,1)} %get-tuple-element.216.refs_0_, bf16[256,640]{1,0:T(8,128)(2,1)} %get-tuple-element.217.refs_1_, ...), custom_call_target="tpu_custom_call" | custom-call | flops 1342177280 | bytes 873813 | tf_op jit(solution)/shard_map/attend/pallas_call | solution.py:291
  123.3 6.4 %collective-permute-done.18.refs_18_ = bf16[3,192,512]{2,1,0:T(8,128)(2,1)} collective-permute-done((bf16[3,192,512]{2,1,0:T(8,128)(2,1)}, bf16[3,192,512]{2,1,0:T(8,128)(2,1)}, u32[]{:S(2)}, u32[]{:S(2)}) %collective-permute-start.18) | collective-permute-done | bytes 589856 | tf_op jit(solution)/shard_map/ppermute | solution.py:54
  142.4 9.8 %collective-permute-done.23.refs_2_ = bf16[256,384]{1,0:T(8,128)(2,1)} collective-permute-done((bf16[256,384]{1,0:T(8,128)(2,1)}, bf16[256,384]{1,0:T(8,128)(2,1)}, u32[]{:S(2)}, u32[]{:S(2)}) %collective-permute-start.23) | collective-permute-done | bytes 196640 | tf_op jit(solution)/shard_map/ppermute | solution.py:49
  155.5 6.2 %join.1 = (f32[256,1536]{1,0:T(8,128)}, bf16[256,1536]{1,0:T(8,128)(2,1)}) custom-call(s32[8]{0:T(128)} %concatenate.42.s_ref, bf16[256,384]{1,0:T(8,128)(2,1)} %get-tuple-element.243.refs_0_, bf16[256,384]{1,0:T(8,128)(2,1)} %collective-permute-done.22.refs_1_, bf16[256,384]{1,0:T(8,128)(2,1)} %collective-permute-done.23.refs_2_, ...), custom_call_target="tpu_custom_call" | custom-call | flops 402653184 | bytes 2883584 | tf_op jit(solution)/shard_map/join/pallas_call | solution.py:411
  176.6 12.8 %collective-permute-done.36.refs_18_ = bf16[3,192,512]{2,1,0:T(8,128)(2,1)S(1)} collective-permute-done((bf16[3,192,512]{2,1,0:T(8,128)(2,1)S(1)}, bf16[3,192,512]{2,1,0:T(8,128)(2,1)S(1)}, u32[]{:S(2)}, u32[]{:S(2)}) %collective-permute-start.36) | collective-permute-done | bytes 589856 | tf_op jit(solution)/shard_map/ppermute | solution.py:49
  189.4 12.9 %collective-permute-done.35.refs_19_ = bf16[3,192,512]{2,1,0:T(8,128)(2,1)S(1)} collective-permute-done((bf16[3,192,512]{2,1,0:T(8,128)(2,1)S(1)}, bf16[3,192,512]{2,1,0:T(8,128)(2,1)S(1)}, u32[]{:S(2)}, u32[]{:S(2)}) %collective-permute-start.35) | collective-permute-done | bytes 589856 | tf_op jit(solution)/shard_map/ppermute | solution.py:54
  210.1 24.7 %collective-permute-done.41.refs_20_ = bf16[3,192,512]{2,1,0:T(8,128)(2,1)S(1)} collective-permute-done((bf16[3,192,512]{2,1,0:T(8,128)(2,1)S(1)}, bf16[3,192,512]{2,1,0:T(8,128)(2,1)S(1)}, u32[]{:S(2)}, u32[]{:S(2)}) %collective-permute-start.41) | collective-permute-done | bytes 589856 | tf_op jit(solution)/shard_map/ppermute | solution.py:54
  240.9 27.3 %experts_rows.2 = (bf16[2048,1536]{1,0:T(8,128)(2,1)}, bf16[2048,1536]{1,0:T(8,128)(2,1)}, bf16[2048,1024]{1,0:T(8,128)(2,1)}, bf16[512,2048]{1,0:T(8,128)(2,1)}, bf16[1536,2048]{1,0:T(8,128)(2,1)}) custom-call(s32[13]{0:T(128)} %stack.499.places_ref, bf16[256,1536]{1,0:T(8,128)(2,1)} %get-tuple-element.287.refs_0_, bf16[256,1536]{1,0:T(8,128)(2,1)} %copy-done.56, ...), custom_call_target="tpu_custom_call" | custom-call | flops 6442450944 | bytes 16666666 | tf_op jit(solution)/shard_map/experts_rows/pallas_call | solution.py:717
  269.5 15.8 %experts_weights.2 = (bf16[2,3,192,512]{3,2,1,0:T(8,128)(2,1)}, bf16[2,3,192,512]{3,2,1,0:T(8,128)(2,1)}, bf16[2,3,192,512]{3,2,1,0:T(8,128)(2,1)}, bf16[2,3,192,512]{3,2,1,0:T(8,128)(2,1)}) custom-call(s32[4]{0:T(128)} %pad_add_fusion.1.s_ref.here_ref, bf16[1536,2048]{1,0:T(8,128)(2,1)} %get-tuple-element.278.h_any, ...), custom_call_target="tpu_custom_call" | custom-call | flops 3221225472 | bytes 6666666 | tf_op jit(solution)/shard_map/experts_weights/pallas_call | solution.py:801
  286.9 30.1 %experts_rows.3 = (bf16[1024,1536]{1,0:T(8,128)(2,1)}, bf16[1024,1536]{1,0:T(8,128)(2,1)}, bf16[1024,1536]{1,0:T(8,128)(2,1)}, bf16[1024,1536]{1,0:T(8,128)(2,1)...) custom-call(s32[13]{0:T(128)} %stack.499.places_ref, bf16[256,1536]{1,0:T(8,128)(2,1)} %get-tuple-element.287.refs_0_, ...), custom_call_target="tpu_custom_call" | custom-call | flops 6442450944 | bytes 16666666 | tf_op jit(solution)/shard_map/experts_rows/pallas_call | solution.py:717
  330.2 15.9 %experts_weights.3 = (bf16[2,3,192,512]{3,2,1,0:T(8,128)(2,1)}, bf16[2,3,192,512]{3,2,1,0:T(8,128)(2,1)}, bf16[2,3,192,512]{3,2,1,0:T(8,128)(2,1)}, bf16[2,3,192,512]{3,2,1,0:T(8,128)(2,1)}) custom-call(s32[4]{0:T(128)} %pad_add_fusion.1.s_ref.here_ref, bf16[1536,2048]{1,0:T(8,128)(2,1)} %get-tuple-element.278.h_any, ...), custom_call_target="tpu_custom_call" | custom-call | flops 3221225472 | bytes 6666666 | tf_op jit(solution)/shard_map/experts_weights/pallas_call | solution.py:801
  346.2 6.7 %collective-permute-done.54 = bf16[2,3,192,512]{3,2,1,0:T(8,128)(2,1)} collective-permute-done((bf16[2,3,192,512]{3,2,1,0:T(8,128)(2,1)}, bf16[2,3,192,512]{3,2,1,0:T(8,128)(2,1)}, u32[]{:S(2)}, u32[]{:S(2)}) %collective-permute-start.54) | collective-permute-done | bytes 1179680 | tf_op jit(solution)/shard_map/ppermute | solution.py:49
  365.4 16.6 %collective-permute-done.58 = bf16[2,3,192,512]{3,2,1,0:T(8,128)(2,1)S(1)} collective-permute-done((bf16[2,3,192,512]{3,2,1,0:T(8,128)(2,1)S(1)}, bf16[2,3,192,512]{3,2,1,0:T(8,128)(2,1)S(1)}, u32[]{:S(2)}, u32[]{:S(2)}) %collective-permute-start.58) | collective-permute-done | bytes 1179680 | tf_op jit(solution)/shard_map/ppermute | solution.py:49
  390.7 8.1 %join_back.1 = (f32[256,1536]{1,0:T(8,128)}, bf16[256,1536]{1,0:T(8,128)(2,1)}, f32[1,1536]{1,0:T(1,128)}, bf16[256,384]{1,0:T(8,128)(2,1)}, bf16[256,384]{1,0:T...) custom-call(s32[8]{0:T(128)} %concatenate.42.s_ref, bf16[1024,1536]{1,0:T(8,128)(2,1)} %get-tuple-element.300.refs_0_, ...), custom_call_target="tpu_custom_call" | custom-call | flops 402653184 | bytes 3932160 | tf_op jit(solution)/shard_map/join_back/pallas_call | solution.py:446
  402.3 6.5 %join_weights.1 = (bf16[2,2,4,48,1536]{4,3,2,1,0:T(8,128)(2,1)}, bf16[2,2,4,48,1536]{4,3,2,1,0:T(8,128)(2,1)}) custom-call(s32[8]{0:T(128)} %concatenate.42.s_ref, s32[4]{0:T(128)} %pad_add_fusion.1.s_ref.here_ref, bf16[256,1536]{1,0:T(8,128)(2,1)} %get-tuple-element.334.br_ref, bf16[256,384]{1,0:T(8,128)(2,1)} %get-tuple-element.243.refs_0_, ...), custom_call_target="tpu_custom_call" | custom-call | flops 402653184 | bytes 2097152 | tf_op jit(solution)/shard_map/join_weights/pallas_call | solution.py:485
  425.2 20.3 %attend_back.1.dq_ref = bf16[1024,640]{1,0:T(8,128)(2,1)} custom-call(s32[8]{0:T(128)} %concatenate.42.s_ref, bf16[256,640]{1,0:T(8,128)(2,1)} %get-tuple-element.216.refs_0_, bf16[256,640]{1,0:T(8,128)(2,1)} %get-tuple-element.217.refs_1_, bf16[256,640]{1,0:T(8,128)(2,1)} %get-tuple-element.218.refs_2_, bf16[256,640]{1,0:T(8,128)(2,1)} %project.3.refs_3_, ...), custom_call_target="tpu_custom_call" | custom-call | flops 3355443200 | bytes 1747626 | tf_op jit(solution)/shard_map/attend_back/pallas_call | solution.py:373
  463.7 9.3 %finish_weights.1 = (bf16[2,2,4,48,768]{4,3,2,1,0:T(8,128)(2,1)}, bf16[2,2,4,48,768]{4,3,2,1,0:T(8,128)(2,1)}) custom-call(s32[8]{0:T(128)} %concatenate.42.s_ref, s32[4]{0:T(128)} %pad_add_fusion.1.s_ref.here_ref, bf16[1024,640]{1,0:T(8,128)(2,1)} %attend_back.1.dq_ref, f32[1,1536]{1,0:T(1,128)} %broadcast_in_dim.59.gain_ref, ...), custom_call_target="tpu_custom_call" | custom-call | flops 671088640 | bytes 3145728 | tf_op jit(solution)/shard_map/finish_weights/pallas_call | solution.py:874
  473.0 12.9 %collective-permute-done.69.their_ref = bf16[192,512]{1,0:T(8,128)(2,1)S(1)} collective-permute-done((bf16[192,512]{1,0:T(8,128)(2,1)}, bf16[192,512]{1,0:T(8,128)(2,1)S(1)}, u32[]{:S(2)}, u32[]{:S(2)}) %collective-permute-start.69) | collective-permute-done | bytes 196640 | tf_op jit(solution)/shard_map/ppermute | solution.py:54
  490.9 21.8 %collective-permute-done.74.their_ref = bf16[192,512]{1,0:T(8,128)(2,1)S(1)} collective-permute-done((bf16[192,512]{1,0:T(8,128)(2,1)S(1)}, bf16[192,512]{1,0:T(8,128)(2,1)S(1)}, u32[]{:S(2)}, u32[]{:S(2)}) %collective-permute-start.74) | collective-permute-done | bytes 196640 | tf_op jit(solution)/shard_map/ppermute | solution.py:54
  519.6 8.4 %collective-permute-done.76 = bf16[2,4,48,768]{3,2,1,0:T(8,128)(2,1)} collective-permute-done((bf16[2,4,48,768]{3,2,1,0:T(8,128)(2,1)}, bf16[2,4,48,768]{3,2,1,0:T(8,128)(2,1)}, u32[]{:S(2)}, u32[]{:S(2)}) %collective-permute-start.76) | collective-permute-done | bytes 589856 | tf_op jit(solution)/shard_map/ppermute | solution.py:54
  555.4 6.4 %collective-permute-done.78 = bf16[256,1536]{1,0:T(8,128)(2,1)S(1)} collective-permute-done((bf16[256,1536]{1,0:T(8,128)(2,1)S(1)}, bf16[256,1536]{1,0:T(8,128)(2,1)S(1)}, u32[]{:S(2)}, u32[]{:S(2)}) %collective-permute-start.78) | collective-permute-done | bytes 786464 | tf_op jit(solution)/shard_map/ppermute | solution.py:49
  568.2 6.9 %collective-permute-done.82 = bf16[48,2304]{1,0:T(8,128)(2,1)S(1)} collective-permute-done((bf16[48,2304]{1,0:T(8,128)(2,1)S(1)}, bf16[48,2304]{1,0:T(8,128)(2,1)S(1)}, u32[]{:S(2)}, u32[]{:S(2)}) %collective-permute-start.82) | collective-permute-done | bytes 221216 | tf_op jit(solution)/shard_map/ppermute | solution.py:49
  (435 shorter events, 259.5 us)
Async XLA Ops:
  100.9 31.1 %collective-permute-start.19 = (bf16[2,3,192,512]{3,2,1,0:T(8,128)(2,1)}, bf16[2,3,192,512]{3,2,1,0:T(8,128)(2,1)}, u32[]{:S(2)}, u32[]{:S(2)}) collective-permute-start(bf16[2,3,192,512]{3,2,1,0:T(8,128)(2,1)} %pad_maximum_fusion.1.refs_16_), channel_id=1, source_target_pairs={{0,16},{16,0},{1,17},{17,1},{2,18},{18,2},{3,19},{19,3},{4,20},{20... | collective-permute-start | bytes 3538952 | tf_op jit(solution)/shard_map/ppermute | solution.py:49
  102.4 29.6 %collective-permute-start.21 = (bf16[256,1664]{1,0:T(8,128)(2,1)S(1)}, bf16[256,1664]{1,0:T(8,128)(2,1)}, u32[]{:S(2)}, u32[]{:S(2)}) collective-permute-start(bf16[256,1664]{1,0:T(8,128)(2,1)S(1)} %pad_maximum_fusion.3.refs_8_.refs_0_), channel_id=1, source_target_pairs={{0,4},{4,0},{8,12},{12,8},{1,5},{5,1},{9,13},{13,9},{2,6},{6,2},{1... | collective-permute-start | bytes 2555912 | tf_op jit(solution)/shard_map/ppermute | solution.py:54
  171.2 31.0 %collective-permute-start.32 = (bf16[256,1536]{1,0:T(8,128)(2,1)}, bf16[256,1536]{1,0:T(8,128)(2,1)S(1)}, u32[]{:S(2)}, u32[]{:S(2)}) collective-permute-start(bf16[256,1536]{1,0:T(8,128)(2,1)} %get-tuple-element.287.refs_0_), channel_id=1, source_target_pairs={{0,1},{1,0},{2,3},{3,2},{4,5},{5,4},{6,7},{7,6},{8,9},{9,8},{10,11... | collective-permute-start | bytes 2359304 | tf_op jit(solution)/shard_map/ppermute | solution.py:54
  171.2 31.0 %collective-permute-start.33 = (bf16[256,1536]{1,0:T(8,128)(2,1)}, bf16[256,1536]{1,0:T(8,128)(2,1)S(1)}, u32[]{:S(2)}, u32[]{:S(2)}) collective-permute-start(bf16[256,1536]{1,0:T(8,128)(2,1)} %get-tuple-element.287.refs_0_), channel_id=1, source_target_pairs={{0,2},{1,3},{2,0},{3,1},{4,6},{5,7},{6,4},{7,5},{8,10},{9,11},{10,... | collective-permute-start | bytes 2359304 | tf_op jit(solution)/shard_map/ppermute | solution.py:54
  171.9 32.5 %collective-permute-start.34 = (bf16[256,1536]{1,0:T(8,128)(2,1)}, bf16[256,1536]{1,0:T(8,128)(2,1)S(1)}, u32[]{:S(2)}, u32[]{:S(2)}) collective-permute-start(bf16[256,1536]{1,0:T(8,128)(2,1)} %get-tuple-element.287.refs_0_), channel_id=1, source_target_pairs={{0,4},{4,0},{8,12},{12,8},{1,5},{5,1},{9,13},{13,9},{2,6},{6,2},{1... | collective-permute-start | bytes 2359304 | tf_op jit(solution)/shard_map/ppermute | solution.py:54
  204.4 30.4 %collective-permute-start.38 = (bf16[256,1536]{1,0:T(8,128)(2,1)S(1)}, bf16[256,1536]{1,0:T(8,128)(2,1)S(1)}, u32[]{:S(2)}, u32[]{:S(2)}) collective-permute-start(bf16[256,1536]{1,0:T(8,128)(2,1)S(1)} %collective-permute-done.33.refs_2_), channel_id=1, source_target_pairs={{0,1},{1,0},{2,3},{3,2},{4,5},{5,4},{6,7},{7,6},{8,9},{9,8},{10,11... | collective-permute-start | bytes 2359304 | tf_op jit(solution)/shard_map/ppermute | solution.py:54
  204.4 30.4 %collective-permute-start.37 = (bf16[256,1536]{1,0:T(8,128)(2,1)S(1)}, bf16[256,1536]{1,0:T(8,128)(2,1)S(1)}, u32[]{:S(2)}, u32[]{:S(2)}) collective-permute-start(bf16[256,1536]{1,0:T(8,128)(2,1)S(1)} %collective-permute-done.34.refs_1_), channel_id=1, source_target_pairs={{0,1},{1,0},{2,3},{3,2},{4,5},{5,4},{6,7},{7,6},{8,9},{9,8},{10,11... | collective-permute-start | bytes 2359304 | tf_op jit(solution)/shard_map/ppermute | solution.py:54
  204.9 29.9 %collective-permute-start.39 = (bf16[256,1536]{1,0:T(8,128)(2,1)S(1)}, bf16[256,1536]{1,0:T(8,128)(2,1)}, u32[]{:S(2)}, u32[]{:S(2)}) collective-permute-start(bf16[256,1536]{1,0:T(8,128)(2,1)S(1)} %collective-permute-done.34.refs_1_), channel_id=1, source_target_pairs={{0,2},{1,3},{2,0},{3,1},{4,6},{5,7},{6,4},{7,5},{8,10},{9,11},{10,... | collective-permute-start | bytes 2359304 | tf_op jit(solution)/shard_map/ppermute | solution.py:54
  206.3 28.5 %collective-permute-start.41 = (bf16[3,192,512]{2,1,0:T(8,128)(2,1)S(1)}, bf16[3,192,512]{2,1,0:T(8,128)(2,1)S(1)}, u32[]{:S(2)}, u32[]{:S(2)}) collective-permute-start(bf16[3,192,512]{2,1,0:T(8,128)(2,1)S(1)} %pad_maximum_fusion.10.refs_16_), channel_id=1, source_target_pairs={{0,8},{4,12},{8,0},{12,4},{1,9},{5,13},{9,1},{13,5},{2,10},{6,14},... | collective-permute-start | bytes 1769480 | tf_op jit(solution)/shard_map/ppermute | solution.py:54
  237.0 31.2 %collective-permute-start.42 = (bf16[3,192,512]{2,1,0:T(8,128)(2,1)}, bf16[3,192,512]{2,1,0:T(8,128)(2,1)}, u32[]{:S(2)}, u32[]{:S(2)}) collective-permute-start(bf16[3,192,512]{2,1,0:T(8,128)(2,1)} %pad_maximum_fusion.11.refs_17_), channel_id=1, source_target_pairs={{0,8},{4,12},{8,0},{12,4},{1,9},{5,13},{9,1},{13,5},{2,10},{6,14},... | collective-permute-start | bytes 1769480 | tf_op jit(solution)/shard_map/ppermute | solution.py:54
  237.0 31.2 %collective-permute-start.43 = (bf16[3,192,512]{2,1,0:T(8,128)(2,1)}, bf16[3,192,512]{2,1,0:T(8,128)(2,1)}, u32[]{:S(2)}, u32[]{:S(2)}) collective-permute-start(bf16[3,192,512]{2,1,0:T(8,128)(2,1)} %pad_maximum_fusion.11.refs_17_), channel_id=1, source_target_pairs={{0,16},{16,0},{1,17},{17,1},{2,18},{18,2},{3,19},{19,3},{4,20},{20... | collective-permute-start | bytes 1769480 | tf_op jit(solution)/shard_map/ppermute | solution.py:49
  237.6 30.7 %collective-permute-start.44 = (bf16[3,192,512]{2,1,0:T(8,128)(2,1)}, bf16[3,192,512]{2,1,0:T(8,128)(2,1)}, u32[]{:S(2)}, u32[]{:S(2)}) collective-permute-start(bf16[3,192,512]{2,1,0:T(8,128)(2,1)} %copy-done.63), channel_id=1, source_target_pairs={{0,16},{16,0},{1,17},{17,1},{2,18},{18,2},{3,19},{19,3},{4,20},{20... | collective-permute-start | bytes 1769480 | tf_op jit(solution)/shard_map/ppermute | solution.py:49
  285.4 31.7 %collective-permute-start.48 = (bf16[2,3,192,512]{3,2,1,0:T(8,128)(2,1)}, bf16[2,3,192,512]{3,2,1,0:T(8,128)(2,1)S(1)}, u32[]{:S(2)}, u32[]{:S(2)}) collective-permute-start(bf16[2,3,192,512]{3,2,1,0:T(8,128)(2,1)} %get-tuple-element.298), channel_id=1, source_target_pairs={{0,16},{16,0},{1,17},{17,1},{2,18},{18,2},{3,19},{19,3},{4,20},{20... | collective-permute-start | bytes 3538952 | tf_op jit(solution)/shard_map/ppermute | solution.py:49
  324.1 30.4 %collective-permute-start.50 = (bf16[1024,1536]{1,0:T(8,128)(2,1)}, bf16[1024,1536]{1,0:T(8,128)(2,1)}, u32[]{:S(2)}, u32[]{:S(2)}) collective-permute-start(bf16[1024,1536]{1,0:T(8,128)(2,1)} %get-tuple-element.305), channel_id=1, source_target_pairs={{0,1},{1,0},{2,3},{3,2},{4,5},{5,4},{6,7},{7,6},{8,9},{9,8},{10,11... | collective-permute-start | bytes 9437192 | tf_op jit(solution)/shard_map/ppermute | solution.py:54
  324.3 28.6 %collective-permute-start.54 = (bf16[2,3,192,512]{3,2,1,0:T(8,128)(2,1)}, bf16[2,3,192,512]{3,2,1,0:T(8,128)(2,1)}, u32[]{:S(2)}, u32[]{:S(2)}) collective-permute-start(bf16[2,3,192,512]{3,2,1,0:T(8,128)(2,1)} %get-tuple-element.309), channel_id=1, source_target_pairs={{0,16},{16,0},{1,17},{17,1},{2,18},{18,2},{3,19},{19,3},{4,20},{20... | collective-permute-start | bytes 3538952 | tf_op jit(solution)/shard_map/ppermute | solution.py:49
  325.0 29.4 %collective-permute-start.53 = (bf16[3,192,512]{2,1,0:T(8,128)(2,1)}, bf16[3,192,512]{2,1,0:T(8,128)(2,1)}, u32[]{:S(2)}, u32[]{:S(2)}) collective-permute-start(bf16[3,192,512]{2,1,0:T(8,128)(2,1)} %get-tuple-element.308), channel_id=1, source_target_pairs={{0,8},{4,12},{8,0},{12,4},{1,9},{5,13},{9,1},{13,5},{2,10},{6,14},... | collective-permute-start | bytes 1769480 | tf_op jit(solution)/shard_map/ppermute | solution.py:54
  359.4 29.8 %collective-permute-start.56 = (bf16[256,1536]{1,0:T(8,128)(2,1)S(1)}, bf16[256,1536]{1,0:T(8,128)(2,1)S(1)}, u32[]{:S(2)}, u32[]{:S(2)}) collective-permute-start(bf16[256,1536]{1,0:T(8,128)(2,1)S(1)} %pad_maximum_fusion.6), channel_id=1, source_target_pairs={{0,4},{4,0},{8,12},{12,8},{1,5},{5,1},{9,13},{13,9},{2,6},{6,2},{1... | collective-permute-start | bytes 2359304 | tf_op jit(solution)/shard_map/ppermute | solution.py:54
  360.7 28.4 %collective-permute-start.55 = (bf16[256,1536]{1,0:T(8,128)(2,1)S(1)}, bf16[256,1536]{1,0:T(8,128)(2,1)}, u32[]{:S(2)}, u32[]{:S(2)}) collective-permute-start(bf16[256,1536]{1,0:T(8,128)(2,1)S(1)} %pad_maximum_fusion.5), channel_id=1, source_target_pairs={{0,2},{1,3},{2,0},{3,1},{4,6},{5,7},{6,4},{7,5},{8,10},{9,11},{10,... | collective-permute-start | bytes 2359304 | tf_op jit(solution)/shard_map/ppermute | solution.py:54
  418.3 36.5 %collective-permute-start.67 = (bf16[2,2,4,48,1536]{4,3,2,1,0:T(8,128)(2,1)}, bf16[2,2,4,48,1536]{4,3,2,1,0:T(8,128)(2,1)}, u32[]{:S(2)}, u32[]{:S(2)}) collective-permute-start(bf16[2,2,4,48,1536]{4,3,2,1,0:T(8,128)(2,1)} %get-tuple-element.349), channel_id=1, source_target_pairs={{0,1},{1,0},{2,3},{3,2},{4,5},{5,4},{6,7},{7,6},{8,9},{9,8},{10,11... | collective-permute-start | bytes 7077896 | tf_op jit(solution)/shard_map/ppermute | solution.py:54
  418.3 35.8 %collective-permute-start.64 = (bf16[256,1536]{1,0:T(8,128)(2,1)}, bf16[256,1536]{1,0:T(8,128)(2,1)S(1)}, u32[]{:S(2)}, u32[]{:S(2)}) collective-permute-start(bf16[256,1536]{1,0:T(8,128)(2,1)} %get-tuple-element.339), channel_id=1, source_target_pairs={{0,2},{1,3},{2,0},{3,1},{4,6},{5,7},{6,4},{7,5},{8,10},{9,11},{10,... | collective-permute-start | bytes 2359304 | tf_op jit(solution)/shard_map/ppermute | solution.py:54
  421.8 33.0 %collective-permute-start.65 = (bf16[256,1536]{1,0:T(8,128)(2,1)}, bf16[256,1536]{1,0:T(8,128)(2,1)S(1)}, u32[]{:S(2)}, u32[]{:S(2)}) collective-permute-start(bf16[256,1536]{1,0:T(8,128)(2,1)} %add_convert_fusion.5), channel_id=1, source_target_pairs={{0,4},{4,0},{8,12},{12,8},{1,5},{5,1},{9,13},{13,9},{2,6},{6,2},{1... | collective-permute-start | bytes 2359304 | tf_op jit(solution)/shard_map/ppermute | solution.py:54
  424.0 30.0 %collective-permute-start.66 = (bf16[3,192,512]{2,1,0:T(8,128)(2,1)S(1)}, bf16[3,192,512]{2,1,0:T(8,128)(2,1)S(1)}, u32[]{:S(2)}, u32[]{:S(2)}) collective-permute-start(bf16[3,192,512]{2,1,0:T(8,128)(2,1)S(1)} %copy-done.61), channel_id=1, source_target_pairs={{0,8},{4,12},{8,0},{12,4},{1,9},{5,13},{9,1},{13,5},{2,10},{6,14},... | collective-permute-start | bytes 1769480 | tf_op jit(solution)/shard_map/ppermute | solution.py:54
  457.6 28.9 %collective-permute-start.70 = (bf16[2,4,48,1536]{3,2,1,0:T(8,128)(2,1)S(1)}, bf16[2,4,48,1536]{3,2,1,0:T(8,128)(2,1)}, u32[]{:S(2)}, u32[]{:S(2)}) collective-permute-start(bf16[2,4,48,1536]{3,2,1,0:T(8,128)(2,1)S(1)} %fusion.9), channel_id=1, source_target_pairs={{0,2},{1,3},{2,0},{3,1},{4,6},{5,7},{6,4},{7,5},{8,10},{9,11},{10,... | collective-permute-start | bytes 3538952 | tf_op jit(solution)/shard_map/ppermute | solution.py:54
  458.0 28.5 %collective-permute-start.71 = (bf16[3,192,512]{2,1,0:T(8,128)(2,1)}, bf16[3,192,512]{2,1,0:T(8,128)(2,1)S(1)}, u32[]{:S(2)}, u32[]{:S(2)}) collective-permute-start(bf16[3,192,512]{2,1,0:T(8,128)(2,1)} %get-tuple-element.364), channel_id=1, source_target_pairs={{0,8},{4,12},{8,0},{12,4},{1,9},{5,13},{9,1},{13,5},{2,10},{6,14},... | collective-permute-start | bytes 1769480 | tf_op jit(solution)/shard_map/ppermute | solution.py:54
  (139 other events, 2381.4 us)

commit v4 on v3

--- a/solution.py
+++ b/solution.py
@@ -1109,21 +1109,22 @@
     tail = run.hold(grad_normed)
     total = shift(tail[0], "ctx", 1)
     gw_b = flip_e(run.hold(gw_b), 1)
-    swap_3 = flip(add(run.hold(x_3[0])[1], z_3[1]), "ctx", 1)
     gw = add(gw_a, gw_b)
-    run.end(total, gw, swap_3)
+    wo_b, wo_far = run.hold([wo_b, wo_far])
+    wo = (wo_a[0].astype(F32) + wo_b[0].astype(F32) + wo_far.astype(F32)).astype(BF)
+    run.end(total, gw, wo)
 
     total = shift(add(run.hold(total), tail[1]), "ctx", 1)
     gw_far = flip_e(run.hold(gw[1]), 2)
-    wo_b, wo_far = run.hold([wo_b, wo_far])
-    wo = (wo_a[0].astype(F32) + wo_b[0].astype(F32) + wo_far.astype(F32)).astype(BF)
-    wo = dp_reduce(list(wo))
-    run.end(total, gw_far, wo)
+    wo = dp_reduce(list(run.hold(wo)))
+    gw = add(gw[0], gw_far)
+    run.end(total, gw, wo)
 
     total = shift(add(run.hold(total), tail[2]), "ctx", 1)
-    gw = dp_reduce(list(run.hold(add(gw[0], gw_far))))
+    gw = dp_reduce(list(run.hold(gw)))
     run.end(total, gw)
 
+    swap_3 = flip(add(run.hold(x_3[0])[1], z_3[1]), "ctx", 1)
     mine = jnp.concatenate(run.hold([gw, wo]), axis=2)
     parts = [pick(mine, z)] + [shift(pick(mine, mod(z + k, nz)), "ctx", k) for k in range(1, nz)]
 

time: 588 us -> 585 us (level)
    ppermute x45, waiting for transfers between devices: 118 us -> 106 us  [flip(): return lax.ppermute(x, axis, [(i, i ^ mask) for i in range(n)])]
    ppermute x34, waiting for transfers between devices: 97.7 us -> 105 us  [shift(): return lax.ppermute(x, axis, [(i, (i + by) % n) for i in range(n)])]
  transfers between devices with their start and end apart: 83 -> 83, of which waited for: 36 -> 35; matrix products, arithmetic and copies ran while one was open for 11% -> 11% of each run, Pallas kernels for 33% -> 33%
where the time goes in v4:
time: 585 us; the launch traced here: 580 us
  waiting for transfers between devices  218 us (37%)
  Pallas kernels  192 us (33%)
  starting transfers between devices  82.9 us (14%)
  other arithmetic  58.9 us (10%)
  local copies, waits for them, and re-layouts  25.9 us (4%)
    ppermute x45, waiting for transfers between devices, flip(): return lax.ppermute(x, axis, [(i, i ^ mask) for i in range(n)])  106 us
    ppermute x34, waiting for transfers between devices, shift(): return lax.ppermute(x, axis, [(i, (i + by) % n) for i in range(n)])  105 us
    pallas_call x2, Pallas kernels, experts_rows(): pl.pallas_call(body, grid=(tiles,), out_shape=sum_shapes + (jax.ShapeDtyp...  57.4 us
    ppermute x34, starting transfers between devices, shift(): return lax.ppermute(x, axis, [(i, (i + by) % n) for i in range(n)])  41.6 us
    ppermute x45, starting transfers between devices, flip(): return lax.ppermute(x, axis, [(i, i ^ mask) for i in range(n)])  34.3 us
    pallas_call x2, Pallas kernels, experts_weights(): pl.pallas_call(body, out_shape=[jax.ShapeDtypeStruct((2, 3, r, width), BF...  31.7 us
    convert_element_type x20, other arithmetic, add(): return (a.astype(F32) + b.astype(F32)).astype(BF)  28.6 us
    pallas_call x1, Pallas kernels, attend_back(): pl.pallas_call(body, out_shape=jax.ShapeDtypeStruct((span, width), BF), i...  20.3 us
  transfers between devices with their start and end apart: 83, of which 35 were waited for; matrix products, arithmetic and copies ran while one was open for 11% of the time, Pallas kernels for 33%

profile of v4, /device:TPU:0, one launch (start us, length us, event | category | flops | bytes accessed | tf_op | source)
XLA Modules:
  0.0 579.6 jit_solution(17405617814414351085)
XLA Ops:
  16.8 13.9 %collective-permute-done.3.refs_1_ = bf16[256,1536]{1,0:T(8,128)(2,1)S(1)} collective-permute-done((bf16[256,1536]{1,0:T(8,128)(2,1)S(1)}, bf16[256,1536]{1,0:T(8,128)(2,1)S(1)}, u32[]{:S(2)}, u32[]{:S(2)}) %collective-permute-start.3) | collective-permute-done | bytes 786464 | tf_op jit(solution)/shard_map/ppermute | solution.py:49
  60.0 7.2 %collective-permute-done.11 = bf16[48,1536]{1,0:T(8,128)(2,1)} collective-permute-done((bf16[48,1536]{1,0:T(8,128)(2,1)}, bf16[48,1536]{1,0:T(8,128)(2,1)}, u32[]{:S(2)}, u32[]{:S(2)}) %collective-permute-start.11) | collective-permute-done | bytes 147488 | tf_op jit(solution)/shard_map/ppermute | solution.py:78
  108.1 13.3 %attend.1 = (bf16[256,384]{1,0:T(8,128)(2,1)}, bf16[256,384]{1,0:T(8,128)(2,1)}, bf16[256,384]{1,0:T(8,128)(2,1)}, bf16[256,384]{1,0:T(8,128)(2,1)}, f32[8,1024]{1,0:T(8,128)}) custom-call(s32[8]{0:T(128)} %concatenate.42.s_ref, bf16[256,640]{1,0:T(8,128)(2,1)} %get-tuple-element.217.refs_0_, bf16[256,640]{1,0:T(8,128)(2,1)} %get-tuple-element.218.refs_1_, ...), custom_call_target="tpu_custom_call" | custom-call | flops 1342177280 | bytes 873813 | tf_op jit(solution)/shard_map/attend/pallas_call | solution.py:291
  123.3 6.5 %collective-permute-done.18.refs_18_ = bf16[3,192,512]{2,1,0:T(8,128)(2,1)} collective-permute-done((bf16[3,192,512]{2,1,0:T(8,128)(2,1)}, bf16[3,192,512]{2,1,0:T(8,128)(2,1)}, u32[]{:S(2)}, u32[]{:S(2)}) %collective-permute-start.18) | collective-permute-done | bytes 589856 | tf_op jit(solution)/shard_map/ppermute | solution.py:54
  142.4 9.8 %collective-permute-done.23.refs_2_ = bf16[256,384]{1,0:T(8,128)(2,1)} collective-permute-done((bf16[256,384]{1,0:T(8,128)(2,1)}, bf16[256,384]{1,0:T(8,128)(2,1)}, u32[]{:S(2)}, u32[]{:S(2)}) %collective-permute-start.23) | collective-permute-done | bytes 196640 | tf_op jit(solution)/shard_map/ppermute | solution.py:49
  155.6 6.2 %join.1 = (f32[256,1536]{1,0:T(8,128)}, bf16[256,1536]{1,0:T(8,128)(2,1)}) custom-call(s32[8]{0:T(128)} %concatenate.42.s_ref, bf16[256,384]{1,0:T(8,128)(2,1)} %get-tuple-element.244.refs_0_, bf16[256,384]{1,0:T(8,128)(2,1)} %collective-permute-done.22.refs_1_, bf16[256,384]{1,0:T(8,128)(2,1)} %collective-permute-done.23.refs_2_, ...), custom_call_target="tpu_custom_call" | custom-call | flops 402653184 | bytes 2883584 | tf_op jit(solution)/shard_map/join/pallas_call | solution.py:411
  176.7 12.7 %collective-permute-done.36.refs_18_ = bf16[3,192,512]{2,1,0:T(8,128)(2,1)S(1)} collective-permute-done((bf16[3,192,512]{2,1,0:T(8,128)(2,1)S(1)}, bf16[3,192,512]{2,1,0:T(8,128)(2,1)S(1)}, u32[]{:S(2)}, u32[]{:S(2)}) %collective-permute-start.36) | collective-permute-done | bytes 589856 | tf_op jit(solution)/shard_map/ppermute | solution.py:49
  189.4 12.9 %collective-permute-done.35.refs_19_ = bf16[3,192,512]{2,1,0:T(8,128)(2,1)S(1)} collective-permute-done((bf16[3,192,512]{2,1,0:T(8,128)(2,1)S(1)}, bf16[3,192,512]{2,1,0:T(8,128)(2,1)S(1)}, u32[]{:S(2)}, u32[]{:S(2)}) %collective-permute-start.35) | collective-permute-done | bytes 589856 | tf_op jit(solution)/shard_map/ppermute | solution.py:54
  210.1 24.7 %collective-permute-done.41.refs_20_ = bf16[3,192,512]{2,1,0:T(8,128)(2,1)S(1)} collective-permute-done((bf16[3,192,512]{2,1,0:T(8,128)(2,1)S(1)}, bf16[3,192,512]{2,1,0:T(8,128)(2,1)S(1)}, u32[]{:S(2)}, u32[]{:S(2)}) %collective-permute-start.41) | collective-permute-done | bytes 589856 | tf_op jit(solution)/shard_map/ppermute | solution.py:54
  240.9 27.3 %experts_rows.2 = (bf16[2048,1536]{1,0:T(8,128)(2,1)}, bf16[2048,1536]{1,0:T(8,128)(2,1)}, bf16[2048,1024]{1,0:T(8,128)(2,1)}, bf16[512,2048]{1,0:T(8,128)(2,1)}, bf16[1536,2048]{1,0:T(8,128)(2,1)}) custom-call(s32[13]{0:T(128)} %stack.499.places_ref, bf16[256,1536]{1,0:T(8,128)(2,1)} %get-tuple-element.288.refs_0_, bf16[256,1536]{1,0:T(8,128)(2,1)} %copy-done.52, ...), custom_call_target="tpu_custom_call" | custom-call | flops 6442450944 | bytes 16666666 | tf_op jit(solution)/shard_map/experts_rows/pallas_call | solution.py:717
  269.5 15.8 %experts_weights.2 = (bf16[2,3,192,512]{3,2,1,0:T(8,128)(2,1)}, bf16[2,3,192,512]{3,2,1,0:T(8,128)(2,1)}, bf16[2,3,192,512]{3,2,1,0:T(8,128)(2,1)}, bf16[2,3,192,512]{3,2,1,0:T(8,128)(2,1)}) custom-call(s32[4]{0:T(128)} %pad_add_fusion.1.s_ref.here_ref, bf16[1536,2048]{1,0:T(8,128)(2,1)} %get-tuple-element.279.h_any, ...), custom_call_target="tpu_custom_call" | custom-call | flops 3221225472 | bytes 6666666 | tf_op jit(solution)/shard_map/experts_weights/pallas_call | solution.py:801
  286.9 30.1 %experts_rows.3 = (bf16[1024,1536]{1,0:T(8,128)(2,1)}, bf16[1024,1536]{1,0:T(8,128)(2,1)}, bf16[1024,1536]{1,0:T(8,128)(2,1)}, bf16[1024,1536]{1,0:T(8,128)(2,1)...) custom-call(s32[13]{0:T(128)} %stack.499.places_ref, bf16[256,1536]{1,0:T(8,128)(2,1)} %get-tuple-element.288.refs_0_, ...), custom_call_target="tpu_custom_call" | custom-call | flops 6442450944 | bytes 16666666 | tf_op jit(solution)/shard_map/experts_rows/pallas_call | solution.py:717
  318.2 5.9 %collective-permute-done.49.refs_1_ = bf16[1024,1536]{1,0:T(8,128)(2,1)S(1)} collective-permute-done((bf16[1024,1536]{1,0:T(8,128)(2,1)}, bf16[1024,1536]{1,0:T(8,128)(2,1)S(1)}, u32[]{:S(2)}, u32[]{:S(2)}) %collective-permute-start.49) | collective-permute-done | bytes 3145760 | tf_op jit(solution)/shard_map/ppermute | solution.py:54
  330.2 15.9 %experts_weights.3 = (bf16[2,3,192,512]{3,2,1,0:T(8,128)(2,1)}, bf16[2,3,192,512]{3,2,1,0:T(8,128)(2,1)}, bf16[2,3,192,512]{3,2,1,0:T(8,128)(2,1)}, bf16[2,3,192,512]{3,2,1,0:T(8,128)(2,1)}) custom-call(s32[4]{0:T(128)} %pad_add_fusion.1.s_ref.here_ref, bf16[1536,2048]{1,0:T(8,128)(2,1)} %get-tuple-element.279.h_any, ...), custom_call_target="tpu_custom_call" | custom-call | flops 3221225472 | bytes 6666666 | tf_op jit(solution)/shard_map/experts_weights/pallas_call | solution.py:801
  346.1 6.7 %collective-permute-done.54 = bf16[2,3,192,512]{3,2,1,0:T(8,128)(2,1)} collective-permute-done((bf16[2,3,192,512]{3,2,1,0:T(8,128)(2,1)}, bf16[2,3,192,512]{3,2,1,0:T(8,128)(2,1)}, u32[]{:S(2)}, u32[]{:S(2)}) %collective-permute-start.54) | collective-permute-done | bytes 1179680 | tf_op jit(solution)/shard_map/ppermute | solution.py:49
  365.4 16.6 %collective-permute-done.58 = bf16[2,3,192,512]{3,2,1,0:T(8,128)(2,1)S(1)} collective-permute-done((bf16[2,3,192,512]{3,2,1,0:T(8,128)(2,1)S(1)}, bf16[2,3,192,512]{3,2,1,0:T(8,128)(2,1)S(1)}, u32[]{:S(2)}, u32[]{:S(2)}) %collective-permute-start.58) | collective-permute-done | bytes 1179680 | tf_op jit(solution)/shard_map/ppermute | solution.py:49
  390.7 8.1 %join_back.1 = (f32[256,1536]{1,0:T(8,128)}, bf16[256,1536]{1,0:T(8,128)(2,1)}, f32[1,1536]{1,0:T(1,128)}, bf16[256,384]{1,0:T(8,128)(2,1)}, bf16[256,384]{1,0:T...) custom-call(s32[8]{0:T(128)} %concatenate.42.s_ref, bf16[1024,1536]{1,0:T(8,128)(2,1)} %get-tuple-element.301.refs_0_, ...), custom_call_target="tpu_custom_call" | custom-call | flops 402653184 | bytes 3932160 | tf_op jit(solution)/shard_map/join_back/pallas_call | solution.py:446
  402.5 6.5 %join_weights.1 = (bf16[2,2,4,48,1536]{4,3,2,1,0:T(8,128)(2,1)}, bf16[2,2,4,48,1536]{4,3,2,1,0:T(8,128)(2,1)}) custom-call(s32[8]{0:T(128)} %concatenate.42.s_ref, s32[4]{0:T(128)} %pad_add_fusion.1.s_ref.here_ref, bf16[256,1536]{1,0:T(8,128)(2,1)} %get-tuple-element.335.br_ref, bf16[256,384]{1,0:T(8,128)(2,1)} %get-tuple-element.244.refs_0_, ...), custom_call_target="tpu_custom_call" | custom-call | flops 402653184 | bytes 2097152 | tf_op jit(solution)/shard_map/join_weights/pallas_call | solution.py:485
  425.4 20.3 %attend_back.1.dq_ref = bf16[1024,640]{1,0:T(8,128)(2,1)} custom-call(s32[8]{0:T(128)} %concatenate.42.s_ref, bf16[256,640]{1,0:T(8,128)(2,1)} %get-tuple-element.217.refs_0_, bf16[256,640]{1,0:T(8,128)(2,1)} %get-tuple-element.218.refs_1_, bf16[256,640]{1,0:T(8,128)(2,1)} %get-tuple-element.219.refs_2_, bf16[256,640]{1,0:T(8,128)(2,1)} %project.3.refs_3_, ...), custom_call_target="tpu_custom_call" | custom-call | flops 3355443200 | bytes 1747626 | tf_op jit(solution)/shard_map/attend_back/pallas_call | solution.py:373
  462.9 9.3 %finish_weights.1 = (bf16[2,2,4,48,768]{4,3,2,1,0:T(8,128)(2,1)}, bf16[2,2,4,48,768]{4,3,2,1,0:T(8,128)(2,1)}) custom-call(s32[8]{0:T(128)} %concatenate.42.s_ref, s32[4]{0:T(128)} %pad_add_fusion.1.s_ref.here_ref, bf16[1024,640]{1,0:T(8,128)(2,1)} %attend_back.1.dq_ref, f32[1,1536]{1,0:T(1,128)} %broadcast_in_dim.59.gain_ref, ...), custom_call_target="tpu_custom_call" | custom-call | flops 671088640 | bytes 3145728 | tf_op jit(solution)/shard_map/finish_weights/pallas_call | solution.py:874
  472.2 13.4 %collective-permute-done.69.their_ref = bf16[192,512]{1,0:T(8,128)(2,1)S(1)} collective-permute-done((bf16[192,512]{1,0:T(8,128)(2,1)S(1)}, bf16[192,512]{1,0:T(8,128)(2,1)S(1)}, u32[]{:S(2)}, u32[]{:S(2)}) %collective-permute-start.69) | collective-permute-done | bytes 196640 | tf_op jit(solution)/shard_map/ppermute | solution.py:54
  492.2 16.6 %collective-permute-done.72 = bf16[256,1536]{1,0:T(8,128)(2,1)S(1)} collective-permute-done((bf16[256,1536]{1,0:T(8,128)(2,1)}, bf16[256,1536]{1,0:T(8,128)(2,1)S(1)}, u32[]{:S(2)}, u32[]{:S(2)}) %collective-permute-start.72) | collective-permute-done | bytes 786464 | tf_op jit(solution)/shard_map/ppermute | solution.py:49
  513.7 11.6 %collective-permute-done.75 = bf16[2,4,48,768]{3,2,1,0:T(8,128)(2,1)} collective-permute-done((bf16[2,4,48,768]{3,2,1,0:T(8,128)(2,1)}, bf16[2,4,48,768]{3,2,1,0:T(8,128)(2,1)}, u32[]{:S(2)}, u32[]{:S(2)}) %collective-permute-start.75) | collective-permute-done | bytes 589856 | tf_op jit(solution)/shard_map/ppermute | solution.py:54
  548.6 9.3 %collective-permute-done.77 = bf16[256,1536]{1,0:T(8,128)(2,1)S(1)} collective-permute-done((bf16[256,1536]{1,0:T(8,128)(2,1)S(1)}, bf16[256,1536]{1,0:T(8,128)(2,1)S(1)}, u32[]{:S(2)}, u32[]{:S(2)}) %collective-permute-start.77) | collective-permute-done | bytes 786464 | tf_op jit(solution)/shard_map/ppermute | solution.py:49
  (427 shorter events, 257.2 us)
Async XLA Ops:
  100.9 31.1 %collective-permute-start.19 = (bf16[2,3,192,512]{3,2,1,0:T(8,128)(2,1)}, bf16[2,3,192,512]{3,2,1,0:T(8,128)(2,1)}, u32[]{:S(2)}, u32[]{:S(2)}) collective-permute-start(bf16[2,3,192,512]{3,2,1,0:T(8,128)(2,1)} %pad_maximum_fusion.1.refs_16_), channel_id=1, source_target_pairs={{0,16},{16,0},{1,17},{17,1},{2,18},{18,2},{3,19},{19,3},{4,20},{20... | collective-permute-start | bytes 3538952 | tf_op jit(solution)/shard_map/ppermute | solution.py:49
  102.4 29.6 %collective-permute-start.21 = (bf16[256,1664]{1,0:T(8,128)(2,1)S(1)}, bf16[256,1664]{1,0:T(8,128)(2,1)}, u32[]{:S(2)}, u32[]{:S(2)}) collective-permute-start(bf16[256,1664]{1,0:T(8,128)(2,1)S(1)} %pad_maximum_fusion.3.refs_8_.refs_0_), channel_id=1, source_target_pairs={{0,4},{4,0},{8,12},{12,8},{1,5},{5,1},{9,13},{13,9},{2,6},{6,2},{1... | collective-permute-start | bytes 2555912 | tf_op jit(solution)/shard_map/ppermute | solution.py:54
  171.3 31.0 %collective-permute-start.32 = (bf16[256,1536]{1,0:T(8,128)(2,1)}, bf16[256,1536]{1,0:T(8,128)(2,1)S(1)}, u32[]{:S(2)}, u32[]{:S(2)}) collective-permute-start(bf16[256,1536]{1,0:T(8,128)(2,1)} %get-tuple-element.288.refs_0_), channel_id=1, source_target_pairs={{0,1},{1,0},{2,3},{3,2},{4,5},{5,4},{6,7},{7,6},{8,9},{9,8},{10,11... | collective-permute-start | bytes 2359304 | tf_op jit(solution)/shard_map/ppermute | solution.py:54
  171.3 31.0 %collective-permute-start.33 = (bf16[256,1536]{1,0:T(8,128)(2,1)}, bf16[256,1536]{1,0:T(8,128)(2,1)S(1)}, u32[]{:S(2)}, u32[]{:S(2)}) collective-permute-start(bf16[256,1536]{1,0:T(8,128)(2,1)} %get-tuple-element.288.refs_0_), channel_id=1, source_target_pairs={{0,2},{1,3},{2,0},{3,1},{4,6},{5,7},{6,4},{7,5},{8,10},{9,11},{10,... | collective-permute-start | bytes 2359304 | tf_op jit(solution)/shard_map/ppermute | solution.py:54
  171.9 32.5 %collective-permute-start.34 = (bf16[256,1536]{1,0:T(8,128)(2,1)}, bf16[256,1536]{1,0:T(8,128)(2,1)S(1)}, u32[]{:S(2)}, u32[]{:S(2)}) collective-permute-start(bf16[256,1536]{1,0:T(8,128)(2,1)} %get-tuple-element.288.refs_0_), channel_id=1, source_target_pairs={{0,4},{4,0},{8,12},{12,8},{1,5},{5,1},{9,13},{13,9},{2,6},{6,2},{1... | collective-permute-start | bytes 2359304 | tf_op jit(solution)/shard_map/ppermute | solution.py:54
  204.4 30.4 %collective-permute-start.38 = (bf16[256,1536]{1,0:T(8,128)(2,1)S(1)}, bf16[256,1536]{1,0:T(8,128)(2,1)S(1)}, u32[]{:S(2)}, u32[]{:S(2)}) collective-permute-start(bf16[256,1536]{1,0:T(8,128)(2,1)S(1)} %collective-permute-done.33.refs_2_), channel_id=1, source_target_pairs={{0,1},{1,0},{2,3},{3,2},{4,5},{5,4},{6,7},{7,6},{8,9},{9,8},{10,11... | collective-permute-start | bytes 2359304 | tf_op jit(solution)/shard_map/ppermute | solution.py:54
  204.5 30.4 %collective-permute-start.37 = (bf16[256,1536]{1,0:T(8,128)(2,1)S(1)}, bf16[256,1536]{1,0:T(8,128)(2,1)S(1)}, u32[]{:S(2)}, u32[]{:S(2)}) collective-permute-start(bf16[256,1536]{1,0:T(8,128)(2,1)S(1)} %collective-permute-done.34.refs_1_), channel_id=1, source_target_pairs={{0,1},{1,0},{2,3},{3,2},{4,5},{5,4},{6,7},{7,6},{8,9},{9,8},{10,11... | collective-permute-start | bytes 2359304 | tf_op jit(solution)/shard_map/ppermute | solution.py:54
  205.0 29.9 %collective-permute-start.39 = (bf16[256,1536]{1,0:T(8,128)(2,1)S(1)}, bf16[256,1536]{1,0:T(8,128)(2,1)}, u32[]{:S(2)}, u32[]{:S(2)}) collective-permute-start(bf16[256,1536]{1,0:T(8,128)(2,1)S(1)} %collective-permute-done.34.refs_1_), channel_id=1, source_target_pairs={{0,2},{1,3},{2,0},{3,1},{4,6},{5,7},{6,4},{7,5},{8,10},{9,11},{10,... | collective-permute-start | bytes 2359304 | tf_op jit(solution)/shard_map/ppermute | solution.py:54
  206.3 28.5 %collective-permute-start.41 = (bf16[3,192,512]{2,1,0:T(8,128)(2,1)S(1)}, bf16[3,192,512]{2,1,0:T(8,128)(2,1)S(1)}, u32[]{:S(2)}, u32[]{:S(2)}) collective-permute-start(bf16[3,192,512]{2,1,0:T(8,128)(2,1)S(1)} %pad_maximum_fusion.10.refs_16_), channel_id=1, source_target_pairs={{0,8},{4,12},{8,0},{12,4},{1,9},{5,13},{9,1},{13,5},{2,10},{6,14},... | collective-permute-start | bytes 1769480 | tf_op jit(solution)/shard_map/ppermute | solution.py:54
  237.1 31.2 %collective-permute-start.42 = (bf16[3,192,512]{2,1,0:T(8,128)(2,1)}, bf16[3,192,512]{2,1,0:T(8,128)(2,1)}, u32[]{:S(2)}, u32[]{:S(2)}) collective-permute-start(bf16[3,192,512]{2,1,0:T(8,128)(2,1)} %pad_maximum_fusion.11.refs_17_), channel_id=1, source_target_pairs={{0,8},{4,12},{8,0},{12,4},{1,9},{5,13},{9,1},{13,5},{2,10},{6,14},... | collective-permute-start | bytes 1769480 | tf_op jit(solution)/shard_map/ppermute | solution.py:54
  237.1 31.2 %collective-permute-start.43 = (bf16[3,192,512]{2,1,0:T(8,128)(2,1)}, bf16[3,192,512]{2,1,0:T(8,128)(2,1)}, u32[]{:S(2)}, u32[]{:S(2)}) collective-permute-start(bf16[3,192,512]{2,1,0:T(8,128)(2,1)} %pad_maximum_fusion.11.refs_17_), channel_id=1, source_target_pairs={{0,16},{16,0},{1,17},{17,1},{2,18},{18,2},{3,19},{19,3},{4,20},{20... | collective-permute-start | bytes 1769480 | tf_op jit(solution)/shard_map/ppermute | solution.py:49
  237.6 30.7 %collective-permute-start.44 = (bf16[3,192,512]{2,1,0:T(8,128)(2,1)}, bf16[3,192,512]{2,1,0:T(8,128)(2,1)}, u32[]{:S(2)}, u32[]{:S(2)}) collective-permute-start(bf16[3,192,512]{2,1,0:T(8,128)(2,1)} %copy-done.59), channel_id=1, source_target_pairs={{0,16},{16,0},{1,17},{17,1},{2,18},{18,2},{3,19},{19,3},{4,20},{20... | collective-permute-start | bytes 1769480 | tf_op jit(solution)/shard_map/ppermute | solution.py:49
  285.3 31.7 %collective-permute-start.48 = (bf16[2,3,192,512]{3,2,1,0:T(8,128)(2,1)}, bf16[2,3,192,512]{3,2,1,0:T(8,128)(2,1)S(1)}, u32[]{:S(2)}, u32[]{:S(2)}) collective-permute-start(bf16[2,3,192,512]{3,2,1,0:T(8,128)(2,1)} %get-tuple-element.299), channel_id=1, source_target_pairs={{0,16},{16,0},{1,17},{17,1},{2,18},{18,2},{3,19},{19,3},{4,20},{20... | collective-permute-start | bytes 3538952 | tf_op jit(solution)/shard_map/ppermute | solution.py:49
  324.1 30.4 %collective-permute-start.50 = (bf16[1024,1536]{1,0:T(8,128)(2,1)}, bf16[1024,1536]{1,0:T(8,128)(2,1)}, u32[]{:S(2)}, u32[]{:S(2)}) collective-permute-start(bf16[1024,1536]{1,0:T(8,128)(2,1)} %get-tuple-element.306), channel_id=1, source_target_pairs={{0,1},{1,0},{2,3},{3,2},{4,5},{5,4},{6,7},{7,6},{8,9},{9,8},{10,11... | collective-permute-start | bytes 9437192 | tf_op jit(solution)/shard_map/ppermute | solution.py:54
  324.3 28.6 %collective-permute-start.54 = (bf16[2,3,192,512]{3,2,1,0:T(8,128)(2,1)}, bf16[2,3,192,512]{3,2,1,0:T(8,128)(2,1)}, u32[]{:S(2)}, u32[]{:S(2)}) collective-permute-start(bf16[2,3,192,512]{3,2,1,0:T(8,128)(2,1)} %get-tuple-element.310), channel_id=1, source_target_pairs={{0,16},{16,0},{1,17},{17,1},{2,18},{18,2},{3,19},{19,3},{4,20},{20... | collective-permute-start | bytes 3538952 | tf_op jit(solution)/shard_map/ppermute | solution.py:49
  325.0 29.4 %collective-permute-start.53 = (bf16[3,192,512]{2,1,0:T(8,128)(2,1)}, bf16[3,192,512]{2,1,0:T(8,128)(2,1)}, u32[]{:S(2)}, u32[]{:S(2)}) collective-permute-start(bf16[3,192,512]{2,1,0:T(8,128)(2,1)} %get-tuple-element.309), channel_id=1, source_target_pairs={{0,8},{4,12},{8,0},{12,4},{1,9},{5,13},{9,1},{13,5},{2,10},{6,14},... | collective-permute-start | bytes 1769480 | tf_op jit(solution)/shard_map/ppermute | solution.py:54
  359.3 29.8 %collective-permute-start.56 = (bf16[256,1536]{1,0:T(8,128)(2,1)S(1)}, bf16[256,1536]{1,0:T(8,128)(2,1)S(1)}, u32[]{:S(2)}, u32[]{:S(2)}) collective-permute-start(bf16[256,1536]{1,0:T(8,128)(2,1)S(1)} %pad_maximum_fusion.6), channel_id=1, source_target_pairs={{0,4},{4,0},{8,12},{12,8},{1,5},{5,1},{9,13},{13,9},{2,6},{6,2},{1... | collective-permute-start | bytes 2359304 | tf_op jit(solution)/shard_map/ppermute | solution.py:54
  360.7 28.4 %collective-permute-start.55 = (bf16[256,1536]{1,0:T(8,128)(2,1)S(1)}, bf16[256,1536]{1,0:T(8,128)(2,1)S(1)}, u32[]{:S(2)}, u32[]{:S(2)}) collective-permute-start(bf16[256,1536]{1,0:T(8,128)(2,1)S(1)} %pad_maximum_fusion.5), channel_id=1, source_target_pairs={{0,2},{1,3},{2,0},{3,1},{4,6},{5,7},{6,4},{7,5},{8,10},{9,11},{10,... | collective-permute-start | bytes 2359304 | tf_op jit(solution)/shard_map/ppermute | solution.py:54
  418.5 36.6 %collective-permute-start.67 = (bf16[2,2,4,48,1536]{4,3,2,1,0:T(8,128)(2,1)}, bf16[2,2,4,48,1536]{4,3,2,1,0:T(8,128)(2,1)}, u32[]{:S(2)}, u32[]{:S(2)}) collective-permute-start(bf16[2,2,4,48,1536]{4,3,2,1,0:T(8,128)(2,1)} %get-tuple-element.350), channel_id=1, source_target_pairs={{0,1},{1,0},{2,3},{3,2},{4,5},{5,4},{6,7},{7,6},{8,9},{9,8},{10,11... | collective-permute-start | bytes 7077896 | tf_op jit(solution)/shard_map/ppermute | solution.py:54
  418.5 35.7 %collective-permute-start.64 = (bf16[256,1536]{1,0:T(8,128)(2,1)}, bf16[256,1536]{1,0:T(8,128)(2,1)}, u32[]{:S(2)}, u32[]{:S(2)}) collective-permute-start(bf16[256,1536]{1,0:T(8,128)(2,1)} %get-tuple-element.340), channel_id=1, source_target_pairs={{0,2},{1,3},{2,0},{3,1},{4,6},{5,7},{6,4},{7,5},{8,10},{9,11},{10,... | collective-permute-start | bytes 2359304 | tf_op jit(solution)/shard_map/ppermute | solution.py:54
  422.0 33.1 %collective-permute-start.65 = (bf16[256,1536]{1,0:T(8,128)(2,1)}, bf16[256,1536]{1,0:T(8,128)(2,1)}, u32[]{:S(2)}, u32[]{:S(2)}) collective-permute-start(bf16[256,1536]{1,0:T(8,128)(2,1)} %add_convert_fusion.5), channel_id=1, source_target_pairs={{0,4},{4,0},{8,12},{12,8},{1,5},{5,1},{9,13},{13,9},{2,6},{6,2},{1... | collective-permute-start | bytes 2359304 | tf_op jit(solution)/shard_map/ppermute | solution.py:54
  424.2 30.0 %collective-permute-start.66 = (bf16[3,192,512]{2,1,0:T(8,128)(2,1)S(1)}, bf16[3,192,512]{2,1,0:T(8,128)(2,1)S(1)}, u32[]{:S(2)}, u32[]{:S(2)}) collective-permute-start(bf16[3,192,512]{2,1,0:T(8,128)(2,1)S(1)} %copy-done.57), channel_id=1, source_target_pairs={{0,8},{4,12},{8,0},{12,4},{1,9},{5,13},{9,1},{13,5},{2,10},{6,14},... | collective-permute-start | bytes 1769480 | tf_op jit(solution)/shard_map/ppermute | solution.py:54
  457.7 28.7 %collective-permute-start.70 = (bf16[2,4,48,1536]{3,2,1,0:T(8,128)(2,1)}, bf16[2,4,48,1536]{3,2,1,0:T(8,128)(2,1)S(1)}, u32[]{:S(2)}, u32[]{:S(2)}) collective-permute-start(bf16[2,4,48,1536]{3,2,1,0:T(8,128)(2,1)} %fusion.9), channel_id=1, source_target_pairs={{0,2},{1,3},{2,0},{3,1},{4,6},{5,7},{6,4},{7,5},{8,10},{9,11},{10,... | collective-permute-start | bytes 3538952 | tf_op jit(solution)/shard_map/ppermute | solution.py:54
  458.0 28.4 %collective-permute-start.71 = (bf16[3,192,512]{2,1,0:T(8,128)(2,1)}, bf16[3,192,512]{2,1,0:T(8,128)(2,1)S(1)}, u32[]{:S(2)}, u32[]{:S(2)}) collective-permute-start(bf16[3,192,512]{2,1,0:T(8,128)(2,1)} %get-tuple-element.365), channel_id=1, source_target_pairs={{0,8},{4,12},{8,0},{12,4},{1,9},{5,13},{9,1},{13,5},{2,10},{6,14},... | collective-permute-start | bytes 1769480 | tf_op jit(solution)/shard_map/ppermute | solution.py:54
  (135 other events, 2264.7 us)

commit v5 on v4

--- a/solution.py
+++ b/solution.py
@@ -426,8 +426,17 @@
     count = len(addends)
 
     def body(s_ref, *refs):
-        ins, (mid_ref, cot_ref, gain_ref, w_ref, gmid_ref, br_ref, gg_ref, *outs) = refs[:count], refs[count:]
+        ins, (mid_ref, cot_ref, gain_ref, w_any, gmid_ref, br_ref, gg_ref, *outs) = refs[:count], refs[count:]
+        *outs, w_ref, sems = outs
         me = s_ref[4]
+        spans = [
+            pl.ds(pl.multiple_of(lax.rem(me - k + blocks, blocks) * part, part), part) for k in range(blocks)
+        ]
+        copies = [
+            pltpu.make_async_copy(w_any.at[spans[k], :], w_ref.at[k], sems.at[k]) for k in range(blocks)
+        ]
+        for copy in copies:
+            copy.start()
         grad_hidden = sum(t[...].astype(F32) for t in ins)
         middle = mid_ref[...]
         inv = rms(middle)
@@ -438,8 +447,8 @@
         gmid_ref[...] = grad_middle
         br_ref[...] = (residual_scale * grad_middle).astype(BF)
         for k in range(blocks):
-            at = pl.ds(pl.multiple_of(lax.rem(me - k + blocks, blocks) * part, part), part)
-            outs[k][...] = mm(br_ref[...], w_ref[at, :], NT).astype(BF)
+            copies[k].wait()
+            outs[k][...] = mm(br_ref[...], w_ref[k], NT).astype(BF)
 
     front = lambda t: pl.BlockSpec((rows, d), lambda i: (0, 0))
     fixed = lambda *shape: pl.BlockSpec(shape, lambda i: (0, 0))
@@ -454,8 +463,9 @@
         + [jax.ShapeDtypeStruct((rows, part), BF)] * blocks,
         in_specs=[SM]
         + [front(t) for t in addends]
-        + [fixed(rows, d), fixed(rows, d), fixed(1, d), fixed(d, d)],
+        + [fixed(rows, d), fixed(rows, d), fixed(1, d), ANY],
         out_specs=[fixed(rows, d), fixed(rows, d), fixed(1, d)] + [fixed(rows, part)] * blocks,
+        scratch_shapes=[pltpu.VMEM((blocks, part, d), BF), pltpu.SemaphoreType.DMA((blocks,))],
         compiler_params=params(),
         cost_estimate=cost(2 * rows * d * d, 2 * d * d + 18 * rows * d),
         name="join_back",
@@ -1088,11 +1098,12 @@
     wo_a, wo_b = join_weights(scalars, here, branch, mixes, nd, ne)
     ready = lax.optimization_barrier((x_0[0], x_1[0], branch))
     swap = jnp.stack([add(ready[0][1], z_0[1]), add(ready[1][1], z_1[1])])
-    run.end(grad_mixes, x_3, far_o1, wo_b, swap)
+    other_o = add(sum_o[1], far_o1)
+    run.end(grad_mixes, x_3, other_o, wo_b, swap)
 
     z_2 = flip(run.hold(x_2[1]), "ctx", 2)
     far_o = flip_e(run.hold(sum_o[2]), 2)
-    other_o = flip(add(sum_o[1], run.hold(far_o1)), "ctx", 1)
+    other_o = flip(run.hold(other_o), "ctx", 1)
     wo_b = flip_e(run.hold(wo_b), 1)
     dqkv = attend_back(scalars, pieces, run.hold(grad_mixes), lse, cos, sin, heads, kvs)
     grad_normed = finish(scalars, dqkv, w_qkv, nz)

time: 585 us -> 581 us (level)
  no operation moved by 1% of the time
where the time goes in v5:
time: 581 us; the launch traced here: 575 us
  waiting for transfers between devices  216 us (37%)
  Pallas kernels  192 us (33%)
  starting transfers between devices  80.6 us (14%)
  other arithmetic  57.5 us (10%)
  local copies, waits for them, and re-layouts  27 us (5%)
    ppermute x45, waiting for transfers between devices, flip(): return lax.ppermute(x, axis, [(i, i ^ mask) for i in range(n)])  106 us
    ppermute x34, waiting for transfers between devices, shift(): return lax.ppermute(x, axis, [(i, (i + by) % n) for i in range(n)])  103 us
    pallas_call x2, Pallas kernels, experts_rows(): pl.pallas_call(body, grid=(tiles,), out_shape=sum_shapes + (jax.ShapeDtyp...  57.4 us
    ppermute x34, starting transfers between devices, shift(): return lax.ppermute(x, axis, [(i, (i + by) % n) for i in range(n)])  41.9 us
    pallas_call x2, Pallas kernels, experts_weights(): pl.pallas_call(body, out_shape=[jax.ShapeDtypeStruct((2, 3, r, width), BF...  31.7 us
    ppermute x45, starting transfers between devices, flip(): return lax.ppermute(x, axis, [(i, i ^ mask) for i in range(n)])  31.7 us
    convert_element_type x20, other arithmetic, add(): return (a.astype(F32) + b.astype(F32)).astype(BF)  27.2 us
    pallas_call x1, Pallas kernels, attend_back(): pl.pallas_call(body, out_shape=jax.ShapeDtypeStruct((span, width), BF), i...  20.3 us
  transfers between devices with their start and end apart: 83, of which 35 were waited for; matrix products, arithmetic and copies ran while one was open for 11% of the time, Pallas kernels for 33%

profile of v5, /device:TPU:0, one launch (start us, length us, event | category | flops | bytes accessed | tf_op | source)
XLA Modules:
  0.0 575.3 jit_solution(16005497497685021147)
XLA Ops:
  16.7 13.9 %collective-permute-done.3.refs_1_ = bf16[256,1536]{1,0:T(8,128)(2,1)S(1)} collective-permute-done((bf16[256,1536]{1,0:T(8,128)(2,1)S(1)}, bf16[256,1536]{1,0:T(8,128)(2,1)S(1)}, u32[]{:S(2)}, u32[]{:S(2)}) %collective-permute-start.3) | collective-permute-done | bytes 786464 | tf_op jit(solution)/shard_map/ppermute | solution.py:49
  60.0 7.2 %collective-permute-done.11 = bf16[48,1536]{1,0:T(8,128)(2,1)} collective-permute-done((bf16[48,1536]{1,0:T(8,128)(2,1)}, bf16[48,1536]{1,0:T(8,128)(2,1)}, u32[]{:S(2)}, u32[]{:S(2)}) %collective-permute-start.11) | collective-permute-done | bytes 147488 | tf_op jit(solution)/shard_map/ppermute | solution.py:78
  108.1 13.3 %attend.1 = (bf16[256,384]{1,0:T(8,128)(2,1)}, bf16[256,384]{1,0:T(8,128)(2,1)}, bf16[256,384]{1,0:T(8,128)(2,1)}, bf16[256,384]{1,0:T(8,128)(2,1)}, f32[8,1024]{1,0:T(8,128)}) custom-call(s32[8]{0:T(128)} %concatenate.42.s_ref, bf16[256,640]{1,0:T(8,128)(2,1)} %get-tuple-element.217.refs_0_, bf16[256,640]{1,0:T(8,128)(2,1)} %get-tuple-element.218.refs_1_, ...), custom_call_target="tpu_custom_call" | custom-call | flops 1342177280 | bytes 873813 | tf_op jit(solution)/shard_map/attend/pallas_call | solution.py:291
  123.6 6.2 %collective-permute-done.18.refs_18_ = bf16[3,192,512]{2,1,0:T(8,128)(2,1)} collective-permute-done((bf16[3,192,512]{2,1,0:T(8,128)(2,1)}, bf16[3,192,512]{2,1,0:T(8,128)(2,1)}, u32[]{:S(2)}, u32[]{:S(2)}) %collective-permute-start.18) | collective-permute-done | bytes 589856 | tf_op jit(solution)/shard_map/ppermute | solution.py:54
  142.4 9.8 %collective-permute-done.23.refs_2_ = bf16[256,384]{1,0:T(8,128)(2,1)} collective-permute-done((bf16[256,384]{1,0:T(8,128)(2,1)}, bf16[256,384]{1,0:T(8,128)(2,1)}, u32[]{:S(2)}, u32[]{:S(2)}) %collective-permute-start.23) | collective-permute-done | bytes 196640 | tf_op jit(solution)/shard_map/ppermute | solution.py:49
  155.6 6.2 %join.1 = (f32[256,1536]{1,0:T(8,128)}, bf16[256,1536]{1,0:T(8,128)(2,1)}) custom-call(s32[8]{0:T(128)} %concatenate.42.s_ref, bf16[256,384]{1,0:T(8,128)(2,1)} %get-tuple-element.244.refs_0_, bf16[256,384]{1,0:T(8,128)(2,1)} %collective-permute-done.22.refs_1_, bf16[256,384]{1,0:T(8,128)(2,1)} %collective-permute-done.23.refs_2_, ...), custom_call_target="tpu_custom_call" | custom-call | flops 402653184 | bytes 2883584 | tf_op jit(solution)/shard_map/join/pallas_call | solution.py:411
  176.8 12.6 %collective-permute-done.36.refs_18_ = bf16[3,192,512]{2,1,0:T(8,128)(2,1)S(1)} collective-permute-done((bf16[3,192,512]{2,1,0:T(8,128)(2,1)S(1)}, bf16[3,192,512]{2,1,0:T(8,128)(2,1)S(1)}, u32[]{:S(2)}, u32[]{:S(2)}) %collective-permute-start.36) | collective-permute-done | bytes 589856 | tf_op jit(solution)/shard_map/ppermute | solution.py:49
  189.4 12.9 %collective-permute-done.35.refs_19_ = bf16[3,192,512]{2,1,0:T(8,128)(2,1)S(1)} collective-permute-done((bf16[3,192,512]{2,1,0:T(8,128)(2,1)S(1)}, bf16[3,192,512]{2,1,0:T(8,128)(2,1)S(1)}, u32[]{:S(2)}, u32[]{:S(2)}) %collective-permute-start.35) | collective-permute-done | bytes 589856 | tf_op jit(solution)/shard_map/ppermute | solution.py:54
  210.1 24.7 %collective-permute-done.41.refs_20_ = bf16[3,192,512]{2,1,0:T(8,128)(2,1)S(1)} collective-permute-done((bf16[3,192,512]{2,1,0:T(8,128)(2,1)S(1)}, bf16[3,192,512]{2,1,0:T(8,128)(2,1)S(1)}, u32[]{:S(2)}, u32[]{:S(2)}) %collective-permute-start.41) | collective-permute-done | bytes 589856 | tf_op jit(solution)/shard_map/ppermute | solution.py:54
  240.8 27.3 %experts_rows.2 = (bf16[2048,1536]{1,0:T(8,128)(2,1)}, bf16[2048,1536]{1,0:T(8,128)(2,1)}, bf16[2048,1024]{1,0:T(8,128)(2,1)}, bf16[512,2048]{1,0:T(8,128)(2,1)}, bf16[1536,2048]{1,0:T(8,128)(2,1)}) custom-call(s32[13]{0:T(128)} %stack.499.places_ref, bf16[256,1536]{1,0:T(8,128)(2,1)} %get-tuple-element.288.refs_0_, bf16[256,1536]{1,0:T(8,128)(2,1)} %copy-done.52, ...), custom_call_target="tpu_custom_call" | custom-call | flops 6442450944 | bytes 16666666 | tf_op jit(solution)/shard_map/experts_rows/pallas_call | solution.py:727
  269.4 15.8 %experts_weights.2 = (bf16[2,3,192,512]{3,2,1,0:T(8,128)(2,1)}, bf16[2,3,192,512]{3,2,1,0:T(8,128)(2,1)}, bf16[2,3,192,512]{3,2,1,0:T(8,128)(2,1)}, bf16[2,3,192,512]{3,2,1,0:T(8,128)(2,1)}) custom-call(s32[4]{0:T(128)} %pad_add_fusion.1.s_ref.here_ref, bf16[1536,2048]{1,0:T(8,128)(2,1)} %get-tuple-element.279.h_any, ...), custom_call_target="tpu_custom_call" | custom-call | flops 3221225472 | bytes 6666666 | tf_op jit(solution)/shard_map/experts_weights/pallas_call | solution.py:811
  286.8 30.1 %experts_rows.3 = (bf16[1024,1536]{1,0:T(8,128)(2,1)}, bf16[1024,1536]{1,0:T(8,128)(2,1)}, bf16[1024,1536]{1,0:T(8,128)(2,1)}, bf16[1024,1536]{1,0:T(8,128)(2,1)...) custom-call(s32[13]{0:T(128)} %stack.499.places_ref, bf16[256,1536]{1,0:T(8,128)(2,1)} %get-tuple-element.288.refs_0_, ...), custom_call_target="tpu_custom_call" | custom-call | flops 6442450944 | bytes 16666666 | tf_op jit(solution)/shard_map/experts_rows/pallas_call | solution.py:727
  318.1 5.9 %collective-permute-done.49.refs_1_ = bf16[1024,1536]{1,0:T(8,128)(2,1)S(1)} collective-permute-done((bf16[1024,1536]{1,0:T(8,128)(2,1)}, bf16[1024,1536]{1,0:T(8,128)(2,1)S(1)}, u32[]{:S(2)}, u32[]{:S(2)}) %collective-permute-start.49) | collective-permute-done | bytes 3145760 | tf_op jit(solution)/shard_map/ppermute | solution.py:54
  330.3 15.9 %experts_weights.3 = (bf16[2,3,192,512]{3,2,1,0:T(8,128)(2,1)}, bf16[2,3,192,512]{3,2,1,0:T(8,128)(2,1)}, bf16[2,3,192,512]{3,2,1,0:T(8,128)(2,1)}, bf16[2,3,192,512]{3,2,1,0:T(8,128)(2,1)}) custom-call(s32[4]{0:T(128)} %pad_add_fusion.1.s_ref.here_ref, bf16[1536,2048]{1,0:T(8,128)(2,1)} %get-tuple-element.279.h_any, ...), custom_call_target="tpu_custom_call" | custom-call | flops 3221225472 | bytes 6666666 | tf_op jit(solution)/shard_map/experts_weights/pallas_call | solution.py:811
  346.2 6.5 %collective-permute-done.54 = bf16[2,3,192,512]{3,2,1,0:T(8,128)(2,1)} collective-permute-done((bf16[2,3,192,512]{3,2,1,0:T(8,128)(2,1)}, bf16[2,3,192,512]{3,2,1,0:T(8,128)(2,1)}, u32[]{:S(2)}, u32[]{:S(2)}) %collective-permute-start.54) | collective-permute-done | bytes 1179680 | tf_op jit(solution)/shard_map/ppermute | solution.py:49
  365.5 16.4 %collective-permute-done.58 = bf16[2,3,192,512]{3,2,1,0:T(8,128)(2,1)S(1)} collective-permute-done((bf16[2,3,192,512]{3,2,1,0:T(8,128)(2,1)S(1)}, bf16[2,3,192,512]{3,2,1,0:T(8,128)(2,1)S(1)}, u32[]{:S(2)}, u32[]{:S(2)}) %collective-permute-start.58) | collective-permute-done | bytes 1179680 | tf_op jit(solution)/shard_map/ppermute | solution.py:49
  391.7 8.2 %join_back.1 = (f32[256,1536]{1,0:T(8,128)}, bf16[256,1536]{1,0:T(8,128)(2,1)}, f32[1,1536]{1,0:T(1,128)}, bf16[256,384]{1,0:T(8,128)(2,1)}, bf16[256,384]{1,0:T...) custom-call(s32[8]{0:T(128)} %concatenate.42.s_ref, bf16[1024,1536]{1,0:T(8,128)(2,1)} %get-tuple-element.301.refs_0_, ...), custom_call_target="tpu_custom_call" | custom-call | flops 402653184 | bytes 3932160 | tf_op jit(solution)/shard_map/join_back/pallas_call | solution.py:455
  403.2 6.5 %join_weights.1 = (bf16[2,2,4,48,1536]{4,3,2,1,0:T(8,128)(2,1)}, bf16[2,2,4,48,1536]{4,3,2,1,0:T(8,128)(2,1)}) custom-call(s32[8]{0:T(128)} %concatenate.42.s_ref, s32[4]{0:T(128)} %pad_add_fusion.1.s_ref.here_ref, bf16[256,1536]{1,0:T(8,128)(2,1)} %get-tuple-element.335.br_ref, bf16[256,384]{1,0:T(8,128)(2,1)} %get-tuple-element.244.refs_0_, ...), custom_call_target="tpu_custom_call" | custom-call | flops 402653184 | bytes 2097152 | tf_op jit(solution)/shard_map/join_weights/pallas_call | solution.py:495
  421.8 20.3 %attend_back.1.dq_ref = bf16[1024,640]{1,0:T(8,128)(2,1)} custom-call(s32[8]{0:T(128)} %concatenate.42.s_ref, bf16[256,640]{1,0:T(8,128)(2,1)} %get-tuple-element.217.refs_0_, bf16[256,640]{1,0:T(8,128)(2,1)} %get-tuple-element.218.refs_1_, bf16[256,640]{1,0:T(8,128)(2,1)} %get-tuple-element.219.refs_2_, bf16[256,640]{1,0:T(8,128)(2,1)} %project.3.refs_3_, ...), custom_call_target="tpu_custom_call" | custom-call | flops 3355443200 | bytes 1747626 | tf_op jit(solution)/shard_map/attend_back/pallas_call | solution.py:373
  459.3 9.3 %finish_weights.1 = (bf16[2,2,4,48,768]{4,3,2,1,0:T(8,128)(2,1)}, bf16[2,2,4,48,768]{4,3,2,1,0:T(8,128)(2,1)}) custom-call(s32[8]{0:T(128)} %concatenate.42.s_ref, s32[4]{0:T(128)} %pad_add_fusion.1.s_ref.here_ref, bf16[1024,640]{1,0:T(8,128)(2,1)} %attend_back.1.dq_ref, f32[1,1536]{1,0:T(1,128)} %broadcast_in_dim.59.gain_ref, ...), custom_call_target="tpu_custom_call" | custom-call | flops 671088640 | bytes 3145728 | tf_op jit(solution)/shard_map/finish_weights/pallas_call | solution.py:884
  468.6 13.3 %collective-permute-done.69.their_ref = bf16[192,512]{1,0:T(8,128)(2,1)S(1)} collective-permute-done((bf16[192,512]{1,0:T(8,128)(2,1)S(1)}, bf16[192,512]{1,0:T(8,128)(2,1)S(1)}, u32[]{:S(2)}, u32[]{:S(2)}) %collective-permute-start.69) | collective-permute-done | bytes 196640 | tf_op jit(solution)/shard_map/ppermute | solution.py:54
  488.5 17.0 %collective-permute-done.72 = bf16[256,1536]{1,0:T(8,128)(2,1)S(1)} collective-permute-done((bf16[256,1536]{1,0:T(8,128)(2,1)}, bf16[256,1536]{1,0:T(8,128)(2,1)S(1)}, u32[]{:S(2)}, u32[]{:S(2)}) %collective-permute-start.72) | collective-permute-done | bytes 786464 | tf_op jit(solution)/shard_map/ppermute | solution.py:49
  510.3 11.8 %collective-permute-done.75 = bf16[2,4,48,768]{3,2,1,0:T(8,128)(2,1)} collective-permute-done((bf16[2,4,48,768]{3,2,1,0:T(8,128)(2,1)}, bf16[2,4,48,768]{3,2,1,0:T(8,128)(2,1)}, u32[]{:S(2)}, u32[]{:S(2)}) %collective-permute-start.75) | collective-permute-done | bytes 589856 | tf_op jit(solution)/shard_map/ppermute | solution.py:54
  544.4 9.3 %collective-permute-done.77 = bf16[256,1536]{1,0:T(8,128)(2,1)S(1)} collective-permute-done((bf16[256,1536]{1,0:T(8,128)(2,1)S(1)}, bf16[256,1536]{1,0:T(8,128)(2,1)S(1)}, u32[]{:S(2)}, u32[]{:S(2)}) %collective-permute-start.77) | collective-permute-done | bytes 786464 | tf_op jit(solution)/shard_map/ppermute | solution.py:49
  (429 shorter events, 252.8 us)
Async XLA Ops:
  100.9 31.1 %collective-permute-start.19 = (bf16[2,3,192,512]{3,2,1,0:T(8,128)(2,1)}, bf16[2,3,192,512]{3,2,1,0:T(8,128)(2,1)}, u32[]{:S(2)}, u32[]{:S(2)}) collective-permute-start(bf16[2,3,192,512]{3,2,1,0:T(8,128)(2,1)} %pad_maximum_fusion.1.refs_16_), channel_id=1, source_target_pairs={{0,16},{16,0},{1,17},{17,1},{2,18},{18,2},{3,19},{19,3},{4,20},{20... | collective-permute-start | bytes 3538952 | tf_op jit(solution)/shard_map/ppermute | solution.py:49
  102.4 29.6 %collective-permute-start.21 = (bf16[256,1664]{1,0:T(8,128)(2,1)S(1)}, bf16[256,1664]{1,0:T(8,128)(2,1)}, u32[]{:S(2)}, u32[]{:S(2)}) collective-permute-start(bf16[256,1664]{1,0:T(8,128)(2,1)S(1)} %pad_maximum_fusion.3.refs_8_.refs_0_), channel_id=1, source_target_pairs={{0,4},{4,0},{8,12},{12,8},{1,5},{5,1},{9,13},{13,9},{2,6},{6,2},{1... | collective-permute-start | bytes 2555912 | tf_op jit(solution)/shard_map/ppermute | solution.py:54
  171.3 31.0 %collective-permute-start.32 = (bf16[256,1536]{1,0:T(8,128)(2,1)}, bf16[256,1536]{1,0:T(8,128)(2,1)S(1)}, u32[]{:S(2)}, u32[]{:S(2)}) collective-permute-start(bf16[256,1536]{1,0:T(8,128)(2,1)} %get-tuple-element.288.refs_0_), channel_id=1, source_target_pairs={{0,1},{1,0},{2,3},{3,2},{4,5},{5,4},{6,7},{7,6},{8,9},{9,8},{10,11... | collective-permute-start | bytes 2359304 | tf_op jit(solution)/shard_map/ppermute | solution.py:54
  171.3 31.0 %collective-permute-start.33 = (bf16[256,1536]{1,0:T(8,128)(2,1)}, bf16[256,1536]{1,0:T(8,128)(2,1)S(1)}, u32[]{:S(2)}, u32[]{:S(2)}) collective-permute-start(bf16[256,1536]{1,0:T(8,128)(2,1)} %get-tuple-element.288.refs_0_), channel_id=1, source_target_pairs={{0,2},{1,3},{2,0},{3,1},{4,6},{5,7},{6,4},{7,5},{8,10},{9,11},{10,... | collective-permute-start | bytes 2359304 | tf_op jit(solution)/shard_map/ppermute | solution.py:54
  171.9 32.5 %collective-permute-start.34 = (bf16[256,1536]{1,0:T(8,128)(2,1)}, bf16[256,1536]{1,0:T(8,128)(2,1)S(1)}, u32[]{:S(2)}, u32[]{:S(2)}) collective-permute-start(bf16[256,1536]{1,0:T(8,128)(2,1)} %get-tuple-element.288.refs_0_), channel_id=1, source_target_pairs={{0,4},{4,0},{8,12},{12,8},{1,5},{5,1},{9,13},{13,9},{2,6},{6,2},{1... | collective-permute-start | bytes 2359304 | tf_op jit(solution)/shard_map/ppermute | solution.py:54
  204.5 30.4 %collective-permute-start.38 = (bf16[256,1536]{1,0:T(8,128)(2,1)S(1)}, bf16[256,1536]{1,0:T(8,128)(2,1)S(1)}, u32[]{:S(2)}, u32[]{:S(2)}) collective-permute-start(bf16[256,1536]{1,0:T(8,128)(2,1)S(1)} %collective-permute-done.33.refs_2_), channel_id=1, source_target_pairs={{0,1},{1,0},{2,3},{3,2},{4,5},{5,4},{6,7},{7,6},{8,9},{9,8},{10,11... | collective-permute-start | bytes 2359304 | tf_op jit(solution)/shard_map/ppermute | solution.py:54
  204.5 30.4 %collective-permute-start.37 = (bf16[256,1536]{1,0:T(8,128)(2,1)S(1)}, bf16[256,1536]{1,0:T(8,128)(2,1)S(1)}, u32[]{:S(2)}, u32[]{:S(2)}) collective-permute-start(bf16[256,1536]{1,0:T(8,128)(2,1)S(1)} %collective-permute-done.34.refs_1_), channel_id=1, source_target_pairs={{0,1},{1,0},{2,3},{3,2},{4,5},{5,4},{6,7},{7,6},{8,9},{9,8},{10,11... | collective-permute-start | bytes 2359304 | tf_op jit(solution)/shard_map/ppermute | solution.py:54
  205.0 29.9 %collective-permute-start.39 = (bf16[256,1536]{1,0:T(8,128)(2,1)S(1)}, bf16[256,1536]{1,0:T(8,128)(2,1)}, u32[]{:S(2)}, u32[]{:S(2)}) collective-permute-start(bf16[256,1536]{1,0:T(8,128)(2,1)S(1)} %collective-permute-done.34.refs_1_), channel_id=1, source_target_pairs={{0,2},{1,3},{2,0},{3,1},{4,6},{5,7},{6,4},{7,5},{8,10},{9,11},{10,... | collective-permute-start | bytes 2359304 | tf_op jit(solution)/shard_map/ppermute | solution.py:54
  206.4 28.5 %collective-permute-start.41 = (bf16[3,192,512]{2,1,0:T(8,128)(2,1)S(1)}, bf16[3,192,512]{2,1,0:T(8,128)(2,1)S(1)}, u32[]{:S(2)}, u32[]{:S(2)}) collective-permute-start(bf16[3,192,512]{2,1,0:T(8,128)(2,1)S(1)} %pad_maximum_fusion.10.refs_16_), channel_id=1, source_target_pairs={{0,8},{4,12},{8,0},{12,4},{1,9},{5,13},{9,1},{13,5},{2,10},{6,14},... | collective-permute-start | bytes 1769480 | tf_op jit(solution)/shard_map/ppermute | solution.py:54
  237.0 31.2 %collective-permute-start.42 = (bf16[3,192,512]{2,1,0:T(8,128)(2,1)}, bf16[3,192,512]{2,1,0:T(8,128)(2,1)}, u32[]{:S(2)}, u32[]{:S(2)}) collective-permute-start(bf16[3,192,512]{2,1,0:T(8,128)(2,1)} %pad_maximum_fusion.11.refs_17_), channel_id=1, source_target_pairs={{0,8},{4,12},{8,0},{12,4},{1,9},{5,13},{9,1},{13,5},{2,10},{6,14},... | collective-permute-start | bytes 1769480 | tf_op jit(solution)/shard_map/ppermute | solution.py:54
  237.0 31.2 %collective-permute-start.43 = (bf16[3,192,512]{2,1,0:T(8,128)(2,1)}, bf16[3,192,512]{2,1,0:T(8,128)(2,1)}, u32[]{:S(2)}, u32[]{:S(2)}) collective-permute-start(bf16[3,192,512]{2,1,0:T(8,128)(2,1)} %pad_maximum_fusion.11.refs_17_), channel_id=1, source_target_pairs={{0,16},{16,0},{1,17},{17,1},{2,18},{18,2},{3,19},{19,3},{4,20},{20... | collective-permute-start | bytes 1769480 | tf_op jit(solution)/shard_map/ppermute | solution.py:49
  237.5 30.7 %collective-permute-start.44 = (bf16[3,192,512]{2,1,0:T(8,128)(2,1)}, bf16[3,192,512]{2,1,0:T(8,128)(2,1)}, u32[]{:S(2)}, u32[]{:S(2)}) collective-permute-start(bf16[3,192,512]{2,1,0:T(8,128)(2,1)} %copy-done.58), channel_id=1, source_target_pairs={{0,16},{16,0},{1,17},{17,1},{2,18},{18,2},{3,19},{19,3},{4,20},{20... | collective-permute-start | bytes 1769480 | tf_op jit(solution)/shard_map/ppermute | solution.py:49
  285.2 31.7 %collective-permute-start.48 = (bf16[2,3,192,512]{3,2,1,0:T(8,128)(2,1)}, bf16[2,3,192,512]{3,2,1,0:T(8,128)(2,1)S(1)}, u32[]{:S(2)}, u32[]{:S(2)}) collective-permute-start(bf16[2,3,192,512]{3,2,1,0:T(8,128)(2,1)} %get-tuple-element.299), channel_id=1, source_target_pairs={{0,16},{16,0},{1,17},{17,1},{2,18},{18,2},{3,19},{19,3},{4,20},{20... | collective-permute-start | bytes 3538952 | tf_op jit(solution)/shard_map/ppermute | solution.py:49
  324.0 30.4 %collective-permute-start.50 = (bf16[1024,1536]{1,0:T(8,128)(2,1)}, bf16[1024,1536]{1,0:T(8,128)(2,1)}, u32[]{:S(2)}, u32[]{:S(2)}) collective-permute-start(bf16[1024,1536]{1,0:T(8,128)(2,1)} %get-tuple-element.306), channel_id=1, source_target_pairs={{0,1},{1,0},{2,3},{3,2},{4,5},{5,4},{6,7},{7,6},{8,9},{9,8},{10,11... | collective-permute-start | bytes 9437192 | tf_op jit(solution)/shard_map/ppermute | solution.py:54
  324.1 28.6 %collective-permute-start.54 = (bf16[2,3,192,512]{3,2,1,0:T(8,128)(2,1)}, bf16[2,3,192,512]{3,2,1,0:T(8,128)(2,1)}, u32[]{:S(2)}, u32[]{:S(2)}) collective-permute-start(bf16[2,3,192,512]{3,2,1,0:T(8,128)(2,1)} %get-tuple-element.310), channel_id=1, source_target_pairs={{0,16},{16,0},{1,17},{17,1},{2,18},{18,2},{3,19},{19,3},{4,20},{20... | collective-permute-start | bytes 3538952 | tf_op jit(solution)/shard_map/ppermute | solution.py:49
  324.9 29.5 %collective-permute-start.53 = (bf16[3,192,512]{2,1,0:T(8,128)(2,1)}, bf16[3,192,512]{2,1,0:T(8,128)(2,1)}, u32[]{:S(2)}, u32[]{:S(2)}) collective-permute-start(bf16[3,192,512]{2,1,0:T(8,128)(2,1)} %get-tuple-element.309), channel_id=1, source_target_pairs={{0,8},{4,12},{8,0},{12,4},{1,9},{5,13},{9,1},{13,5},{2,10},{6,14},... | collective-permute-start | bytes 1769480 | tf_op jit(solution)/shard_map/ppermute | solution.py:54
  355.6 28.3 %collective-permute-start.57 = (bf16[3,192,512]{2,1,0:T(8,128)(2,1)S(1)}, bf16[3,192,512]{2,1,0:T(8,128)(2,1)}, u32[]{:S(2)}, u32[]{:S(2)}) collective-permute-start(bf16[3,192,512]{2,1,0:T(8,128)(2,1)S(1)} %get-tuple-element.322), channel_id=1, source_target_pairs={{0,8},{4,12},{8,0},{12,4},{1,9},{5,13},{9,1},{13,5},{2,10},{6,14},... | collective-permute-start | bytes 1769480 | tf_op jit(solution)/shard_map/ppermute | solution.py:54
  359.2 29.7 %collective-permute-start.56 = (bf16[256,1536]{1,0:T(8,128)(2,1)S(1)}, bf16[256,1536]{1,0:T(8,128)(2,1)S(1)}, u32[]{:S(2)}, u32[]{:S(2)}) collective-permute-start(bf16[256,1536]{1,0:T(8,128)(2,1)S(1)} %pad_maximum_fusion.6), channel_id=1, source_target_pairs={{0,4},{4,0},{8,12},{12,8},{1,5},{5,1},{9,13},{13,9},{2,6},{6,2},{1... | collective-permute-start | bytes 2359304 | tf_op jit(solution)/shard_map/ppermute | solution.py:54
  360.6 28.4 %collective-permute-start.55 = (bf16[256,1536]{1,0:T(8,128)(2,1)S(1)}, bf16[256,1536]{1,0:T(8,128)(2,1)S(1)}, u32[]{:S(2)}, u32[]{:S(2)}) collective-permute-start(bf16[256,1536]{1,0:T(8,128)(2,1)S(1)} %pad_maximum_fusion.5), channel_id=1, source_target_pairs={{0,2},{1,3},{2,0},{3,1},{4,6},{5,7},{6,4},{7,5},{8,10},{9,11},{10,... | collective-permute-start | bytes 2359304 | tf_op jit(solution)/shard_map/ppermute | solution.py:54
  417.9 34.0 %collective-permute-start.67 = (bf16[2,2,4,48,1536]{4,3,2,1,0:T(8,128)(2,1)}, bf16[2,2,4,48,1536]{4,3,2,1,0:T(8,128)(2,1)}, u32[]{:S(2)}, u32[]{:S(2)}) collective-permute-start(bf16[2,2,4,48,1536]{4,3,2,1,0:T(8,128)(2,1)} %get-tuple-element.350), channel_id=1, source_target_pairs={{0,1},{1,0},{2,3},{3,2},{4,5},{5,4},{6,7},{7,6},{8,9},{9,8},{10,11... | collective-permute-start | bytes 7077896 | tf_op jit(solution)/shard_map/ppermute | solution.py:54
  417.9 32.3 %collective-permute-start.64 = (bf16[256,1536]{1,0:T(8,128)(2,1)}, bf16[256,1536]{1,0:T(8,128)(2,1)}, u32[]{:S(2)}, u32[]{:S(2)}) collective-permute-start(bf16[256,1536]{1,0:T(8,128)(2,1)} %get-tuple-element.340), channel_id=1, source_target_pairs={{0,2},{1,3},{2,0},{3,1},{4,6},{5,7},{6,4},{7,5},{8,10},{9,11},{10,... | collective-permute-start | bytes 2359304 | tf_op jit(solution)/shard_map/ppermute | solution.py:54
  419.3 32.6 %collective-permute-start.65 = (bf16[256,1536]{1,0:T(8,128)(2,1)}, bf16[256,1536]{1,0:T(8,128)(2,1)}, u32[]{:S(2)}, u32[]{:S(2)}) collective-permute-start(bf16[256,1536]{1,0:T(8,128)(2,1)} %add_convert_fusion.5), channel_id=1, source_target_pairs={{0,4},{4,0},{8,12},{12,8},{1,5},{5,1},{9,13},{13,9},{2,6},{6,2},{1... | collective-permute-start | bytes 2359304 | tf_op jit(solution)/shard_map/ppermute | solution.py:54
  420.1 30.1 %collective-permute-start.66 = (bf16[3,192,512]{2,1,0:T(8,128)(2,1)}, bf16[3,192,512]{2,1,0:T(8,128)(2,1)S(1)}, u32[]{:S(2)}, u32[]{:S(2)}) collective-permute-start(bf16[3,192,512]{2,1,0:T(8,128)(2,1)} %get-tuple-element.349), channel_id=1, source_target_pairs={{0,8},{4,12},{8,0},{12,4},{1,9},{5,13},{9,1},{13,5},{2,10},{6,14},... | collective-permute-start | bytes 1769480 | tf_op jit(solution)/shard_map/ppermute | solution.py:54
  454.5 28.7 %collective-permute-start.70 = (bf16[2,4,48,1536]{3,2,1,0:T(8,128)(2,1)}, bf16[2,4,48,1536]{3,2,1,0:T(8,128)(2,1)S(1)}, u32[]{:S(2)}, u32[]{:S(2)}) collective-permute-start(bf16[2,4,48,1536]{3,2,1,0:T(8,128)(2,1)} %fusion.9), channel_id=1, source_target_pairs={{0,2},{1,3},{2,0},{3,1},{4,6},{5,7},{6,4},{7,5},{8,10},{9,11},{10,... | collective-permute-start | bytes 3538952 | tf_op jit(solution)/shard_map/ppermute | solution.py:54
  (136 other events, 2247.3 us)

commit v6 on v5

--- a/solution.py
+++ b/solution.py
@@ -1107,14 +1107,14 @@
     wo_b = flip_e(run.hold(wo_b), 1)
     dqkv = attend_back(scalars, pieces, run.hold(grad_mixes), lse, cos, sin, heads, kvs)
     grad_normed = finish(scalars, dqkv, w_qkv, nz)
-    run.end(z_2, far_o, other_o, wo_b, grad_normed)
+    wo_far = add(lax.optimization_barrier((wo_a, grad_normed[3]))[0][1], wo_b[1])
+    run.end(z_2, far_o, other_o, wo_far, grad_normed)
 
     z_3 = flip(run.hold(x_3[1]), "ctx", 2)
     gw_a, gw_b = finish_weights(scalars, here, dqkv, run.hold(grad_normed), toks, gain_a, grad_gain_m, nd, ne)
     swap = flip(run.hold(swap), "ctx", 1)
     swap_2 = flip(add(run.hold(x_2[0])[1], z_2[1]), "ctx", 1)
-    wo_b = run.hold(wo_b)
-    wo_far = flip_e(add(wo_a[1], wo_b[1]), 2)
+    wo_far = flip_e(run.hold(wo_far), 2)
     run.end(gw_b, swap, swap_2, wo_far, z_3)
 
     tail = run.hold(grad_normed)

time: 581 us -> 578 us (level)
  transfers between devices with their start and end apart: 83 -> 83, of which waited for: 35 -> 35; matrix products, arithmetic and copies ran while one was open for 11% -> 12% of each run, Pallas kernels for 33% -> 33%
where the time goes in v6:
time: 578 us; the launch traced here: 573 us
  waiting for transfers between devices  217 us (38%)
  Pallas kernels  192 us (33%)
  starting transfers between devices  77.8 us (13%)
  other arithmetic  57.6 us (10%)
  local copies, waits for them, and re-layouts  26.9 us (5%)
    ppermute x45, waiting for transfers between devices, flip(): return lax.ppermute(x, axis, [(i, i ^ mask) for i in range(n)])  106 us
    ppermute x34, waiting for transfers between devices, shift(): return lax.ppermute(x, axis, [(i, (i + by) % n) for i in range(n)])  103 us
    pallas_call x2, Pallas kernels, experts_rows(): pl.pallas_call(body, grid=(tiles,), out_shape=sum_shapes + (jax.ShapeDtyp...  57.4 us
    ppermute x34, starting transfers between devices, shift(): return lax.ppermute(x, axis, [(i, (i + by) % n) for i in range(n)])  40.6 us
    pallas_call x2, Pallas kernels, experts_weights(): pl.pallas_call(body, out_shape=[jax.ShapeDtypeStruct((2, 3, r, width), BF...  31.7 us
    ppermute x45, starting transfers between devices, flip(): return lax.ppermute(x, axis, [(i, i ^ mask) for i in range(n)])  30.2 us
    convert_element_type x20, other arithmetic, add(): return (a.astype(F32) + b.astype(F32)).astype(BF)  27.2 us
    pallas_call x1, Pallas kernels, attend_back(): pl.pallas_call(body, out_shape=jax.ShapeDtypeStruct((span, width), BF), i...  20.3 us
  transfers between devices with their start and end apart: 83, of which 35 were waited for; matrix products, arithmetic and copies ran while one was open for 12% of the time, Pallas kernels for 33%

profile of v6, /device:TPU:0, one launch (start us, length us, event | category | flops | bytes accessed | tf_op | source)
XLA Modules:
  0.0 573.1 jit_solution(15754060692628955304)
XLA Ops:
  16.7 13.9 %collective-permute-done.3.refs_1_ = bf16[256,1536]{1,0:T(8,128)(2,1)S(1)} collective-permute-done((bf16[256,1536]{1,0:T(8,128)(2,1)S(1)}, bf16[256,1536]{1,0:T(8,128)(2,1)S(1)}, u32[]{:S(2)}, u32[]{:S(2)}) %collective-permute-start.3) | collective-permute-done | bytes 786464 | tf_op jit(solution)/shard_map/ppermute | solution.py:49
  60.0 7.2 %collective-permute-done.11 = bf16[48,1536]{1,0:T(8,128)(2,1)} collective-permute-done((bf16[48,1536]{1,0:T(8,128)(2,1)}, bf16[48,1536]{1,0:T(8,128)(2,1)}, u32[]{:S(2)}, u32[]{:S(2)}) %collective-permute-start.11) | collective-permute-done | bytes 147488 | tf_op jit(solution)/shard_map/ppermute | solution.py:78
  108.1 13.3 %attend.1 = (bf16[256,384]{1,0:T(8,128)(2,1)}, bf16[256,384]{1,0:T(8,128)(2,1)}, bf16[256,384]{1,0:T(8,128)(2,1)}, bf16[256,384]{1,0:T(8,128)(2,1)}, f32[8,1024]{1,0:T(8,128)}) custom-call(s32[8]{0:T(128)} %concatenate.42.s_ref, bf16[256,640]{1,0:T(8,128)(2,1)} %get-tuple-element.218.refs_0_, bf16[256,640]{1,0:T(8,128)(2,1)} %get-tuple-element.219.refs_1_, ...), custom_call_target="tpu_custom_call" | custom-call | flops 1342177280 | bytes 873813 | tf_op jit(solution)/shard_map/attend/pallas_call | solution.py:291
  123.6 6.2 %collective-permute-done.18.refs_18_ = bf16[3,192,512]{2,1,0:T(8,128)(2,1)} collective-permute-done((bf16[3,192,512]{2,1,0:T(8,128)(2,1)}, bf16[3,192,512]{2,1,0:T(8,128)(2,1)}, u32[]{:S(2)}, u32[]{:S(2)}) %collective-permute-start.18) | collective-permute-done | bytes 589856 | tf_op jit(solution)/shard_map/ppermute | solution.py:54
  142.4 9.8 %collective-permute-done.23.refs_2_ = bf16[256,384]{1,0:T(8,128)(2,1)} collective-permute-done((bf16[256,384]{1,0:T(8,128)(2,1)}, bf16[256,384]{1,0:T(8,128)(2,1)}, u32[]{:S(2)}, u32[]{:S(2)}) %collective-permute-start.23) | collective-permute-done | bytes 196640 | tf_op jit(solution)/shard_map/ppermute | solution.py:49
  155.6 6.2 %join.1 = (f32[256,1536]{1,0:T(8,128)}, bf16[256,1536]{1,0:T(8,128)(2,1)}) custom-call(s32[8]{0:T(128)} %concatenate.42.s_ref, bf16[256,384]{1,0:T(8,128)(2,1)} %get-tuple-element.245.refs_0_, bf16[256,384]{1,0:T(8,128)(2,1)} %collective-permute-done.22.refs_1_, bf16[256,384]{1,0:T(8,128)(2,1)} %collective-permute-done.23.refs_2_, ...), custom_call_target="tpu_custom_call" | custom-call | flops 402653184 | bytes 2883584 | tf_op jit(solution)/shard_map/join/pallas_call | solution.py:411
  176.8 12.6 %collective-permute-done.36.refs_18_ = bf16[3,192,512]{2,1,0:T(8,128)(2,1)S(1)} collective-permute-done((bf16[3,192,512]{2,1,0:T(8,128)(2,1)S(1)}, bf16[3,192,512]{2,1,0:T(8,128)(2,1)S(1)}, u32[]{:S(2)}, u32[]{:S(2)}) %collective-permute-start.36) | collective-permute-done | bytes 589856 | tf_op jit(solution)/shard_map/ppermute | solution.py:49
  189.4 12.9 %collective-permute-done.35.refs_19_ = bf16[3,192,512]{2,1,0:T(8,128)(2,1)S(1)} collective-permute-done((bf16[3,192,512]{2,1,0:T(8,128)(2,1)S(1)}, bf16[3,192,512]{2,1,0:T(8,128)(2,1)S(1)}, u32[]{:S(2)}, u32[]{:S(2)}) %collective-permute-start.35) | collective-permute-done | bytes 589856 | tf_op jit(solution)/shard_map/ppermute | solution.py:54
  210.1 24.7 %collective-permute-done.41.refs_20_ = bf16[3,192,512]{2,1,0:T(8,128)(2,1)S(1)} collective-permute-done((bf16[3,192,512]{2,1,0:T(8,128)(2,1)S(1)}, bf16[3,192,512]{2,1,0:T(8,128)(2,1)S(1)}, u32[]{:S(2)}, u32[]{:S(2)}) %collective-permute-start.41) | collective-permute-done | bytes 589856 | tf_op jit(solution)/shard_map/ppermute | solution.py:54
  240.8 27.3 %experts_rows.2 = (bf16[2048,1536]{1,0:T(8,128)(2,1)}, bf16[2048,1536]{1,0:T(8,128)(2,1)}, bf16[2048,1024]{1,0:T(8,128)(2,1)}, bf16[512,2048]{1,0:T(8,128)(2,1)}, bf16[1536,2048]{1,0:T(8,128)(2,1)}) custom-call(s32[13]{0:T(128)} %stack.499.places_ref, bf16[256,1536]{1,0:T(8,128)(2,1)} %get-tuple-element.289.refs_0_, bf16[256,1536]{1,0:T(8,128)(2,1)} %copy-done.52, ...), custom_call_target="tpu_custom_call" | custom-call | flops 6442450944 | bytes 16666666 | tf_op jit(solution)/shard_map/experts_rows/pallas_call | solution.py:727
  269.4 15.8 %experts_weights.2 = (bf16[2,3,192,512]{3,2,1,0:T(8,128)(2,1)}, bf16[2,3,192,512]{3,2,1,0:T(8,128)(2,1)}, bf16[2,3,192,512]{3,2,1,0:T(8,128)(2,1)}, bf16[2,3,192,512]{3,2,1,0:T(8,128)(2,1)}) custom-call(s32[4]{0:T(128)} %pad_add_fusion.1.s_ref.here_ref, bf16[1536,2048]{1,0:T(8,128)(2,1)} %get-tuple-element.280.h_any, ...), custom_call_target="tpu_custom_call" | custom-call | flops 3221225472 | bytes 6666666 | tf_op jit(solution)/shard_map/experts_weights/pallas_call | solution.py:811
  286.8 30.1 %experts_rows.3 = (bf16[1024,1536]{1,0:T(8,128)(2,1)}, bf16[1024,1536]{1,0:T(8,128)(2,1)}, bf16[1024,1536]{1,0:T(8,128)(2,1)}, bf16[1024,1536]{1,0:T(8,128)(2,1)...) custom-call(s32[13]{0:T(128)} %stack.499.places_ref, bf16[256,1536]{1,0:T(8,128)(2,1)} %get-tuple-element.289.refs_0_, ...), custom_call_target="tpu_custom_call" | custom-call | flops 6442450944 | bytes 16666666 | tf_op jit(solution)/shard_map/experts_rows/pallas_call | solution.py:727
  318.1 5.9 %collective-permute-done.49.refs_1_ = bf16[1024,1536]{1,0:T(8,128)(2,1)S(1)} collective-permute-done((bf16[1024,1536]{1,0:T(8,128)(2,1)}, bf16[1024,1536]{1,0:T(8,128)(2,1)S(1)}, u32[]{:S(2)}, u32[]{:S(2)}) %collective-permute-start.49) | collective-permute-done | bytes 3145760 | tf_op jit(solution)/shard_map/ppermute | solution.py:54
  330.3 15.9 %experts_weights.3 = (bf16[2,3,192,512]{3,2,1,0:T(8,128)(2,1)}, bf16[2,3,192,512]{3,2,1,0:T(8,128)(2,1)}, bf16[2,3,192,512]{3,2,1,0:T(8,128)(2,1)}, bf16[2,3,192,512]{3,2,1,0:T(8,128)(2,1)}) custom-call(s32[4]{0:T(128)} %pad_add_fusion.1.s_ref.here_ref, bf16[1536,2048]{1,0:T(8,128)(2,1)} %get-tuple-element.280.h_any, ...), custom_call_target="tpu_custom_call" | custom-call | flops 3221225472 | bytes 6666666 | tf_op jit(solution)/shard_map/experts_weights/pallas_call | solution.py:811
  346.2 6.5 %collective-permute-done.54 = bf16[2,3,192,512]{3,2,1,0:T(8,128)(2,1)} collective-permute-done((bf16[2,3,192,512]{3,2,1,0:T(8,128)(2,1)}, bf16[2,3,192,512]{3,2,1,0:T(8,128)(2,1)}, u32[]{:S(2)}, u32[]{:S(2)}) %collective-permute-start.54) | collective-permute-done | bytes 1179680 | tf_op jit(solution)/shard_map/ppermute | solution.py:49
  365.5 16.4 %collective-permute-done.58 = bf16[2,3,192,512]{3,2,1,0:T(8,128)(2,1)S(1)} collective-permute-done((bf16[2,3,192,512]{3,2,1,0:T(8,128)(2,1)S(1)}, bf16[2,3,192,512]{3,2,1,0:T(8,128)(2,1)S(1)}, u32[]{:S(2)}, u32[]{:S(2)}) %collective-permute-start.58) | collective-permute-done | bytes 1179680 | tf_op jit(solution)/shard_map/ppermute | solution.py:49
  391.7 8.2 %join_back.1 = (f32[256,1536]{1,0:T(8,128)}, bf16[256,1536]{1,0:T(8,128)(2,1)}, f32[1,1536]{1,0:T(1,128)}, bf16[256,384]{1,0:T(8,128)(2,1)}, bf16[256,384]{1,0:T...) custom-call(s32[8]{0:T(128)} %concatenate.42.s_ref, bf16[1024,1536]{1,0:T(8,128)(2,1)} %get-tuple-element.302.refs_0_, ...), custom_call_target="tpu_custom_call" | custom-call | flops 402653184 | bytes 3932160 | tf_op jit(solution)/shard_map/join_back/pallas_call | solution.py:455
  403.2 6.5 %join_weights.1 = (bf16[2,2,4,48,1536]{4,3,2,1,0:T(8,128)(2,1)}, bf16[2,2,4,48,1536]{4,3,2,1,0:T(8,128)(2,1)}) custom-call(s32[8]{0:T(128)} %concatenate.42.s_ref, s32[4]{0:T(128)} %pad_add_fusion.1.s_ref.here_ref, bf16[256,1536]{1,0:T(8,128)(2,1)} %get-tuple-element.336.br_ref, bf16[256,384]{1,0:T(8,128)(2,1)} %get-tuple-element.245.refs_0_, ...), custom_call_target="tpu_custom_call" | custom-call | flops 402653184 | bytes 2097152 | tf_op jit(solution)/shard_map/join_weights/pallas_call | solution.py:495
  421.8 20.3 %attend_back.1.dq_ref = bf16[1024,640]{1,0:T(8,128)(2,1)} custom-call(s32[8]{0:T(128)} %concatenate.42.s_ref, bf16[256,640]{1,0:T(8,128)(2,1)} %get-tuple-element.218.refs_0_, bf16[256,640]{1,0:T(8,128)(2,1)} %get-tuple-element.219.refs_1_, bf16[256,640]{1,0:T(8,128)(2,1)} %get-tuple-element.220.refs_2_, bf16[256,640]{1,0:T(8,128)(2,1)} %project.3.refs_3_, ...), custom_call_target="tpu_custom_call" | custom-call | flops 3355443200 | bytes 1747626 | tf_op jit(solution)/shard_map/attend_back/pallas_call | solution.py:373
  456.2 9.3 %finish_weights.1 = (bf16[2,2,4,48,768]{4,3,2,1,0:T(8,128)(2,1)}, bf16[2,2,4,48,768]{4,3,2,1,0:T(8,128)(2,1)}) custom-call(s32[8]{0:T(128)} %concatenate.42.s_ref, s32[4]{0:T(128)} %pad_add_fusion.1.s_ref.here_ref, bf16[1024,640]{1,0:T(8,128)(2,1)} %attend_back.1.dq_ref, f32[1,1536]{1,0:T(1,128)} %broadcast_in_dim.59.gain_ref, ...), custom_call_target="tpu_custom_call" | custom-call | flops 671088640 | bytes 3145728 | tf_op jit(solution)/shard_map/finish_weights/pallas_call | solution.py:884
  465.5 13.4 %collective-permute-done.69.their_ref = bf16[192,512]{1,0:T(8,128)(2,1)S(1)} collective-permute-done((bf16[192,512]{1,0:T(8,128)(2,1)S(1)}, bf16[192,512]{1,0:T(8,128)(2,1)S(1)}, u32[]{:S(2)}, u32[]{:S(2)}) %collective-permute-start.69) | collective-permute-done | bytes 196640 | tf_op jit(solution)/shard_map/ppermute | solution.py:54
  485.7 18.1 %collective-permute-done.72 = bf16[256,1536]{1,0:T(8,128)(2,1)S(1)} collective-permute-done((bf16[256,1536]{1,0:T(8,128)(2,1)}, bf16[256,1536]{1,0:T(8,128)(2,1)S(1)}, u32[]{:S(2)}, u32[]{:S(2)}) %collective-permute-start.72) | collective-permute-done | bytes 786464 | tf_op jit(solution)/shard_map/ppermute | solution.py:49
  508.1 12.3 %collective-permute-done.75 = bf16[2,4,48,768]{3,2,1,0:T(8,128)(2,1)} collective-permute-done((bf16[2,4,48,768]{3,2,1,0:T(8,128)(2,1)}, bf16[2,4,48,768]{3,2,1,0:T(8,128)(2,1)}, u32[]{:S(2)}, u32[]{:S(2)}) %collective-permute-start.75) | collective-permute-done | bytes 589856 | tf_op jit(solution)/shard_map/ppermute | solution.py:54
  542.2 9.3 %collective-permute-done.77 = bf16[256,1536]{1,0:T(8,128)(2,1)S(1)} collective-permute-done((bf16[256,1536]{1,0:T(8,128)(2,1)S(1)}, bf16[256,1536]{1,0:T(8,128)(2,1)S(1)}, u32[]{:S(2)}, u32[]{:S(2)}) %collective-permute-start.77) | collective-permute-done | bytes 786464 | tf_op jit(solution)/shard_map/ppermute | solution.py:49
  (429 shorter events, 249.0 us)
Async XLA Ops:
  100.9 31.1 %collective-permute-start.19 = (bf16[2,3,192,512]{3,2,1,0:T(8,128)(2,1)}, bf16[2,3,192,512]{3,2,1,0:T(8,128)(2,1)}, u32[]{:S(2)}, u32[]{:S(2)}) collective-permute-start(bf16[2,3,192,512]{3,2,1,0:T(8,128)(2,1)} %pad_maximum_fusion.1.refs_16_), channel_id=1, source_target_pairs={{0,16},{16,0},{1,17},{17,1},{2,18},{18,2},{3,19},{19,3},{4,20},{20... | collective-permute-start | bytes 3538952 | tf_op jit(solution)/shard_map/ppermute | solution.py:49
  102.4 29.6 %collective-permute-start.21 = (bf16[256,1664]{1,0:T(8,128)(2,1)S(1)}, bf16[256,1664]{1,0:T(8,128)(2,1)}, u32[]{:S(2)}, u32[]{:S(2)}) collective-permute-start(bf16[256,1664]{1,0:T(8,128)(2,1)S(1)} %pad_maximum_fusion.3.refs_8_.refs_0_), channel_id=1, source_target_pairs={{0,4},{4,0},{8,12},{12,8},{1,5},{5,1},{9,13},{13,9},{2,6},{6,2},{1... | collective-permute-start | bytes 2555912 | tf_op jit(solution)/shard_map/ppermute | solution.py:54
  171.3 31.0 %collective-permute-start.32 = (bf16[256,1536]{1,0:T(8,128)(2,1)}, bf16[256,1536]{1,0:T(8,128)(2,1)S(1)}, u32[]{:S(2)}, u32[]{:S(2)}) collective-permute-start(bf16[256,1536]{1,0:T(8,128)(2,1)} %get-tuple-element.289.refs_0_), channel_id=1, source_target_pairs={{0,1},{1,0},{2,3},{3,2},{4,5},{5,4},{6,7},{7,6},{8,9},{9,8},{10,11... | collective-permute-start | bytes 2359304 | tf_op jit(solution)/shard_map/ppermute | solution.py:54
  171.3 31.0 %collective-permute-start.33 = (bf16[256,1536]{1,0:T(8,128)(2,1)}, bf16[256,1536]{1,0:T(8,128)(2,1)S(1)}, u32[]{:S(2)}, u32[]{:S(2)}) collective-permute-start(bf16[256,1536]{1,0:T(8,128)(2,1)} %get-tuple-element.289.refs_0_), channel_id=1, source_target_pairs={{0,2},{1,3},{2,0},{3,1},{4,6},{5,7},{6,4},{7,5},{8,10},{9,11},{10,... | collective-permute-start | bytes 2359304 | tf_op jit(solution)/shard_map/ppermute | solution.py:54
  171.9 32.5 %collective-permute-start.34 = (bf16[256,1536]{1,0:T(8,128)(2,1)}, bf16[256,1536]{1,0:T(8,128)(2,1)S(1)}, u32[]{:S(2)}, u32[]{:S(2)}) collective-permute-start(bf16[256,1536]{1,0:T(8,128)(2,1)} %get-tuple-element.289.refs_0_), channel_id=1, source_target_pairs={{0,4},{4,0},{8,12},{12,8},{1,5},{5,1},{9,13},{13,9},{2,6},{6,2},{1... | collective-permute-start | bytes 2359304 | tf_op jit(solution)/shard_map/ppermute | solution.py:54
  204.5 30.4 %collective-permute-start.38 = (bf16[256,1536]{1,0:T(8,128)(2,1)S(1)}, bf16[256,1536]{1,0:T(8,128)(2,1)S(1)}, u32[]{:S(2)}, u32[]{:S(2)}) collective-permute-start(bf16[256,1536]{1,0:T(8,128)(2,1)S(1)} %collective-permute-done.33.refs_2_), channel_id=1, source_target_pairs={{0,1},{1,0},{2,3},{3,2},{4,5},{5,4},{6,7},{7,6},{8,9},{9,8},{10,11... | collective-permute-start | bytes 2359304 | tf_op jit(solution)/shard_map/ppermute | solution.py:54
  204.5 30.4 %collective-permute-start.37 = (bf16[256,1536]{1,0:T(8,128)(2,1)S(1)}, bf16[256,1536]{1,0:T(8,128)(2,1)S(1)}, u32[]{:S(2)}, u32[]{:S(2)}) collective-permute-start(bf16[256,1536]{1,0:T(8,128)(2,1)S(1)} %collective-permute-done.34.refs_1_), channel_id=1, source_target_pairs={{0,1},{1,0},{2,3},{3,2},{4,5},{5,4},{6,7},{7,6},{8,9},{9,8},{10,11... | collective-permute-start | bytes 2359304 | tf_op jit(solution)/shard_map/ppermute | solution.py:54
  205.0 29.9 %collective-permute-start.39 = (bf16[256,1536]{1,0:T(8,128)(2,1)S(1)}, bf16[256,1536]{1,0:T(8,128)(2,1)}, u32[]{:S(2)}, u32[]{:S(2)}) collective-permute-start(bf16[256,1536]{1,0:T(8,128)(2,1)S(1)} %collective-permute-done.34.refs_1_), channel_id=1, source_target_pairs={{0,2},{1,3},{2,0},{3,1},{4,6},{5,7},{6,4},{7,5},{8,10},{9,11},{10,... | collective-permute-start | bytes 2359304 | tf_op jit(solution)/shard_map/ppermute | solution.py:54
  206.4 28.5 %collective-permute-start.41 = (bf16[3,192,512]{2,1,0:T(8,128)(2,1)S(1)}, bf16[3,192,512]{2,1,0:T(8,128)(2,1)S(1)}, u32[]{:S(2)}, u32[]{:S(2)}) collective-permute-start(bf16[3,192,512]{2,1,0:T(8,128)(2,1)S(1)} %pad_maximum_fusion.10.refs_16_), channel_id=1, source_target_pairs={{0,8},{4,12},{8,0},{12,4},{1,9},{5,13},{9,1},{13,5},{2,10},{6,14},... | collective-permute-start | bytes 1769480 | tf_op jit(solution)/shard_map/ppermute | solution.py:54
  237.0 31.2 %collective-permute-start.42 = (bf16[3,192,512]{2,1,0:T(8,128)(2,1)}, bf16[3,192,512]{2,1,0:T(8,128)(2,1)}, u32[]{:S(2)}, u32[]{:S(2)}) collective-permute-start(bf16[3,192,512]{2,1,0:T(8,128)(2,1)} %pad_maximum_fusion.11.refs_17_), channel_id=1, source_target_pairs={{0,8},{4,12},{8,0},{12,4},{1,9},{5,13},{9,1},{13,5},{2,10},{6,14},... | collective-permute-start | bytes 1769480 | tf_op jit(solution)/shard_map/ppermute | solution.py:54
  237.0 31.2 %collective-permute-start.43 = (bf16[3,192,512]{2,1,0:T(8,128)(2,1)}, bf16[3,192,512]{2,1,0:T(8,128)(2,1)}, u32[]{:S(2)}, u32[]{:S(2)}) collective-permute-start(bf16[3,192,512]{2,1,0:T(8,128)(2,1)} %pad_maximum_fusion.11.refs_17_), channel_id=1, source_target_pairs={{0,16},{16,0},{1,17},{17,1},{2,18},{18,2},{3,19},{19,3},{4,20},{20... | collective-permute-start | bytes 1769480 | tf_op jit(solution)/shard_map/ppermute | solution.py:49
  237.5 30.7 %collective-permute-start.44 = (bf16[3,192,512]{2,1,0:T(8,128)(2,1)}, bf16[3,192,512]{2,1,0:T(8,128)(2,1)}, u32[]{:S(2)}, u32[]{:S(2)}) collective-permute-start(bf16[3,192,512]{2,1,0:T(8,128)(2,1)} %copy-done.58), channel_id=1, source_target_pairs={{0,16},{16,0},{1,17},{17,1},{2,18},{18,2},{3,19},{19,3},{4,20},{20... | collective-permute-start | bytes 1769480 | tf_op jit(solution)/shard_map/ppermute | solution.py:49
  285.2 31.7 %collective-permute-start.48 = (bf16[2,3,192,512]{3,2,1,0:T(8,128)(2,1)}, bf16[2,3,192,512]{3,2,1,0:T(8,128)(2,1)S(1)}, u32[]{:S(2)}, u32[]{:S(2)}) collective-permute-start(bf16[2,3,192,512]{3,2,1,0:T(8,128)(2,1)} %get-tuple-element.300), channel_id=1, source_target_pairs={{0,16},{16,0},{1,17},{17,1},{2,18},{18,2},{3,19},{19,3},{4,20},{20... | collective-permute-start | bytes 3538952 | tf_op jit(solution)/shard_map/ppermute | solution.py:49
  324.0 30.4 %collective-permute-start.50 = (bf16[1024,1536]{1,0:T(8,128)(2,1)}, bf16[1024,1536]{1,0:T(8,128)(2,1)}, u32[]{:S(2)}, u32[]{:S(2)}) collective-permute-start(bf16[1024,1536]{1,0:T(8,128)(2,1)} %get-tuple-element.307), channel_id=1, source_target_pairs={{0,1},{1,0},{2,3},{3,2},{4,5},{5,4},{6,7},{7,6},{8,9},{9,8},{10,11... | collective-permute-start | bytes 9437192 | tf_op jit(solution)/shard_map/ppermute | solution.py:54
  324.1 28.6 %collective-permute-start.54 = (bf16[2,3,192,512]{3,2,1,0:T(8,128)(2,1)}, bf16[2,3,192,512]{3,2,1,0:T(8,128)(2,1)}, u32[]{:S(2)}, u32[]{:S(2)}) collective-permute-start(bf16[2,3,192,512]{3,2,1,0:T(8,128)(2,1)} %get-tuple-element.311), channel_id=1, source_target_pairs={{0,16},{16,0},{1,17},{17,1},{2,18},{18,2},{3,19},{19,3},{4,20},{20... | collective-permute-start | bytes 3538952 | tf_op jit(solution)/shard_map/ppermute | solution.py:49
  324.9 29.5 %collective-permute-start.53 = (bf16[3,192,512]{2,1,0:T(8,128)(2,1)}, bf16[3,192,512]{2,1,0:T(8,128)(2,1)}, u32[]{:S(2)}, u32[]{:S(2)}) collective-permute-start(bf16[3,192,512]{2,1,0:T(8,128)(2,1)} %get-tuple-element.310), channel_id=1, source_target_pairs={{0,8},{4,12},{8,0},{12,4},{1,9},{5,13},{9,1},{13,5},{2,10},{6,14},... | collective-permute-start | bytes 1769480 | tf_op jit(solution)/shard_map/ppermute | solution.py:54
  355.6 28.3 %collective-permute-start.57 = (bf16[3,192,512]{2,1,0:T(8,128)(2,1)S(1)}, bf16[3,192,512]{2,1,0:T(8,128)(2,1)}, u32[]{:S(2)}, u32[]{:S(2)}) collective-permute-start(bf16[3,192,512]{2,1,0:T(8,128)(2,1)S(1)} %get-tuple-element.323), channel_id=1, source_target_pairs={{0,8},{4,12},{8,0},{12,4},{1,9},{5,13},{9,1},{13,5},{2,10},{6,14},... | collective-permute-start | bytes 1769480 | tf_op jit(solution)/shard_map/ppermute | solution.py:54
  359.2 29.7 %collective-permute-start.56 = (bf16[256,1536]{1,0:T(8,128)(2,1)S(1)}, bf16[256,1536]{1,0:T(8,128)(2,1)S(1)}, u32[]{:S(2)}, u32[]{:S(2)}) collective-permute-start(bf16[256,1536]{1,0:T(8,128)(2,1)S(1)} %pad_maximum_fusion.6), channel_id=1, source_target_pairs={{0,4},{4,0},{8,12},{12,8},{1,5},{5,1},{9,13},{13,9},{2,6},{6,2},{1... | collective-permute-start | bytes 2359304 | tf_op jit(solution)/shard_map/ppermute | solution.py:54
  360.6 28.4 %collective-permute-start.55 = (bf16[256,1536]{1,0:T(8,128)(2,1)S(1)}, bf16[256,1536]{1,0:T(8,128)(2,1)S(1)}, u32[]{:S(2)}, u32[]{:S(2)}) collective-permute-start(bf16[256,1536]{1,0:T(8,128)(2,1)S(1)} %pad_maximum_fusion.5), channel_id=1, source_target_pairs={{0,2},{1,3},{2,0},{3,1},{4,6},{5,7},{6,4},{7,5},{8,10},{9,11},{10,... | collective-permute-start | bytes 2359304 | tf_op jit(solution)/shard_map/ppermute | solution.py:54
  417.9 29.9 %collective-permute-start.67 = (bf16[2,2,4,48,1536]{4,3,2,1,0:T(8,128)(2,1)}, bf16[2,2,4,48,1536]{4,3,2,1,0:T(8,128)(2,1)}, u32[]{:S(2)}, u32[]{:S(2)}) collective-permute-start(bf16[2,2,4,48,1536]{4,3,2,1,0:T(8,128)(2,1)} %get-tuple-element.353), channel_id=1, source_target_pairs={{0,1},{1,0},{2,3},{3,2},{4,5},{5,4},{6,7},{7,6},{8,9},{9,8},{10,11... | collective-permute-start | bytes 7077896 | tf_op jit(solution)/shard_map/ppermute | solution.py:54
  417.9 32.5 %collective-permute-start.66 = (bf16[3,192,512]{2,1,0:T(8,128)(2,1)}, bf16[3,192,512]{2,1,0:T(8,128)(2,1)S(1)}, u32[]{:S(2)}, u32[]{:S(2)}) collective-permute-start(bf16[3,192,512]{2,1,0:T(8,128)(2,1)} %get-tuple-element.350), channel_id=1, source_target_pairs={{0,8},{4,12},{8,0},{12,4},{1,9},{5,13},{9,1},{13,5},{2,10},{6,14},... | collective-permute-start | bytes 1769480 | tf_op jit(solution)/shard_map/ppermute | solution.py:54
  420.1 30.3 %collective-permute-start.64 = (bf16[256,1536]{1,0:T(8,128)(2,1)}, bf16[256,1536]{1,0:T(8,128)(2,1)}, u32[]{:S(2)}, u32[]{:S(2)}) collective-permute-start(bf16[256,1536]{1,0:T(8,128)(2,1)} %get-tuple-element.341), channel_id=1, source_target_pairs={{0,2},{1,3},{2,0},{3,1},{4,6},{5,7},{6,4},{7,5},{8,10},{9,11},{10,... | collective-permute-start | bytes 2359304 | tf_op jit(solution)/shard_map/ppermute | solution.py:54
  420.7 31.8 %collective-permute-start.65 = (bf16[256,1536]{1,0:T(8,128)(2,1)}, bf16[256,1536]{1,0:T(8,128)(2,1)}, u32[]{:S(2)}, u32[]{:S(2)}) collective-permute-start(bf16[256,1536]{1,0:T(8,128)(2,1)} %add_convert_fusion.5), channel_id=1, source_target_pairs={{0,4},{4,0},{8,12},{12,8},{1,5},{5,1},{9,13},{13,9},{2,6},{6,2},{1... | collective-permute-start | bytes 2359304 | tf_op jit(solution)/shard_map/ppermute | solution.py:54
  452.5 29.0 %collective-permute-start.70 = (bf16[2,4,48,1536]{3,2,1,0:T(8,128)(2,1)}, bf16[2,4,48,1536]{3,2,1,0:T(8,128)(2,1)S(1)}, u32[]{:S(2)}, u32[]{:S(2)}) collective-permute-start(bf16[2,4,48,1536]{3,2,1,0:T(8,128)(2,1)} %fusion.9), channel_id=1, source_target_pairs={{0,2},{1,3},{2,0},{3,1},{4,6},{5,7},{6,4},{7,5},{8,10},{9,11},{10,... | collective-permute-start | bytes 3538952 | tf_op jit(solution)/shard_map/ppermute | solution.py:54
  (136 other events, 2233.2 us)
